TPU v7x, 512 devices: a whole 4x4x16 slice. The times are simulated.
512 devices in a mesh: section: 16 (over x, z_hi), seq: 32 (over z_lo, y, core).
Axes of the slice: x: 4, y: 4, z: 16 (z_hi: 4, z_lo: 4; z = z_hi * 4 + z_lo), core: 2. Of those that a mesh axis runs over, the one named last changes fastest.
Arguments:
- queries: bfloat16 [16, 768, 4096], P('section', 'seq'), as said below
- keys: bfloat16 [16, 768, 4096], P('section', 'seq'), as said below
- values: bfloat16 [16, 768, 4096], P('section', 'seq'), may hold values from -6 to 6
- latent: bfloat16 [16, 768, 4096], P('section', 'seq'), may hold values from -6 to 6
- entering: bfloat16 [768, 4096], P('seq'), may hold values from -6 to 6
- noise_level: int32 [16], P('section'), may hold values from 0 to 15
- token_counts: int32 [16], replicated, may hold values from 384 to 768, as said below
- block_mask: int32 [16, 16], replicated, may hold values from 0 to 1, as said below
- gate_table: float32 [16, 4096], replicated, may hold values from 0.3 to 3
Outputs:
- updated: bfloat16 [16, 768, 4096], P('section', 'seq')
- advanced: bfloat16 [16, 768, 4096], P('section', 'seq')
Inputs may be any that keep to these rules, and one draw needn't show every extreme that they name: `queries`: entries lie in -6 to 6. `keys`: entries lie in -4 to 4. `token_counts`: at least 384 tokens of every block are valid; one block is full in every draw. block_mask[s, s] = 1 and block_mask[s, t] = 0 for t > s; blocks before s may be 0 or 1.
All inputs are finite; a program needn't handle non-finite values.
Results may differ from a plain program's by a relative error of at most 0.0065.
Values may be sent and summed in bfloat16 or wider, within the bound.
No kernel may reach another device: no remote copies, remote signals or barrier semaphores. Data moves between devices by JAX's collectives and lax.ppermute only.
A program may use at most 64 MiB of HBM per device.

v0:
```python
import jax
import jax.numpy as jnp
from jax import lax
from jax.sharding import PartitionSpec as P

HD = 128


def shifted(value, axis, steps):
    count = lax.axis_size(axis)
    leading, last = (max(0, -steps), min(count, count - steps))
    return lax.ppermute(value, axis, [(source, source + steps) for source in range(leading, last)])


def make_attend(query_local, mask_row, token_counts, block_len, local_heads):
    positions = jnp.arange(block_len, dtype=jnp.int32)
    scale = HD ** (-0.5)
    block_total = mask_row.shape[0]

    def attend(carry, pieces, start):
        key_part, value_part = pieces
        pieces_held = key_part.shape[0]

        def visit(inner, offset):
            inside = (offset >= 0) & (offset < block_total)
            safe_id = jnp.clip(offset, 0, block_total - 1)
            flag = jnp.where(
                inside, lax.dynamic_index_in_dim(mask_row, safe_id, 0, keepdims=False), 0
            )
            valid_len = lax.dynamic_index_in_dim(token_counts, safe_id, 0, keepdims=False)

            def work(state):
                running_max, denominator, numerator = state
                key_tile = lax.dynamic_index_in_dim(key_part, offset, 0, keepdims=False).reshape(
                    block_len, local_heads, HD
                )
                value_tile = lax.dynamic_index_in_dim(
                    value_part, offset, 0, keepdims=False
                ).reshape(block_len, local_heads, HD)
                usable = positions < valid_len
                scores = (
                    jnp.einsum(
                        "ihd,jhd->hij", query_local, key_tile, preferred_element_type=jnp.float32
                    )
                    * scale
                )
                scores = jnp.where(usable[None, None, :], scores, jnp.float32(-1e30))
                new_max = jnp.maximum(running_max, jnp.max(scores, axis=-1))
                rescale = jnp.exp(running_max - new_max)
                weights = jnp.where(
                    usable[None, None, :], jnp.exp(scores - new_max[..., None]), jnp.float32(0.0)
                )
                denominator = denominator * rescale + jnp.sum(weights, axis=-1)
                product = jnp.einsum(
                    "hij,jhd->hid",
                    weights.astype(jnp.bfloat16),
                    value_tile,
                    preferred_element_type=jnp.float32,
                )
                numerator = numerator * rescale[..., None] + product
                return (new_max, denominator, numerator)

            def skip(state):
                return state

            return (lax.cond(flag == 1, work, skip, inner), None)

        carry, _ = lax.scan(visit, carry, jnp.arange(pieces_held, dtype=jnp.int32))
        return carry

    return attend


def local(
    queries, keys, values, latent, entering, noise_level, token_counts, block_mask, gate_table
):
    section_index = lax.axis_index("section")
    seq_count = lax.axis_size("seq")
    tok_rows = queries.shape[1]
    features = queries.shape[2]
    block_len = tok_rows * seq_count
    local_feat = features // seq_count
    local_heads = local_feat // HD
    mask_row = lax.dynamic_index_in_dim(block_mask, section_index, 0, keepdims=False)
    initial = (
        jnp.full((local_heads, block_len), -1e30, jnp.float32),
        jnp.zeros((local_heads, block_len), jnp.float32),
        jnp.zeros((local_heads, block_len, HD), jnp.float32),
    )
    query_moved, keys_moved, values_moved = (
        lax.all_to_all(queries, "seq", split_axis=2, concat_axis=1, tiled=True),
        lax.all_to_all(keys, "seq", split_axis=2, concat_axis=1, tiled=True),
        lax.all_to_all(values, "seq", split_axis=2, concat_axis=1, tiled=True),
    )
    query_local = query_moved.reshape(block_len, local_heads, HD)
    attend = make_attend(query_local, mask_row, token_counts, block_len, local_heads)
    result = attend(
        initial,
        (
            lax.all_gather(keys_moved, "section", axis=0, tiled=True),
            lax.all_gather(values_moved, "section", axis=0, tiled=True),
        ),
        jnp.int32(0),
    )
    running_max, denominator, numerator = result
    attended = (numerator / denominator[..., None]).astype(jnp.bfloat16)
    outgoing = jnp.transpose(attended, (1, 0, 2)).reshape(1, block_len, local_feat)
    returned = lax.all_to_all(outgoing, "seq", split_axis=1, concat_axis=2, tiled=True)
    widened = returned.astype(jnp.float32)
    normed = widened / jnp.sqrt(jnp.mean(widened * widened, axis=-1, keepdims=True) + 1e-06)
    gate_row = lax.dynamic_index_in_dim(gate_table, noise_level[0], 0, keepdims=True)
    updated = (latent.astype(jnp.float32) + gate_row[None] * normed).astype(jnp.bfloat16)
    moved = shifted(updated, "section", 1)
    advanced = jnp.where(section_index == 0, entering[None], moved)
    return (updated, advanced)


def solution(mesh):
    placed = (
        P("section", "seq", None),
        P("section", "seq", None),
        P("section", "seq", None),
        P("section", "seq", None),
        P("seq", None),
        P("section"),
        P(),
        P(),
        P(),
    )
    return jax.shard_map(
        local,
        mesh=mesh,
        in_specs=placed,
        out_specs=(P("section", "seq", None), P("section", "seq", None)),
        check_vma=False,
    )
```

profile of v0, /device:TPU:486, one launch (start us, length us, event | category | flops | bytes accessed | tf_op | source)
XLA Modules:
  0.0 493.0 jit_solution(8689200467528087493)
XLA Ops:
  7.2 4.4 copy.54
  12.2 22.4 %reduce.17 = bf16[4096,24]{1,0:T(8,128)(2,1)S(1)} reduce(bf16[4096,1,24]{2,1,0:T(2,128)(2,1)S(1)} %bitcast.84, bf16[]{:T(256)} %broadcast.94), dimensions={1}, to_apply=%bitcast.58.reduce_sub_computation | reduce | bytes 393218
  36.0 15.2 %all_to_all.60 = bf16[32,2,1536]{2,1,0:T(2,128)(2,1)S(1)} all-to-all(bf16[32,2,1536]{2,1,0:T(2,128)(2,1)S(1)} %reshape.142), channel_id=1, replica_groups=mesh['section'=16,'seq'=32] {'seq'}, dimensions={0} | all-to-all | bytes 393216 | tf_op jit(solution)/shard_map/all_to_all | solution.py:92
  51.2 3.0 reshape.143
  54.2 2.1 copy.55
  57.4 2.8 copy.60
  60.1 22.4 %reduce.19 = bf16[4096,24]{1,0:T(8,128)(2,1)S(1)} reduce(bf16[4096,1,24]{2,1,0:T(2,128)(2,1)S(1)} %bitcast.88, bf16[]{:T(256)} %broadcast.94), dimensions={1}, to_apply=%bitcast.62.reduce_sub_computation | reduce | bytes 393218
  83.9 16.0 %all_to_all.61 = bf16[32,2,1536]{2,1,0:T(2,128)(2,1)S(1)} all-to-all(bf16[32,2,1536]{2,1,0:T(2,128)(2,1)S(1)} %reshape.146), channel_id=1, replica_groups=mesh['section'=16,'seq'=32] {'seq'}, dimensions={0} | all-to-all | bytes 393216 | tf_op jit(solution)/shard_map/all_to_all | solution.py:93
  99.9 3.0 reshape.147
  105.9 2.8 copy.57
  108.7 22.4 %reduce.18 = bf16[4096,24]{1,0:T(8,128)(2,1)S(1)} reduce(bf16[4096,1,24]{2,1,0:T(2,128)(2,1)S(1)} %bitcast.89, bf16[]{:T(256)} %broadcast.94), dimensions={1}, to_apply=%bitcast.60.reduce_sub_computation | reduce | bytes 393218
  133.1 6.9 %all-to-all-start.1 = ((bf16[32,2,1536]{2,1,0:T(2,128)(2,1)}), bf16[32,2,1536]{2,1,0:T(2,128)(2,1)S(1)}, u32[]{:S(2)}, u32[]{:S(2)}) async-start(bf16[32,2,1536]{2,1,0:T(2,128)(2,1)} %reshape.144), calls=%async_computation.1 | async-start | bytes 393216 | tf_op jit(solution)/shard_map/all_to_all | solution.py:91
  140.7 27.5 %all-to-all-done.1 = bf16[32,2,1536]{2,1,0:T(2,128)(2,1)S(1)} async-done(((bf16[32,2,1536]{2,1,0:T(2,128)(2,1)}), bf16[32,2,1536]{2,1,0:T(2,128)(2,1)S(1)}, u32[]{:S(2)}, u32[]{:S(2)}) %all-to-all-start.1) | async-done | bytes 196640 | tf_op jit(solution)/shard_map/all_to_all | solution.py:91
  168.3 3.0 reshape.145
  173.5 110.6 %all-gather.5.cloned.1.call-done = bf16[16,768,128]{2,1,0:T(8,128)(2,1)} async-done(((bf16[1,768,128]{2,1,0:T(8,128)(2,1)}), bf16[16,768,128]{2,1,0:T(8,128)(2,1)}) %all-gather.5.cloned.1.call-update) | async-done | bytes 3145744 | tf_op jit(solution)/shard_map/all_gather | solution.py:101
  284.2 154.9 %while.15 = (s32[]{:T(128)}, f32[1,768]{1,0:T(1,128)S(1)}, f32[1,768]{1,0:T(1,128)S(1)}, f32[1,768,128]{2,1,0:T(8,128)S(1)}, s32[16]{0:T(128)S(1)}, /*index=5*/s...) while((s32[]{:T(128)}, f32[1,768]{1,0:T(1,128)S(1)}, ...), condition=%wide.region_5.6_spmd.clone, body=%wide.region_0.5_spmd.clone.sunk | while | flops 309857280 | bytes 8516015 | solution.py:68
  287.9 7.3 %conditional.3 = ((f32[1,768]{1,0:T(1,128)S(1)}, f32[1,768]{1,0:T(1,128)S(1)}, f32[1,768,128]{2,1,0:T(8,128)S(1)})) conditional(s32[]{:T(128)} %convert_element_type.63, (f32[1,768]{1,0:T(1,128)S(1)}, f32[1,768]{1,0:T(1,128)S(1)}, f32[1,768,128]{2,1,0:T(8,128)S(1)}) %tuple.39, (s32[16]{0:T(128)S(1)}, s32[]{:T(128)}, s32[768]{0:T(1024)S(1)}, ...), branch_computations={%region_1.1_spmd, %region_2.4_spmd} | conditional | flops 309857280 | bytes 8512602 | solution.py:66
  298.9 7.3 %conditional.3 = ((f32[1,768]{1,0:T(1,128)S(1)}, f32[1,768]{1,0:T(1,128)S(1)}, f32[1,768,128]{2,1,0:T(8,128)S(1)})) conditional(s32[]{:T(128)} %convert_element_type.63, (f32[1,768]{1,0:T(1,128)S(1)}, f32[1,768]{1,0:T(1,128)S(1)}, f32[1,768,128]{2,1,0:T(8,128)S(1)}) %tuple.39, (s32[16]{0:T(128)S(1)}, s32[]{:T(128)}, s32[768]{0:T(1024)S(1)}, ...), branch_computations={%region_1.1_spmd, %region_2.4_spmd} | conditional | flops 309857280 | bytes 8512602 | solution.py:66
  310.0 7.3 %conditional.3 = ((f32[1,768]{1,0:T(1,128)S(1)}, f32[1,768]{1,0:T(1,128)S(1)}, f32[1,768,128]{2,1,0:T(8,128)S(1)})) conditional(s32[]{:T(128)} %convert_element_type.63, (f32[1,768]{1,0:T(1,128)S(1)}, f32[1,768]{1,0:T(1,128)S(1)}, f32[1,768,128]{2,1,0:T(8,128)S(1)}) %tuple.39, (s32[16]{0:T(128)S(1)}, s32[]{:T(128)}, s32[768]{0:T(1024)S(1)}, ...), branch_computations={%region_1.1_spmd, %region_2.4_spmd} | conditional | flops 309857280 | bytes 8512602 | solution.py:66
  321.0 7.3 %conditional.3 = ((f32[1,768]{1,0:T(1,128)S(1)}, f32[1,768]{1,0:T(1,128)S(1)}, f32[1,768,128]{2,1,0:T(8,128)S(1)})) conditional(s32[]{:T(128)} %convert_element_type.63, (f32[1,768]{1,0:T(1,128)S(1)}, f32[1,768]{1,0:T(1,128)S(1)}, f32[1,768,128]{2,1,0:T(8,128)S(1)}) %tuple.39, (s32[16]{0:T(128)S(1)}, s32[]{:T(128)}, s32[768]{0:T(1024)S(1)}, ...), branch_computations={%region_1.1_spmd, %region_2.4_spmd} | conditional | flops 309857280 | bytes 8512602 | solution.py:66
  332.1 7.3 %conditional.3 = ((f32[1,768]{1,0:T(1,128)S(1)}, f32[1,768]{1,0:T(1,128)S(1)}, f32[1,768,128]{2,1,0:T(8,128)S(1)})) conditional(s32[]{:T(128)} %convert_element_type.63, (f32[1,768]{1,0:T(1,128)S(1)}, f32[1,768]{1,0:T(1,128)S(1)}, f32[1,768,128]{2,1,0:T(8,128)S(1)}) %tuple.39, (s32[16]{0:T(128)S(1)}, s32[]{:T(128)}, s32[768]{0:T(1024)S(1)}, ...), branch_computations={%region_1.1_spmd, %region_2.4_spmd} | conditional | flops 309857280 | bytes 8512602 | solution.py:66
  343.1 7.3 %conditional.3 = ((f32[1,768]{1,0:T(1,128)S(1)}, f32[1,768]{1,0:T(1,128)S(1)}, f32[1,768,128]{2,1,0:T(8,128)S(1)})) conditional(s32[]{:T(128)} %convert_element_type.63, (f32[1,768]{1,0:T(1,128)S(1)}, f32[1,768]{1,0:T(1,128)S(1)}, f32[1,768,128]{2,1,0:T(8,128)S(1)}) %tuple.39, (s32[16]{0:T(128)S(1)}, s32[]{:T(128)}, s32[768]{0:T(1024)S(1)}, ...), branch_computations={%region_1.1_spmd, %region_2.4_spmd} | conditional | flops 309857280 | bytes 8512602 | solution.py:66
  354.2 7.3 %conditional.3 = ((f32[1,768]{1,0:T(1,128)S(1)}, f32[1,768]{1,0:T(1,128)S(1)}, f32[1,768,128]{2,1,0:T(8,128)S(1)})) conditional(s32[]{:T(128)} %convert_element_type.63, (f32[1,768]{1,0:T(1,128)S(1)}, f32[1,768]{1,0:T(1,128)S(1)}, f32[1,768,128]{2,1,0:T(8,128)S(1)}) %tuple.39, (s32[16]{0:T(128)S(1)}, s32[]{:T(128)}, s32[768]{0:T(1024)S(1)}, ...), branch_computations={%region_1.1_spmd, %region_2.4_spmd} | conditional | flops 309857280 | bytes 8512602 | solution.py:66
  365.2 7.3 %conditional.3 = ((f32[1,768]{1,0:T(1,128)S(1)}, f32[1,768]{1,0:T(1,128)S(1)}, f32[1,768,128]{2,1,0:T(8,128)S(1)})) conditional(s32[]{:T(128)} %convert_element_type.63, (f32[1,768]{1,0:T(1,128)S(1)}, f32[1,768]{1,0:T(1,128)S(1)}, f32[1,768,128]{2,1,0:T(8,128)S(1)}) %tuple.39, (s32[16]{0:T(128)S(1)}, s32[]{:T(128)}, s32[768]{0:T(1024)S(1)}, ...), branch_computations={%region_1.1_spmd, %region_2.4_spmd} | conditional | flops 309857280 | bytes 8512602 | solution.py:66
  380.0 7.3 %conditional.3 = ((f32[1,768]{1,0:T(1,128)S(1)}, f32[1,768]{1,0:T(1,128)S(1)}, f32[1,768,128]{2,1,0:T(8,128)S(1)})) conditional(s32[]{:T(128)} %convert_element_type.63, (f32[1,768]{1,0:T(1,128)S(1)}, f32[1,768]{1,0:T(1,128)S(1)}, f32[1,768,128]{2,1,0:T(8,128)S(1)}) %tuple.39, (s32[16]{0:T(128)S(1)}, s32[]{:T(128)}, s32[768]{0:T(1024)S(1)}, ...), branch_computations={%region_1.1_spmd, %region_2.4_spmd} | conditional | flops 309857280 | bytes 8512602 | solution.py:66
  394.8 7.3 %conditional.3 = ((f32[1,768]{1,0:T(1,128)S(1)}, f32[1,768]{1,0:T(1,128)S(1)}, f32[1,768,128]{2,1,0:T(8,128)S(1)})) conditional(s32[]{:T(128)} %convert_element_type.63, (f32[1,768]{1,0:T(1,128)S(1)}, f32[1,768]{1,0:T(1,128)S(1)}, f32[1,768,128]{2,1,0:T(8,128)S(1)}) %tuple.39, (s32[16]{0:T(128)S(1)}, s32[]{:T(128)}, s32[768]{0:T(1024)S(1)}, ...), branch_computations={%region_1.1_spmd, %region_2.4_spmd} | conditional | flops 309857280 | bytes 8512602 | solution.py:66
  409.6 7.3 %conditional.3 = ((f32[1,768]{1,0:T(1,128)S(1)}, f32[1,768]{1,0:T(1,128)S(1)}, f32[1,768,128]{2,1,0:T(8,128)S(1)})) conditional(s32[]{:T(128)} %convert_element_type.63, (f32[1,768]{1,0:T(1,128)S(1)}, f32[1,768]{1,0:T(1,128)S(1)}, f32[1,768,128]{2,1,0:T(8,128)S(1)}) %tuple.39, (s32[16]{0:T(128)S(1)}, s32[]{:T(128)}, s32[768]{0:T(1024)S(1)}, ...), branch_computations={%region_1.1_spmd, %region_2.4_spmd} | conditional | flops 309857280 | bytes 8512602 | solution.py:66
  420.7 7.3 %conditional.3 = ((f32[1,768]{1,0:T(1,128)S(1)}, f32[1,768]{1,0:T(1,128)S(1)}, f32[1,768,128]{2,1,0:T(8,128)S(1)})) conditional(s32[]{:T(128)} %convert_element_type.63, (f32[1,768]{1,0:T(1,128)S(1)}, f32[1,768]{1,0:T(1,128)S(1)}, f32[1,768,128]{2,1,0:T(8,128)S(1)}) %tuple.39, (s32[16]{0:T(128)S(1)}, s32[]{:T(128)}, s32[768]{0:T(1024)S(1)}, ...), branch_computations={%region_1.1_spmd, %region_2.4_spmd} | conditional | flops 309857280 | bytes 8512602 | solution.py:66
  431.7 7.3 %conditional.3 = ((f32[1,768]{1,0:T(1,128)S(1)}, f32[1,768]{1,0:T(1,128)S(1)}, f32[1,768,128]{2,1,0:T(8,128)S(1)})) conditional(s32[]{:T(128)} %convert_element_type.63, (f32[1,768]{1,0:T(1,128)S(1)}, f32[1,768]{1,0:T(1,128)S(1)}, f32[1,768,128]{2,1,0:T(8,128)S(1)}) %tuple.39, (s32[16]{0:T(128)S(1)}, s32[]{:T(128)}, s32[768]{0:T(1024)S(1)}, ...), branch_computations={%region_1.1_spmd, %region_2.4_spmd} | conditional | flops 309857280 | bytes 8512602 | solution.py:66
  442.1 7.8 %all-to-all-start.3 = ((bf16[32,2,1536]{2,1,0:T(2,128)(2,1)}), bf16[32,2,1536]{2,1,0:T(2,128)(2,1)S(1)}, u32[]{:S(2)}, u32[]{:S(2)}) async-start(bf16[32,2,1536]{2,1,0:T(2,128)(2,1)} %reshape.148), calls=%async_computation.3 | async-start | bytes 393216 | tf_op jit(solution)/shard_map/all_to_all | solution.py:108
  450.6 6.7 %all-to-all-done.3 = bf16[32,2,1536]{2,1,0:T(2,128)(2,1)S(1)} async-done(((bf16[32,2,1536]{2,1,0:T(2,128)(2,1)}), bf16[32,2,1536]{2,1,0:T(2,128)(2,1)S(1)}, u32[]{:S(2)}, u32[]{:S(2)}) %all-to-all-start.3) | async-done | bytes 196640 | tf_op jit(solution)/shard_map/all_to_all | solution.py:108
  461.1 24.4 %collective-permute-done = bf16[1,24,4096]{2,1,0:T(8,128)(2,1)S(1)} collective-permute-done((bf16[1,24,4096]{2,1,0:T(8,128)(2,1)S(1)}, bf16[1,24,4096]{2,1,0:T(8,128)(2,1)S(1)}, u32[]{:S(2)}, u32[]{:S(2)}) %collective-permute-start) | collective-permute-done | bytes 196640 | tf_op jit(solution)/shard_map/ppermute | solution.py:12
  (209 shorter events, 107.6 us)
Async XLA Ops:
  7.2 443.4 %copy-start = (f32[16,4096]{1,0:T(8,128)S(1)}, f32[16,4096]{1,0:T(8,128)}, u32[]{:S(2)}) copy-start(f32[16,4096]{1,0:T(8,128)} %param.21) | copy-start | bytes 786436
  7.2 166.4 %all-gather.3.cloned.1.call-start = ((), (), s32[]{:S(2)}) async-start(), calls=%async_computation.4 | async-start | bytes 3342336 | tf_op jit(solution)/shard_map/all_gather | solution.py:100
  54.1 3.2 copy-start.1
  57.1 227.0 %all-gather.5.cloned.1.call-start = ((), (), s32[]{:S(2)}) async-start(), calls=%async_computation.5 | async-start | bytes 3342336 | tf_op jit(solution)/shard_map/all_gather | solution.py:101
  102.9 3.0 copy-start.2
  133.1 35.1 %all-to-all-start.1 = ((bf16[32,2,1536]{2,1,0:T(2,128)(2,1)}), bf16[32,2,1536]{2,1,0:T(2,128)(2,1)S(1)}, u32[]{:S(2)}, u32[]{:S(2)}) async-start(bf16[32,2,1536]{2,1,0:T(2,128)(2,1)} %reshape.144), calls=%async_computation.1 | async-start | bytes 393216 | tf_op jit(solution)/shard_map/all_to_all | solution.py:91
  171.2 112.9 %copy-start.6 = (s32[16]{0:T(128)S(1)}, s32[16]{0:T(128)}, u32[]{:S(2)}) copy-start(s32[16]{0:T(128)} %param.19) | copy-start | bytes 196
  439.1 20.5 %copy-start.3 = (bf16[1,24,4096]{2,1,0:T(8,128)(2,1)S(1)}, bf16[1,24,4096]{2,1,0:T(8,128)(2,1)}, u32[]{:S(2)}) copy-start(bf16[1,24,4096]{2,1,0:T(8,128)(2,1)} %param.16) | copy-start | bytes 589828
  439.3 46.2 %copy-start.4 = (bf16[24,4096]{1,0:T(8,128)(2,1)S(1)}, bf16[24,4096]{1,0:T(8,128)(2,1)}, u32[]{:S(2)}) copy-start(bf16[24,4096]{1,0:T(8,128)(2,1)} %param.17) | copy-start | bytes 589828
  442.1 15.2 %all-to-all-start.3 = ((bf16[32,2,1536]{2,1,0:T(2,128)(2,1)}), bf16[32,2,1536]{2,1,0:T(2,128)(2,1)S(1)}, u32[]{:S(2)}, u32[]{:S(2)}) async-start(bf16[32,2,1536]{2,1,0:T(2,128)(2,1)} %reshape.148), calls=%async_computation.3 | async-start | bytes 393216 | tf_op jit(solution)/shard_map/all_to_all | solution.py:108
  459.7 26.5 %copy-start.5 = (bf16[1,24,4096]{2,1,0:T(8,128)(2,1)}, bf16[1,24,4096]{2,1,0:T(8,128)(2,1)S(1)}, u32[]{:S(2)}) copy-start(bf16[1,24,4096]{2,1,0:T(8,128)(2,1)S(1)} %fusion.25) | copy-start | bytes 589828
  459.8 25.7 %collective-permute-start = (bf16[1,24,4096]{2,1,0:T(8,128)(2,1)S(1)}, bf16[1,24,4096]{2,1,0:T(8,128)(2,1)S(1)}, u32[]{:S(2)}, u32[]{:S(2)}) collective-permute-start(bf16[1,24,4096]{2,1,0:T(8,128)(2,1)S(1)} %fusion.25), channel_id=1, source_target_pairs={{0,32},{32,64},{64,96},{96,128},{128,160},{160,192},{192,224},{224... | collective-permute-start | bytes 589832 | tf_op jit(solution)/shard_map/ppermute | solution.py:12
Sparse Core Ops, SparseCore 0:
  57.2 110.2 all-gather.2
  170.6 113.5 all-gather.4
where the time goes:
time: 495 us; the launch traced here: 493 us
  waiting for transfers between devices  169 us (34%)
  other arithmetic  89.1 us (18%)
  loops' own time  67.1 us (14%)
  local copies, waits for them, and re-layouts  61.2 us (12%)
  matrix products  43.8 us (9%)
  blocking collectives  31.2 us (6%)
  starting transfers between devices  16.2 us (3%)
  between operations  15.1 us (3%)
    all_gather x1, waiting for transfers between devices, local(): lax.all_gather(values_moved, 'section', axis=0, tiled=True)  111 us
    unnamed x4, other arithmetic  69 us
    another operation x1, loops' own time, attend(): carry, _ = lax.scan(visit, carry, jnp.arange(pieces_held, dtype=jnp.int32))  41 us
    all_to_all x1, waiting for transfers between devices, local(): lax.all_to_all(queries, 'seq', split_axis=2, concat_axis=1, tiled=True)  27.5 us
    another operation x16, loops' own time, visit(): return (lax.cond(flag == 1, work, skip, inner), None)  26.1 us
    unnamed x29, local copies, waits for them, and re-layouts  25.2 us
    dot_general x13, matrix products, work(): jnp.einsum('hij,jhd->hid', weights.astype(jnp.bfloat16), value_tile, pref...  24.8 us
    ppermute x1, waiting for transfers between devices, shifted(): lax.ppermute(value, axis, [(source, source + steps) for source in range(l...  24.4 us
  transfers between devices with their start and end apart: 5, of which 4 were waited for; matrix products, arithmetic and copies ran while one was open for 13% of the time, Pallas kernels for 0%

commit v1 on v0

v1 whole, which is shorter than its diff:
```python
import math

import jax
import jax.numpy as jnp
from jax import lax
from jax.experimental import pallas as pl
from jax.experimental.pallas import tpu as pltpu
from jax.sharding import Mesh
from jax.sharding import PartitionSpec as P

HD = 128
HEADS = 32
ROWS = 24
QUARTER = 192
BLOCK = 768
STAT = 16
SCALE = math.log2(math.e) / math.sqrt(HD)
LOW = -1e30
f32 = jnp.float32
bf16 = jnp.bfloat16

VM = pl.BlockSpec(memory_space=pltpu.VMEM)
SM = pl.BlockSpec(memory_space=pltpu.SMEM)
PARAMS = pltpu.CompilerParams(vmem_limit_bytes=48 * 2**20)
HEAD_AXES = ("zh", "zl", "c")


def pack_kernel(q_ref, k_ref, v_ref, o_ref):
    for i, ref in enumerate((q_ref, k_ref, v_ref)):
        for h in range(HEADS):
            o_ref[h, i] = ref[0, :, h * HD : (h + 1) * HD]


def pack(queries, keys, values):
    return pl.pallas_call(
        pack_kernel,
        out_shape=jax.ShapeDtypeStruct((HEADS, 3, ROWS, HD), bf16),
        in_specs=[VM] * 3,
        out_specs=VM,
        compiler_params=PARAMS,
    )(queries, keys, values)


def token_of(shape, dim, y):
    i = lax.broadcasted_iota(jnp.int32, shape, dim)
    one, nil = jnp.int32(1), jnp.int32(0)
    part = sum(jnp.where(i >= e * QUARTER, one, nil) for e in (1, 2, 3))
    inner = i - part * QUARTER
    run = sum(jnp.where(inner >= e * 48, one, nil) for e in (1, 2, 3))
    return inner + run * (QUARTER - 48) + ((y + part) & 3) * 48


def attend_kernel(
    count_ref, flag_ref, y_ref, q0, q1, q2, q3, kv0, kv1, kv2, kv3, o_ref,
    q_sc, k_sc, v_sc, m_sc, acc_sc, s0, s1, p0, p1, a0, a1, units,
):
    def build(e, n):
        slot, t = e // 4, e % 4
        active = flag_ref[slot * 4, t]
        for g in range(1, 4):
            active = active | flag_ref[slot * 4 + g, t]

        @pl.when(active == 1)
        def _():
            units[0, n] = slot
            units[1, n] = t

        return n + active

    for i in range(2):
        units[0, i] = 4
        units[1, i] = 0
    n = lax.fori_loop(0, 16, build, jnp.int32(2))
    for i in range(4):
        units[0, n + i] = 4
        units[1, n + i] = 0

    for slot, ref in enumerate((q0, q1, q2, q3)):
        q_sc[slot] = ref[...].reshape(BLOCK, HD)

    token = token_of((BLOCK, HD), 0, y_ref[0])
    token_row = token_of((STAT, BLOCK), 1, y_ref[0])
    for t in range(4):
        k = jnp.concatenate([ref[t, :, 0].reshape(QUARTER, HD) for ref in (kv0, kv1, kv2, kv3)])
        v = jnp.concatenate([ref[t, :, 1].reshape(QUARTER, HD) for ref in (kv0, kv1, kv2, kv3)])
        valid = token < count_ref[t]
        k_sc[t] = jnp.where(valid, k, jnp.broadcast_to(k[0:1], k.shape))
        v_sc[t, :HD] = jnp.where(valid, v, jnp.zeros_like(v)).T
        v_sc[t, HD:] = jnp.where(token_row < count_ref[t], 1.0, 0.0).astype(bf16)

    m_sc[...] = jnp.full(m_sc.shape, LOW, f32)
    acc_sc[...] = jnp.zeros(acc_sc.shape, f32)
    lane = lax.broadcasted_iota(jnp.int32, (8, BLOCK), 1)

    def score(i, s):
        slot = jnp.minimum(units[0, i], 3)
        s[...] = lax.dot_general(
            k_sc[units[1, i]], q_sc[slot], (((1,), (1,)), ((), ())), preferred_element_type=f32
        )

    def weigh(i, s, p, a):
        slot, t = units[0, i], units[1, i]
        first = jnp.minimum(slot, 3) * 4
        flag = jnp.full((8, BLOCK), flag_ref[first, t], jnp.int32)
        for g in range(1, 4):
            flag = jnp.where(lane >= g * QUARTER, flag_ref[first + g, t], flag)
        on = flag == 1
        old = m_sc[slot]
        top = jnp.max(s[...], axis=0, keepdims=True) * SCALE
        new = jnp.where(on, jnp.maximum(old, top), old)
        m_sc[slot] = new
        a[...] = jnp.exp2(old - new)
        p[...] = jnp.exp2(s[...] * SCALE - jnp.where(on, new, -LOW)[:1]).astype(bf16)

    def gather(i, p, a):
        slot = units[0, i]
        part = jnp.dot(v_sc[units[1, i]], p[...], preferred_element_type=f32)
        acc_sc[slot] = acc_sc[slot] * a[:1] + part

    def step(h, carry):
        i = 2 + 2 * h
        gather(i - 2, p0, a0)
        weigh(i - 1, s1, p1, a1)
        score(i, s0)
        gather(i - 1, p1, a1)
        weigh(i, s0, p0, a0)
        score(i + 1, s1)
        return carry

    p0[...] = jnp.zeros(p0.shape, bf16)
    p1[...] = jnp.zeros(p1.shape, bf16)
    s1[...] = jnp.zeros(s1.shape, f32)
    lax.fori_loop(0, (n + 1) // 2, step, 0)

    for slot in range(4):
        total = acc_sc[slot, HD : HD + 1]
        some = total > 0.0
        safe = jnp.where(some, total, 1.0)
        o_ref[slot, :HD] = (acc_sc[slot, :HD] * (1.0 / safe)).astype(bf16)
        level = jnp.where(some, m_sc[slot, :1] + jnp.log2(safe), LOW)
        hi = level.astype(bf16)
        mid = (level - hi.astype(f32)).astype(bf16)
        lo = (level - hi.astype(f32) - mid.astype(f32)).astype(bf16)
        pad = jnp.zeros((STAT - 3, BLOCK), bf16)
        o_ref[slot, HD:] = jnp.concatenate([hi, mid, lo, pad], axis=0)


def attend(counts, flags, y, qs, kvs):
    vmem = pltpu.VMEM
    return pl.pallas_call(
        attend_kernel,
        out_shape=jax.ShapeDtypeStruct((4, HD + STAT, BLOCK), bf16),
        in_specs=[SM] * 3 + [VM] * 8,
        out_specs=VM,
        scratch_shapes=[
            vmem((4, BLOCK, HD), bf16),
            vmem((4, BLOCK, HD), bf16),
            vmem((4, HD + STAT, BLOCK), bf16),
            vmem((5, 8, BLOCK), f32),
            vmem((5, HD + STAT, BLOCK), f32),
            vmem((BLOCK, BLOCK), f32),
            vmem((BLOCK, BLOCK), f32),
            vmem((BLOCK, BLOCK), bf16),
            vmem((BLOCK, BLOCK), bf16),
            vmem((8, BLOCK), f32),
            vmem((8, BLOCK), f32),
            pltpu.SMEM((2, 24), jnp.int32),
        ],
        compiler_params=PARAMS,
    )(counts, flags, y, *qs, *kvs)


def merge_kernel(x_ref, r0, r1, r2, r3, o_ref):
    refs = (r0, r1, r2, r3)
    levels = []
    for k, ref in enumerate(refs):
        stat = ref[HD:].astype(f32)
        level = stat[0:1] + stat[1:2] + stat[2:3]
        levels.append(jnp.where(x_ref[0] >= k, level, LOW) if k else level)
    top = jnp.maximum(jnp.maximum(levels[0], levels[1]), jnp.maximum(levels[2], levels[3]))
    shares = [jnp.exp2(level - top) for level in levels]
    whole = shares[0] + shares[1] + shares[2] + shares[3]
    total = sum(ref[:HD].astype(f32) * (share / whole) for ref, share in zip(refs, shares))
    o_ref[...] = total.T.astype(bf16).reshape(HEADS, ROWS, HD)


def merge(x, parts):
    return pl.pallas_call(
        merge_kernel,
        out_shape=jax.ShapeDtypeStruct((HEADS, ROWS, HD), bf16),
        in_specs=[SM] + [VM] * 4,
        out_specs=VM,
        compiler_params=PARAMS,
    )(x, *parts)


def finish_kernel(level_ref, r_ref, latent_ref, gate_ref, o_ref):
    squares = jnp.zeros((ROWS, HD), f32)
    for h in range(HEADS):
        wide = r_ref[h].astype(f32)
        squares = squares + wide * wide
    mean = jnp.sum(squares, axis=-1, keepdims=True) * (1.0 / (HEADS * HD))
    factor = 1.0 / jnp.sqrt(mean + 1e-06)
    mine = lax.broadcasted_iota(jnp.int32, (gate_ref.shape[0], HD), 0) == level_ref[0]
    for h in range(HEADS):
        span = slice(h * HD, (h + 1) * HD)
        gate = jnp.sum(jnp.where(mine, gate_ref[:, span], 0.0), axis=0, keepdims=True)
        wide = r_ref[h].astype(f32)
        o_ref[0, :, span] = (
            latent_ref[0, :, span].astype(f32) + gate * (wide * factor)
        ).astype(bf16)


def finish(noise_level, returned, latent, gate_table):
    return pl.pallas_call(
        finish_kernel,
        out_shape=jax.ShapeDtypeStruct(latent.shape, bf16),
        in_specs=[SM] + [VM] * 3,
        out_specs=VM,
        compiler_params=PARAMS,
    )(noise_level, returned, latent, gate_table)


def local(
    queries, keys, values, latent, entering, noise_level, token_counts, block_mask, gate_table
):
    x = lax.axis_index("x")
    y = lax.axis_index("y")
    packed = pack(queries, keys, values)
    packed = lax.all_to_all(packed, HEAD_AXES, split_axis=0, concat_axis=0, tiled=True)
    kv = packed[:, 1:3].reshape(4, 8, 2, ROWS, HD)
    q = packed[:, 0]
    kvs = [kv] + [
        lax.ppermute(kv, "y", [(source, (source - k) % 4) for source in range(4)])
        for k in (1, 2, 3)
    ]
    qs = [q] + [
        lax.ppermute(q, "x", [(source, source - k) for source in range(k, 4)]) for k in (1, 2, 3)
    ]
    padded = jnp.concatenate([block_mask, jnp.zeros_like(block_mask)], axis=0)
    flags = lax.dynamic_slice(padded, (4 * x, 4 * x), (16, 4))
    counts = lax.dynamic_slice(token_counts, (4 * x,), (4,))
    parts = attend(counts, flags, y.reshape(1), qs, kvs)
    received = [parts[0]] + [
        lax.ppermute(parts[k], "x", [(source, source + k) for source in range(4 - k)])
        for k in (1, 2, 3)
    ]
    attended = merge(x.reshape(1), received)
    returned = lax.all_to_all(attended, HEAD_AXES, split_axis=0, concat_axis=0, tiled=True)
    updated = finish(noise_level, returned, latent, gate_table)
    moved = lax.ppermute(updated, ("x", "zh"), [(s, s + 1) for s in range(15)])
    first = (x == 0) & (lax.axis_index("zh") == 0)
    advanced = jnp.where(first, entering[None], moved)
    return (updated, advanced)


def solution(mesh):
    fine = Mesh(mesh.devices.reshape(4, 4, 4, 4, 2), ("x", "zh", "zl", "y", "c"))
    section, seq = ("x", "zh"), ("zl", "y", "c")
    placed = (
        P(section, seq, None),
        P(section, seq, None),
        P(section, seq, None),
        P(section, seq, None),
        P(seq, None),
        P(section),
        P(),
        P(),
        P(),
    )
    return jax.shard_map(
        local,
        mesh=fine,
        in_specs=placed,
        out_specs=(P(section, seq, None), P(section, seq, None)),
        check_vma=False,
    )
```

time: 495 us -> 163 us (0.33)
  the two profiles are of different devices: /device:TPU:486 before, /device:TPU:102 now
where the time goes in v1:
time: 163 us
  waiting for transfers between devices  69.2 us (42%)
  blocking collectives  47.5 us (29%)
  starting transfers between devices  31.1 us (19%)
  Pallas kernels  9.18 us (6%)
  local copies, waits for them, and re-layouts  3.72 us (2%)
    all_to_all x1, blocking collectives, local(): lax.all_to_all(packed, HEAD_AXES, split_axis=0, concat_axis=0, tiled=True)  47.5 us
    ppermute x1, waiting for transfers between devices, local(): moved = lax.ppermute(updated, ('x', 'zh'), [(s, s + 1) for s in range(15)])  23.7 us
    ppermute x3, waiting for transfers between devices, local(): lax.ppermute(parts[k], 'x', [(source, source + k) for source in range(4 -...  17.8 us
    all_to_all x1, waiting for transfers between devices, local(): lax.all_to_all(attended, HEAD_AXES, split_axis=0, concat_axis=0, tiled=True)  16.4 us
    ppermute x3, starting transfers between devices, local(): lax.ppermute(kv, 'y', [(source, (source - k) % 4) for source in range(4)])  10.3 us
    ppermute x3, waiting for transfers between devices, local(): lax.ppermute(kv, 'y', [(source, (source - k) % 4) for source in range(4)])  7.8 us
    all_to_all x1, starting transfers between devices, local(): lax.all_to_all(attended, HEAD_AXES, split_axis=0, concat_axis=0, tiled=True)  7.63 us
    pallas_call x1, Pallas kernels, attend(): pl.pallas_call(attend_kernel, out_shape=jax.ShapeDtypeStruct((4, HD + STA...  7.23 us
  transfers between devices with their start and end apart: 11, of which 9 were waited for; matrix products, arithmetic and copies ran while one was open for 0% of the time, Pallas kernels for 0%

profile of v1, /device:TPU:102, one launch (start us, length us, event | category | flops | bytes accessed | tf_op | source)
XLA Modules:
  0.0 162.8 jit_solution(10884241171969142655)
XLA Ops:
  0.6 0.9 copy-done.1
  1.6 0.9 copy-done.2
  2.5 0.9 copy-done.3
  3.4 0.1 shard_map.104
  3.5 47.5 %all_to_all.10 = bf16[32,3,24,128]{3,2,1,0:T(8,128)(2,1)S(1)} all-to-all(bf16[32,3,24,128]{3,2,1,0:T(8,128)(2,1)S(1)} %shard_map.104), channel_id=1, replica_groups=mesh['x'=4,'zh'=4,'zl'=4,'y'=4,'c'=2] {'zh','zl','c'}, dimensions={0} | all-to-all | bytes 1179648 | tf_op jit(solution)/shard_map/all_to_all | solution.py:230
  51.0 2.7 %collective-permute-start = (bf16[32,24,128]{2,1,0:T(8,128)(2,1)S(1)}, bf16[32,24,128]{2,1,0:T(8,128)(2,1)S(1)}, u32[]{:S(2)}, u32[]{:S(2)}) collective-permute-start(bf16[32,24,128]{2,1,0:T(8,128)(2,1)S(1)} %slice_bitcast_fusion.4.q0), channel_id=1, source_target_pairs={{128,0},{256,128},{384,256},{129,1},{257,129},{385,257},{130,2},{2... | collective-permute-start | bytes 589832 | tf_op jit(solution)/shard_map/ppermute | solution.py:238
  53.8 4.9 %collective-permute-start.3 = (bf16[4,8,2,24,128]{4,3,2,1,0:T(8,128)(2,1)S(1)}, bf16[4,8,2,24,128]{4,3,2,1,0:T(8,128)(2,1)S(1)}, u32[]{:S(2)}, u32[]{:S(2)}) collective-permute-start(bf16[4,8,2,24,128]{4,3,2,1,0:T(8,128)(2,1)S(1)} %bitcast.17), channel_id=1, source_target_pairs={{0,6},{2,0},{4,2},{6,4},{1,7},{3,1},{5,3},{7,5},{8,14},{10,8},{12,... | collective-permute-start | bytes 1179656 | tf_op jit(solution)/shard_map/ppermute | solution.py:234
  58.8 2.5 %collective-permute-start.4 = (bf16[4,8,2,24,128]{4,3,2,1,0:T(8,128)(2,1)S(1)}, bf16[4,8,2,24,128]{4,3,2,1,0:T(8,128)(2,1)S(1)}, u32[]{:S(2)}, u32[]{:S(2)}) collective-permute-start(bf16[4,8,2,24,128]{4,3,2,1,0:T(8,128)(2,1)S(1)} %bitcast.18), channel_id=1, source_target_pairs={{0,4},{2,6},{4,0},{6,2},{1,5},{3,7},{5,1},{7,3},{8,12},{10,14},{12... | collective-permute-start | bytes 1179656 | tf_op jit(solution)/shard_map/ppermute | solution.py:234
  61.3 2.9 %collective-permute-start.5 = (bf16[4,8,2,24,128]{4,3,2,1,0:T(8,128)(2,1)S(1)}, bf16[4,8,2,24,128]{4,3,2,1,0:T(8,128)(2,1)S(1)}, u32[]{:S(2)}, u32[]{:S(2)}) collective-permute-start(bf16[4,8,2,24,128]{4,3,2,1,0:T(8,128)(2,1)S(1)} %bitcast.19), channel_id=1, source_target_pairs={{0,2},{2,4},{4,6},{6,0},{1,3},{3,5},{5,7},{7,1},{8,10},{10,12},{12... | collective-permute-start | bytes 1179656 | tf_op jit(solution)/shard_map/ppermute | solution.py:234
  64.2 3.0 %collective-permute-start.1 = (bf16[32,24,128]{2,1,0:T(8,128)(2,1)S(1)}, bf16[32,24,128]{2,1,0:T(8,128)(2,1)S(1)}, u32[]{:S(2)}, u32[]{:S(2)}) collective-permute-start(bf16[32,24,128]{2,1,0:T(8,128)(2,1)S(1)} %slice_bitcast_fusion.4.q0), channel_id=1, source_target_pairs={{256,0},{384,128},{257,1},{385,129},{258,2},{386,130},{259,3},{387... | collective-permute-start | bytes 589832 | tf_op jit(solution)/shard_map/ppermute | solution.py:238
  67.2 1.3 collective-permute-start.2
  68.6 0.6 copy-done.7
  69.2 0.1 dynamic_slice.6.count_ref
  69.3 0.1 pad_dynamic-slice_fusion.flag_ref
  69.4 1.0 collective-permute-done.1.q2
  70.4 2.5 %collective-permute-done.2.q3 = bf16[32,24,128]{2,1,0:T(8,128)(2,1)S(1)} collective-permute-done((bf16[32,24,128]{2,1,0:T(8,128)(2,1)S(1)}, bf16[32,24,128]{2,1,0:T(8,128)(2,1)S(1)}, u32[]{:S(2)}, u32[]{:S(2)}) %collective-permute-start.2) | collective-permute-done | bytes 196640 | tf_op jit(solution)/shard_map/ppermute | solution.py:238
  72.8 2.2 %collective-permute-done.3.kv1 = bf16[4,8,2,24,128]{4,3,2,1,0:T(8,128)(2,1)S(1)} collective-permute-done((bf16[4,8,2,24,128]{4,3,2,1,0:T(8,128)(2,1)S(1)}, bf16[4,8,2,24,128]{4,3,2,1,0:T(8,128)(2,1)S(1)}, u32[]{:S(2)}, u32[]{:S(2)}) %collective-permute-start.3) | collective-permute-done | bytes 393248 | tf_op jit(solution)/shard_map/ppermute | solution.py:234
  75.0 5.6 %collective-permute-done.5.kv3 = bf16[4,8,2,24,128]{4,3,2,1,0:T(8,128)(2,1)S(1)} collective-permute-done((bf16[4,8,2,24,128]{4,3,2,1,0:T(8,128)(2,1)S(1)}, bf16[4,8,2,24,128]{4,3,2,1,0:T(8,128)(2,1)S(1)}, u32[]{:S(2)}, u32[]{:S(2)}) %collective-permute-start.5) | collective-permute-done | bytes 393248 | tf_op jit(solution)/shard_map/ppermute | solution.py:234
  80.6 7.2 %shard_map.105 = bf16[4,144,768]{2,1,0:T(8,128)(2,1)S(1)} custom-call(s32[4]{0:T(128)S(1)} %dynamic_slice.6.count_ref, s32[16,4]{1,0:T(8,128)S(1)} %pad_dynamic-slice_fusion.flag_ref, s32[1]{0:T(128)} %bitcast.1.y_ref, bf16[32,24,128]{2,1,0:T(8,128)(2,1)S(1)} %slice_bitcast_fusion.4.q0, bf16[32,24,128]{2,1,0:T(8,128)(2,1)S(1)} %collective-permute-done.q1, ...), custom_call_target="tpu_custom_call" | custom-call | tf_op jit(solution)/shard_map/pallas_call | solution.py:150
  87.9 1.3 collective-permute-start.6
  89.2 1.3 collective-permute-start.7
  90.5 1.3 collective-permute-start.8
  91.8 7.7 %collective-permute-done.6.r1 = bf16[144,768]{1,0:T(8,128)(2,1)S(1)} collective-permute-done((bf16[144,768]{1,0:T(8,128)(2,1)S(1)}, bf16[144,768]{1,0:T(8,128)(2,1)S(1)}, u32[]{:S(2)}, u32[]{:S(2)}) %collective-permute-start.6) | collective-permute-done | bytes 221216 | tf_op jit(solution)/shard_map/ppermute | solution.py:245
  99.5 5.5 %collective-permute-done.7.r2 = bf16[144,768]{1,0:T(8,128)(2,1)S(1)} collective-permute-done((bf16[144,768]{1,0:T(8,128)(2,1)S(1)}, bf16[144,768]{1,0:T(8,128)(2,1)S(1)}, u32[]{:S(2)}, u32[]{:S(2)}) %collective-permute-start.7) | collective-permute-done | bytes 221216 | tf_op jit(solution)/shard_map/ppermute | solution.py:245
  105.1 4.6 %collective-permute-done.8.r3 = bf16[144,768]{1,0:T(8,128)(2,1)S(1)} collective-permute-done((bf16[144,768]{1,0:T(8,128)(2,1)S(1)}, bf16[144,768]{1,0:T(8,128)(2,1)S(1)}, u32[]{:S(2)}, u32[]{:S(2)}) %collective-permute-start.8) | collective-permute-done | bytes 221216 | tf_op jit(solution)/shard_map/ppermute | solution.py:245
  109.7 1.0 shard_map.106
  110.7 7.6 %all-to-all-start.1 = ((bf16[32,24,128]{2,1,0:T(8,128)(2,1)}), bf16[32,24,128]{2,1,0:T(8,128)(2,1)S(1)}, u32[]{:S(2)}, u32[]{:S(2)}) async-start(bf16[32,24,128]{2,1,0:T(8,128)(2,1)} %shard_map.106), calls=%async_computation.1 | async-start | bytes 393216 | tf_op jit(solution)/shard_map/all_to_all | solution.py:249
  119.0 16.4 %all-to-all-done.1.r_ref = bf16[32,24,128]{2,1,0:T(8,128)(2,1)S(1)} async-done(((bf16[32,24,128]{2,1,0:T(8,128)(2,1)}), bf16[32,24,128]{2,1,0:T(8,128)(2,1)S(1)}, u32[]{:S(2)}, u32[]{:S(2)}) %all-to-all-start.1) | async-done | bytes 196640 | tf_op jit(solution)/shard_map/all_to_all | solution.py:249
  135.3 0.9 shard_map.107
  136.2 2.2 %collective-permute-start.9 = (bf16[1,24,4096]{2,1,0:T(8,128)(2,1)}, bf16[1,24,4096]{2,1,0:T(8,128)(2,1)S(1)}, u32[]{:S(2)}, u32[]{:S(2)}) collective-permute-start(bf16[1,24,4096]{2,1,0:T(8,128)(2,1)} %shard_map.107), channel_id=1, source_target_pairs={{0,32},{32,64},{64,96},{96,128},{128,160},{160,192},{192,224},{224... | collective-permute-start | bytes 589832 | tf_op jit(solution)/shard_map/ppermute | solution.py:251
  138.4 23.7 %collective-permute-done.9 = bf16[1,24,4096]{2,1,0:T(8,128)(2,1)S(1)} collective-permute-done((bf16[1,24,4096]{2,1,0:T(8,128)(2,1)}, bf16[1,24,4096]{2,1,0:T(8,128)(2,1)S(1)}, u32[]{:S(2)}, u32[]{:S(2)}) %collective-permute-start.9) | collective-permute-done | bytes 196640 | tf_op jit(solution)/shard_map/ppermute | solution.py:251
  162.1 0.7 bitcast_select_fusion
  (17 shorter events, 0.2 us)
Async XLA Ops:
  0.6 0.9 copy-start.1
  1.6 0.9 copy-start.2
  2.5 0.9 copy-start.3
  51.0 16.2 %collective-permute-start = (bf16[32,24,128]{2,1,0:T(8,128)(2,1)S(1)}, bf16[32,24,128]{2,1,0:T(8,128)(2,1)S(1)}, u32[]{:S(2)}, u32[]{:S(2)}) collective-permute-start(bf16[32,24,128]{2,1,0:T(8,128)(2,1)S(1)} %slice_bitcast_fusion.4.q0), channel_id=1, source_target_pairs={{128,0},{256,128},{384,256},{129,1},{257,129},{385,257},{130,2},{2... | collective-permute-start | bytes 589832 | tf_op jit(solution)/shard_map/ppermute | solution.py:238
  53.8 21.2 %collective-permute-start.3 = (bf16[4,8,2,24,128]{4,3,2,1,0:T(8,128)(2,1)S(1)}, bf16[4,8,2,24,128]{4,3,2,1,0:T(8,128)(2,1)S(1)}, u32[]{:S(2)}, u32[]{:S(2)}) collective-permute-start(bf16[4,8,2,24,128]{4,3,2,1,0:T(8,128)(2,1)S(1)} %bitcast.17), channel_id=1, source_target_pairs={{0,6},{2,0},{4,2},{6,4},{1,7},{3,1},{5,3},{7,5},{8,14},{10,8},{12,... | collective-permute-start | bytes 1179656 | tf_op jit(solution)/shard_map/ppermute | solution.py:234
  58.8 16.3 %collective-permute-start.4 = (bf16[4,8,2,24,128]{4,3,2,1,0:T(8,128)(2,1)S(1)}, bf16[4,8,2,24,128]{4,3,2,1,0:T(8,128)(2,1)S(1)}, u32[]{:S(2)}, u32[]{:S(2)}) collective-permute-start(bf16[4,8,2,24,128]{4,3,2,1,0:T(8,128)(2,1)S(1)} %bitcast.18), channel_id=1, source_target_pairs={{0,4},{2,6},{4,0},{6,2},{1,5},{3,7},{5,1},{7,3},{8,12},{10,14},{12... | collective-permute-start | bytes 1179656 | tf_op jit(solution)/shard_map/ppermute | solution.py:234
  61.3 19.3 %collective-permute-start.5 = (bf16[4,8,2,24,128]{4,3,2,1,0:T(8,128)(2,1)S(1)}, bf16[4,8,2,24,128]{4,3,2,1,0:T(8,128)(2,1)S(1)}, u32[]{:S(2)}, u32[]{:S(2)}) collective-permute-start(bf16[4,8,2,24,128]{4,3,2,1,0:T(8,128)(2,1)S(1)} %bitcast.19), channel_id=1, source_target_pairs={{0,2},{2,4},{4,6},{6,0},{1,3},{3,5},{5,7},{7,1},{8,10},{10,12},{12... | collective-permute-start | bytes 1179656 | tf_op jit(solution)/shard_map/ppermute | solution.py:234
  64.2 6.2 %collective-permute-start.1 = (bf16[32,24,128]{2,1,0:T(8,128)(2,1)S(1)}, bf16[32,24,128]{2,1,0:T(8,128)(2,1)S(1)}, u32[]{:S(2)}, u32[]{:S(2)}) collective-permute-start(bf16[32,24,128]{2,1,0:T(8,128)(2,1)S(1)} %slice_bitcast_fusion.4.q0), channel_id=1, source_target_pairs={{256,0},{384,128},{257,1},{385,129},{258,2},{386,130},{259,3},{387... | collective-permute-start | bytes 589832 | tf_op jit(solution)/shard_map/ppermute | solution.py:238
  67.2 5.6 %collective-permute-start.2 = (bf16[32,24,128]{2,1,0:T(8,128)(2,1)S(1)}, bf16[32,24,128]{2,1,0:T(8,128)(2,1)S(1)}, u32[]{:S(2)}, u32[]{:S(2)}) collective-permute-start(bf16[32,24,128]{2,1,0:T(8,128)(2,1)S(1)} %slice_bitcast_fusion.4.q0), channel_id=1, source_target_pairs={{384,0},{385,1},{386,2},{387,3},{388,4},{389,5},{390,6},{391,7},{3... | collective-permute-start | bytes 589832 | tf_op jit(solution)/shard_map/ppermute | solution.py:238
  68.6 0.8 copy-start.6
  68.6 0.7 copy-start.7
  87.9 11.6 %collective-permute-start.6 = (bf16[144,768]{1,0:T(8,128)(2,1)S(1)}, bf16[144,768]{1,0:T(8,128)(2,1)S(1)}, u32[]{:S(2)}, u32[]{:S(2)}) collective-permute-start(bf16[144,768]{1,0:T(8,128)(2,1)S(1)} %get-tuple-element.4), channel_id=1, source_target_pairs={{0,128},{128,256},{256,384},{1,129},{129,257},{257,385},{2,130},{1... | collective-permute-start | bytes 663560 | tf_op jit(solution)/shard_map/ppermute | solution.py:245
  89.2 15.8 %collective-permute-start.7 = (bf16[144,768]{1,0:T(8,128)(2,1)S(1)}, bf16[144,768]{1,0:T(8,128)(2,1)S(1)}, u32[]{:S(2)}, u32[]{:S(2)}) collective-permute-start(bf16[144,768]{1,0:T(8,128)(2,1)S(1)} %get-tuple-element.3), channel_id=1, source_target_pairs={{0,256},{128,384},{1,257},{129,385},{2,258},{130,386},{3,259},{131... | collective-permute-start | bytes 663560 | tf_op jit(solution)/shard_map/ppermute | solution.py:245
  90.5 19.1 %collective-permute-start.8 = (bf16[144,768]{1,0:T(8,128)(2,1)S(1)}, bf16[144,768]{1,0:T(8,128)(2,1)S(1)}, u32[]{:S(2)}, u32[]{:S(2)}) collective-permute-start(bf16[144,768]{1,0:T(8,128)(2,1)S(1)} %get-tuple-element.2), channel_id=1, source_target_pairs={{0,384},{1,385},{2,386},{3,387},{4,388},{5,389},{6,390},{7,391},{8... | collective-permute-start | bytes 663560 | tf_op jit(solution)/shard_map/ppermute | solution.py:245
  109.7 25.6 %copy-start.4 = (bf16[1,24,4096]{2,1,0:T(8,128)(2,1)S(1)}, bf16[1,24,4096]{2,1,0:T(8,128)(2,1)}, u32[]{:S(2)}) copy-start(bf16[1,24,4096]{2,1,0:T(8,128)(2,1)} %latent_ref.1) | copy-start | bytes 589828
  110.7 24.7 %copy-start = (f32[16,4096]{1,0:T(8,128)S(1)}, f32[16,4096]{1,0:T(8,128)}, u32[]{:S(2)}) copy-start(f32[16,4096]{1,0:T(8,128)} %gate_ref.1) | copy-start | bytes 786436
  110.7 24.7 %all-to-all-start.1 = ((bf16[32,24,128]{2,1,0:T(8,128)(2,1)}), bf16[32,24,128]{2,1,0:T(8,128)(2,1)S(1)}, u32[]{:S(2)}, u32[]{:S(2)}) async-start(bf16[32,24,128]{2,1,0:T(8,128)(2,1)} %shard_map.106), calls=%async_computation.1 | async-start | bytes 393216 | tf_op jit(solution)/shard_map/all_to_all | solution.py:249
  118.9 43.2 %copy-start.5 = (bf16[24,4096]{1,0:T(8,128)(2,1)S(1)}, bf16[24,4096]{1,0:T(8,128)(2,1)}, u32[]{:S(2)}) copy-start(bf16[24,4096]{1,0:T(8,128)(2,1)} %param.13) | copy-start | bytes 589828
  136.2 25.9 %collective-permute-start.9 = (bf16[1,24,4096]{2,1,0:T(8,128)(2,1)}, bf16[1,24,4096]{2,1,0:T(8,128)(2,1)S(1)}, u32[]{:S(2)}, u32[]{:S(2)}) collective-permute-start(bf16[1,24,4096]{2,1,0:T(8,128)(2,1)} %shard_map.107), channel_id=1, source_target_pairs={{0,32},{32,64},{64,96},{96,128},{128,160},{160,192},{192,224},{224... | collective-permute-start | bytes 589832 | tf_op jit(solution)/shard_map/ppermute | solution.py:251

commit v2 on v1

v2 whole, which is shorter than its diff:
```python
import math

import jax
import jax.numpy as jnp
from jax import lax
from jax.experimental import pallas as pl
from jax.experimental.pallas import tpu as pltpu
from jax.sharding import Mesh
from jax.sharding import PartitionSpec as P

HD = 128
HEADS = 32
ROWS = 24
QUARTER = 192
BLOCK = 768
STAT = 16
SCALE = math.log2(math.e) / math.sqrt(HD)
LOW = -1e30
f32 = jnp.float32
bf16 = jnp.bfloat16

VM = pl.BlockSpec(memory_space=pltpu.VMEM)
SM = pl.BlockSpec(memory_space=pltpu.SMEM)
PARAMS = pltpu.CompilerParams(vmem_limit_bytes=48 * 2**20)
HEAD_AXES = ("zh", "zl", "c")


def pack_kernel(level_ref, q_hbm, k_hbm, v_hbm, latent_hbm, o_ref, latent_ref, buf, sems):
    sources = (q_hbm, k_hbm, v_hbm, latent_hbm)
    copies = [pltpu.make_async_copy(ref, buf.at[i], sems.at[i]) for i, ref in enumerate(sources)]
    for copy in copies:
        copy.start()
    latent_ref[0, :, HEADS * HD :] = jnp.full((ROWS, HD), level_ref[0], jnp.int32).astype(
        f32
    ).astype(bf16)
    for i in range(3):
        copies[i].wait()
        for h in range(HEADS):
            o_ref[h, i] = buf[i, 0, :, h * HD : (h + 1) * HD]
    copies[3].wait()
    latent_ref[0, :, : HEADS * HD] = buf[3, 0]


def pack(level, queries, keys, values, latent):
    hbm = pl.BlockSpec(memory_space=pltpu.HBM)
    return pl.pallas_call(
        pack_kernel,
        out_shape=[
            jax.ShapeDtypeStruct((HEADS, 3, ROWS, HD), bf16),
            jax.ShapeDtypeStruct((1, ROWS, HEADS * HD + HD), bf16),
        ],
        in_specs=[SM] + [hbm] * 4,
        out_specs=[VM] * 2,
        scratch_shapes=[
            pltpu.VMEM((4, 1, ROWS, HEADS * HD), bf16),
            pltpu.SemaphoreType.DMA((4,)),
        ],
        compiler_params=PARAMS,
    )(level, queries, keys, values, latent)


def token_of(shape, dim):
    i = lax.broadcasted_iota(jnp.int32, shape, dim)
    one, nil = jnp.int32(1), jnp.int32(0)
    part = sum(jnp.where(i >= e * QUARTER, one, nil) for e in (1, 2, 3))
    inner = i - part * QUARTER
    run = sum(jnp.where(inner >= e * 48, one, nil) for e in (1, 2, 3))
    return inner + run * (QUARTER - 48) + part * 48


def attend_kernel(
    count_ref, flag_ref, place_ref, kv_ref, q_ref, o0, o1, o2, o3,
    q_sc, k_sc, v_sc, m_sc, acc_sc, s0, s1, p0, p1, a0, a1, units,
):
    def build(e, n):
        slot, t = e // 4, e % 4
        active = flag_ref[slot * 4, t]
        for g in range(1, 4):
            active = active | flag_ref[slot * 4 + g, t]

        @pl.when(active == 1)
        def _():
            units[0, n] = slot
            units[1, n] = t

        return n + active

    for i in range(2):
        units[0, i] = 4
        units[1, i] = 0
    n = lax.fori_loop(0, 16, build, jnp.int32(2))
    for i in range(4):
        units[0, n + i] = 4
        units[1, n + i] = 0

    for slot in range(4):
        q_sc[slot] = q_ref[jnp.minimum(place_ref[0] + slot, 3)].reshape(BLOCK, HD)

    token = token_of((BLOCK, HD), 0)
    token_row = token_of((STAT, BLOCK), 1)
    for t in range(4):
        k = jnp.concatenate([kv_ref[y, t, :, 0].reshape(QUARTER, HD) for y in range(4)])
        v = jnp.concatenate([kv_ref[y, t, :, 1].reshape(QUARTER, HD) for y in range(4)])
        valid = token < count_ref[t]
        k_sc[t] = jnp.where(valid, k, jnp.broadcast_to(k[0:1], k.shape))
        v_sc[t, :HD] = jnp.where(valid, v, jnp.zeros_like(v)).T
        v_sc[t, HD:] = jnp.where(token_row < count_ref[t], 1.0, 0.0).astype(bf16)

    m_sc[...] = jnp.full(m_sc.shape, LOW, f32)
    acc_sc[...] = jnp.zeros(acc_sc.shape, f32)
    lane = lax.broadcasted_iota(jnp.int32, (8, BLOCK), 1)

    def score(i, s):
        slot = jnp.minimum(units[0, i], 3)
        s[...] = lax.dot_general(
            k_sc[units[1, i]], q_sc[slot], (((1,), (1,)), ((), ())), preferred_element_type=f32
        )

    def weigh(i, s, p, a):
        slot, t = units[0, i], units[1, i]
        first = jnp.minimum(slot, 3) * 4
        flag = jnp.full((8, BLOCK), flag_ref[first, t], jnp.int32)
        for g in range(1, 4):
            flag = jnp.where(lane >= g * QUARTER, flag_ref[first + g, t], flag)
        on = flag == 1
        old = m_sc[slot]
        top = jnp.max(s[...], axis=0, keepdims=True) * SCALE
        new = jnp.where(on, jnp.maximum(old, top), old)
        m_sc[slot] = new
        a[...] = jnp.exp2(old - new)
        p[...] = jnp.exp2(s[...] * SCALE - jnp.where(on, new, -LOW)[:1]).astype(bf16)

    def gather(i, p, a):
        slot = units[0, i]
        part = jnp.dot(v_sc[units[1, i]], p[...], preferred_element_type=f32)
        acc_sc[slot] = acc_sc[slot] * a[:1] + part

    def step(h, carry):
        i = 2 + 2 * h
        gather(i - 2, p0, a0)
        weigh(i - 1, s1, p1, a1)
        score(i, s0)
        gather(i - 1, p1, a1)
        weigh(i, s0, p0, a0)
        score(i + 1, s1)
        return carry

    lax.fori_loop(0, (n + 1) // 2, step, 0)

    outs = (o0, o1, o2, o3)
    for slot in range(4):
        total = acc_sc[slot, HD : HD + 1]
        some = total > 0.0
        safe = jnp.where(some, total, 1.0)
        head = (acc_sc[slot, :HD] * (1.0 / safe)).astype(bf16)
        level = jnp.where(some, m_sc[slot, :1] + jnp.log2(safe), LOW)
        hi = level.astype(bf16)
        mid = (level - hi.astype(f32)).astype(bf16)
        lo = (level - hi.astype(f32) - mid.astype(f32)).astype(bf16)
        stat = jnp.concatenate([hi, mid, lo, jnp.zeros((STAT - 3, BLOCK), bf16)], axis=0)
        outs[slot][:HD, :BLOCK] = head
        outs[slot][HD:, :BLOCK] = stat
        if slot < 3:
            outs[slot + 1][:HD, BLOCK:] = head[:, BLOCK - QUARTER :]
            outs[slot + 1][HD:, BLOCK:] = stat[:, BLOCK - QUARTER :]


def attend(counts, flags, place, q, kv):
    vmem = pltpu.VMEM
    return pl.pallas_call(
        attend_kernel,
        out_shape=[
            jax.ShapeDtypeStruct((HD + STAT, BLOCK + (QUARTER if slot else 0)), bf16)
            for slot in range(4)
        ],
        in_specs=[SM] * 3 + [VM] * 2,
        out_specs=[VM] * 4,
        scratch_shapes=[
            vmem((4, BLOCK, HD), bf16),
            vmem((4, BLOCK, HD), bf16),
            vmem((4, HD + STAT, BLOCK), bf16),
            vmem((5, 8, BLOCK), f32),
            vmem((5, HD + STAT, BLOCK), f32),
            vmem((BLOCK, BLOCK), f32),
            vmem((BLOCK, BLOCK), f32),
            vmem((BLOCK, BLOCK), bf16),
            vmem((BLOCK, BLOCK), bf16),
            vmem((8, BLOCK), f32),
            vmem((8, BLOCK), f32),
            pltpu.SMEM((2, 24), jnp.int32),
        ],
        compiler_params=PARAMS,
        cost_estimate=pl.CostEstimate(
            flops=64 * BLOCK * BLOCK * HD, bytes_accessed=8 << 20, transcendentals=16 * BLOCK * BLOCK
        ),
    )(counts, flags, place, kv, q)


def blend(stats, heads):
    levels = [stat[0:1] + stat[1:2] + stat[2:3] for stat in stats]
    top = levels[0]
    for level in levels[1:]:
        top = jnp.maximum(top, level)
    shares = [jnp.exp2(level - top) for level in levels]
    whole = sum(shares[1:], shares[0])
    total = sum(head.astype(f32) * (share / whole) for head, share in zip(heads, shares))
    return total.T.astype(bf16)


def merge_kernel(x_ref, r0, r1, r2, r3, o_ref):
    stats, heads = [r0[HD:].astype(f32)], [r0[:HD]]
    for k, ref in ((1, r1), (2, r2), (3, r3)):
        stat = ref[HD:].astype(f32)
        row = lax.broadcasted_iota(jnp.int32, stat.shape, 0)
        stats.append(jnp.where(x_ref[0] >= k, stat, jnp.where(row == 0, LOW, 0.0)))
        heads.append(ref[:HD])
    own = blend([stat[:, :BLOCK] for stat in stats], [head[:, :BLOCK] for head in heads])
    tail = blend([stat[:, BLOCK:] for stat in stats[1:]], [head[:, BLOCK:] for head in heads[1:]])
    own = own.reshape(HEADS, ROWS, HD)
    o_ref[:, 0] = own
    o_ref[:8, 1] = tail.reshape(8, ROWS, HD)
    o_ref[8:, 1] = own[: HEADS - 8]


def merge(x, parts):
    return pl.pallas_call(
        merge_kernel,
        out_shape=jax.ShapeDtypeStruct((HEADS, 2, ROWS, HD), bf16),
        in_specs=[SM] + [VM] * 4,
        out_specs=VM,
        compiler_params=PARAMS,
    )(x, *parts)


def finish_kernel(
    level_ref, first_ref, r_ref, latent_ref, latent_before_ref, entering_ref, gate_ref,
    updated_ref, advanced_ref,
):
    def update(which, level, residual):
        squares = jnp.zeros((ROWS, HD), f32)
        for h in range(HEADS):
            wide = r_ref[h, which].astype(f32)
            squares = squares + wide * wide
        mean = jnp.sum(squares, axis=-1, keepdims=True) * (1.0 / (HEADS * HD))
        factor = 1.0 / jnp.sqrt(mean + 1e-06)
        index = lax.broadcasted_iota(jnp.int32, (gate_ref.shape[0], HD), 0)
        mine = index.astype(f32) == level
        for h in range(HEADS):
            span = slice(h * HD, (h + 1) * HD)
            gate = jnp.sum(jnp.where(mine, gate_ref[:, span], 0.0), axis=0, keepdims=True)
            wide = r_ref[h, which].astype(f32)
            yield span, residual[0, :, span].astype(f32) + gate * (wide * factor)

    for span, value in update(0, level_ref[0].astype(f32), latent_ref):
        updated_ref[0, :, span] = value.astype(bf16)
    first = first_ref[0] == 1
    before = latent_before_ref[0, :1, HEADS * HD :].astype(f32)
    for span, value in update(1, before, latent_before_ref):
        advanced_ref[0, :, span] = jnp.where(first, entering_ref[:, span], value.astype(bf16))


def finish(level, first, returned, latent, latent_before, entering, gate_table):
    return pl.pallas_call(
        finish_kernel,
        out_shape=[jax.ShapeDtypeStruct(latent.shape, bf16)] * 2,
        in_specs=[SM] * 2 + [VM] * 5,
        out_specs=[VM] * 2,
        compiler_params=PARAMS,
    )(level, first, returned, latent, latent_before, entering, gate_table)


def local(
    queries, keys, values, latent, entering, noise_level, token_counts, block_mask, gate_table
):
    x = lax.axis_index("x")
    packed, latent_level = pack(noise_level, queries, keys, values, latent)
    packed = lax.all_to_all(packed, HEAD_AXES, split_axis=0, concat_axis=0, tiled=True)
    packed, latent_level = lax.optimization_barrier((packed, latent_level))
    kv = packed[:, 1:3].reshape(4, 8, 2, ROWS, HD)
    kv, packed = lax.optimization_barrier((kv, packed))
    q = lax.all_gather(packed[:, 0], "x", axis=0, tiled=False)
    kv = jnp.broadcast_to(kv[None], (4, *kv.shape))
    kv = lax.all_to_all(kv, "y", split_axis=0, concat_axis=0, tiled=True)
    onward = [(s, s + 1) for s in range(15)]
    latent_before = lax.ppermute(latent_level, ("x", "zh"), onward)
    padded = jnp.concatenate([block_mask, jnp.zeros_like(block_mask)], axis=0)
    flags = lax.dynamic_slice(padded, (4 * x, 4 * x), (16, 4))
    counts = lax.dynamic_slice(token_counts, (4 * x,), (4,))
    parts = attend(counts, flags, x.reshape(1), q, kv)
    parts, latent_before = lax.optimization_barrier((parts, latent_before))
    received = [parts[0]] + [
        lax.ppermute(parts[k], "x", [(source, source + k) for source in range(4 - k)])
        for k in (1, 2, 3)
    ]
    attended = merge(x.reshape(1), received)
    returned = lax.all_to_all(attended, HEAD_AXES, split_axis=0, concat_axis=0, tiled=True)
    first = ((x == 0) & (lax.axis_index("zh") == 0)).astype(jnp.int32).reshape(1)
    return tuple(
        finish(
            noise_level, first, returned, latent, latent_before, entering, gate_table
        )
    )


def solution(mesh):
    fine = Mesh(mesh.devices.reshape(4, 4, 4, 4, 2), ("x", "zh", "zl", "y", "c"))
    section, seq = ("x", "zh"), ("zl", "y", "c")
    placed = (
        P(section, seq, None),
        P(section, seq, None),
        P(section, seq, None),
        P(section, seq, None),
        P(seq, None),
        P(section),
        P(),
        P(),
        P(),
    )
    return jax.shard_map(
        local,
        mesh=fine,
        in_specs=placed,
        out_specs=(P(section, seq, None), P(section, seq, None)),
        check_vma=False,
    )
```

time: 163 us -> 152 us (0.933)
  the two profiles are of different devices: /device:TPU:102 before, /device:TPU:5 now
where the time goes in v2:
time: 152 us; the launch traced here: 151 us
  blocking collectives  63.4 us (42%)
  waiting for transfers between devices  51.1 us (34%)
  starting transfers between devices  16.1 us (11%)
  Pallas kernels  13.7 us (9%)
  local copies, waits for them, and re-layouts  5.41 us (4%)
    all_to_all x1, blocking collectives, local(): lax.all_to_all(packed, HEAD_AXES, split_axis=0, concat_axis=0, tiled=True)  52 us
    all_to_all x1, waiting for transfers between devices, local(): lax.all_to_all(attended, HEAD_AXES, split_axis=0, concat_axis=0, tiled=True)  28 us
    ppermute x3, waiting for transfers between devices, local(): lax.ppermute(parts[k], 'x', [(source, source + k) for source in range(4 -...  16.5 us
    all_gather x1, blocking collectives, local(): q = lax.all_gather(packed[:, 0], 'x', axis=0, tiled=False)  11.4 us
    pallas_call x1, Pallas kernels, attend(): pl.pallas_call(attend_kernel, out_shape=[jax.ShapeDtypeStruct((HD + STAT,...  10.4 us
    all_to_all x1, waiting for transfers between devices, local(): kv = lax.all_to_all(kv, 'y', split_axis=0, concat_axis=0, tiled=True)  6.52 us
    all_to_all x1, starting transfers between devices, local(): lax.all_to_all(attended, HEAD_AXES, split_axis=0, concat_axis=0, tiled=True)  5.82 us
    all_to_all x1, starting transfers between devices, local(): kv = lax.all_to_all(kv, 'y', split_axis=0, concat_axis=0, tiled=True)  4.31 us
  transfers between devices with their start and end apart: 6, of which 4 were waited for; matrix products, arithmetic and copies ran while one was open for 0% of the time, Pallas kernels for 7%

profile of v2, /device:TPU:5, one launch (start us, length us, event | category | flops | bytes accessed | tf_op | source)
XLA Modules:
  0.0 151.0 jit_solution(938299156492340498)
XLA Ops:
  1.3 0.0 copy-start
  1.3 0.9 copy-done
  2.2 0.9 copy-done.3
  3.1 0.9 copy-done.4
  4.1 0.9 copy-done.5
  5.0 1.1 shard_map.104
  6.1 52.0 %all_to_all.15 = bf16[32,3,24,128]{3,2,1,0:T(8,128)(2,1)S(1)} all-to-all(bf16[32,3,24,128]{3,2,1,0:T(8,128)(2,1)S(1)} %get-tuple-element.17), channel_id=1, replica_groups=mesh['x'=4,'zh'=4,'zl'=4,'y'=4,'c'=2] {'zh','zl','c'}, dimensions={0} | all-to-all | bytes 1179648 | tf_op jit(solution)/shard_map/all_to_all | solution.py:277
  58.2 1.5 broadcast_in_dim.2
  59.7 4.3 %all-to-all-start.1 = ((bf16[4,4,8,2,24,128]{5,4,3,2,1,0:T(8,128)(2,1)}), bf16[4,4,8,2,24,128]{5,4,3,2,1,0:T(8,128)(2,1)S(1)}, u32[]{:S(2)}, u32[]{:S(2)}) async-start(bf16[4,4,8,2,24,128]{5,4,3,2,1,0:T(8,128)(2,1)} %broadcast_in_dim.2), calls=%async_computation.1 | async-start | bytes 3145728 | tf_op jit(solution)/shard_map/all_to_all | solution.py:283
  64.0 0.0 copy-done.8
  64.0 0.1 dynamic_slice.6.count_ref
  64.0 0.0 copy-done.7
  64.0 0.1 pad_dynamic-slice_fusion.flag_ref
  64.2 1.9 %collective-permute-start = (bf16[1,24,4224]{2,1,0:T(8,128)(2,1)S(1)}, bf16[1,24,4224]{2,1,0:T(8,128)(2,1)S(1)}, u32[]{:S(2)}, u32[]{:S(2)}) collective-permute-start(bf16[1,24,4224]{2,1,0:T(8,128)(2,1)S(1)} %get-tuple-element.26), channel_id=1, source_target_pairs={{0,32},{32,64},{64,96},{96,128},{128,160},{160,192},{192,224},{224... | collective-permute-start | bytes 608264 | tf_op jit(solution)/shard_map/ppermute | solution.py:285
  66.1 11.4 %all-gather = bf16[128,1,24,128]{3,2,1,0:T(8,128)(2,1)S(1)} all-gather(bf16[32,1,24,128]{3,2,1,0:T(8,128)(2,1)S(1)} %slice.7), channel_id=2, replica_groups=mesh['x'=4,'zh'=4,'zl'=4,'y'=4,'c'=2] {'x'}, dimensions={0}, use_global_device_ids=true | all-gather | bytes 983040 | tf_op jit(solution)/shard_map/all_gather | solution.py:281
  77.5 6.5 %all-to-all-done.1.kv_ref = bf16[4,4,8,2,24,128]{5,4,3,2,1,0:T(8,128)(2,1)S(1)} async-done(((bf16[4,4,8,2,24,128]{5,4,3,2,1,0:T(8,128)(2,1)}), bf16[4,4,8,2,24,128]{5,4,3,2,1,0:T(8,128)(2,1)S(1)}, u32[]{:S(2)}, u32[]{:S(2)}) %all-to-all-start.1) | async-done | bytes 1572896 | tf_op jit(solution)/shard_map/all_to_all | solution.py:283
  84.0 10.4 %shard_map.105 = (bf16[144,768]{1,0:T(8,128)(2,1)S(1)}, bf16[144,960]{1,0:T(8,128)(2,1)S(1)}, bf16[144,960]{1,0:T(8,128)(2,1)S(1)}, bf16[144,960]{1,0:T(8,128)(2,1)S(1)}) custom-call(s32[4]{0:T(128)S(1)} %dynamic_slice.6.count_ref, s32[16,4]{1,0:T(8,128)S(1)} %pad_dynamic-slice_fusion.flag_ref, s32[1]{0:T(128)} %bitcast.1.place_ref.x_ref, ...), custom_call_target="tpu_custom_call" | custom-call | flops 4831838208 | bytes 8388608 | tf_op jit(solution)/shard_map/pallas_call | solution.py:170
  94.4 0.0 copy-start.2
  94.4 0.0 copy-start.6
  94.4 0.0 collective-permute-done.latent_before_ref
  94.5 2.1 %collective-permute-start.1 = (bf16[144,960]{1,0:T(8,128)(2,1)S(1)}, bf16[144,960]{1,0:T(8,128)(2,1)S(1)}, u32[]{:S(2)}, u32[]{:S(2)}) collective-permute-start(bf16[144,960]{1,0:T(8,128)(2,1)S(1)} %get-tuple-element.28), channel_id=1, source_target_pairs={{0,128},{128,256},{256,384},{1,129},{129,257},{257,385},{2,130},{1... | collective-permute-start | bytes 829448 | tf_op jit(solution)/shard_map/ppermute | solution.py:292
  96.5 1.3 collective-permute-start.2
  97.8 0.7 collective-permute-start.3
  98.5 7.4 %collective-permute-done.1.r1 = bf16[144,960]{1,0:T(8,128)(2,1)S(1)} collective-permute-done((bf16[144,960]{1,0:T(8,128)(2,1)S(1)}, bf16[144,960]{1,0:T(8,128)(2,1)S(1)}, u32[]{:S(2)}, u32[]{:S(2)}) %collective-permute-start.1) | collective-permute-done | bytes 276512 | tf_op jit(solution)/shard_map/ppermute | solution.py:292
  105.9 9.1 %collective-permute-done.2.r2 = bf16[144,960]{1,0:T(8,128)(2,1)S(1)} collective-permute-done((bf16[144,960]{1,0:T(8,128)(2,1)S(1)}, bf16[144,960]{1,0:T(8,128)(2,1)S(1)}, u32[]{:S(2)}, u32[]{:S(2)}) %collective-permute-start.2) | collective-permute-done | bytes 276512 | tf_op jit(solution)/shard_map/ppermute | solution.py:292
  115.0 0.0 collective-permute-done.3.r3
  115.0 1.1 shard_map.106
  116.1 5.8 %all-to-all-start.2 = ((bf16[32,2,24,128]{3,2,1,0:T(8,128)(2,1)}), bf16[32,2,24,128]{3,2,1,0:T(8,128)(2,1)S(1)}, u32[]{:S(2)}, u32[]{:S(2)}) async-start(bf16[32,2,24,128]{3,2,1,0:T(8,128)(2,1)} %shard_map.106), calls=%async_computation.2 | async-start | bytes 786432 | tf_op jit(solution)/shard_map/all_to_all | solution.py:296
  122.0 28.0 %all-to-all-done.2.r_ref = bf16[32,2,24,128]{3,2,1,0:T(8,128)(2,1)S(1)} async-done(((bf16[32,2,24,128]{3,2,1,0:T(8,128)(2,1)}), bf16[32,2,24,128]{3,2,1,0:T(8,128)(2,1)S(1)}, u32[]{:S(2)}, u32[]{:S(2)}) %all-to-all-start.2) | async-done | bytes 393248 | tf_op jit(solution)/shard_map/all_to_all | solution.py:296
  150.0 0.0 copy-done.1
  150.0 0.0 copy-done.2
  150.0 1.0 shard_map.107
  (9 shorter events, 0.1 us)
Async XLA Ops:
  1.3 0.9 copy-start
  2.2 0.9 copy-start.3
  3.1 0.9 copy-start.4
  4.1 0.9 copy-start.5
  59.6 4.3 %copy-start.8 = (s32[16]{0:T(128)S(1)}, s32[16]{0:T(128)}, u32[]{:S(2)}) copy-start(s32[16]{0:T(128)} %param.15) | copy-start | bytes 196
  59.7 4.4 %copy-start.7 = (s32[16,16]{1,0:T(8,128)S(1)}, s32[16,16]{1,0:T(8,128)}, u32[]{:S(2)}) copy-start(s32[16,16]{1,0:T(8,128)} %param.16) | copy-start | bytes 3076
  59.7 24.3 %all-to-all-start.1 = ((bf16[4,4,8,2,24,128]{5,4,3,2,1,0:T(8,128)(2,1)}), bf16[4,4,8,2,24,128]{5,4,3,2,1,0:T(8,128)(2,1)S(1)}, u32[]{:S(2)}, u32[]{:S(2)}) async-start(bf16[4,4,8,2,24,128]{5,4,3,2,1,0:T(8,128)(2,1)} %broadcast_in_dim.2), calls=%async_computation.1 | async-start | bytes 3145728 | tf_op jit(solution)/shard_map/all_to_all | solution.py:283
  64.2 30.3 %collective-permute-start = (bf16[1,24,4224]{2,1,0:T(8,128)(2,1)S(1)}, bf16[1,24,4224]{2,1,0:T(8,128)(2,1)S(1)}, u32[]{:S(2)}, u32[]{:S(2)}) collective-permute-start(bf16[1,24,4224]{2,1,0:T(8,128)(2,1)S(1)} %get-tuple-element.26), channel_id=1, source_target_pairs={{0,32},{32,64},{64,96},{96,128},{128,160},{160,192},{192,224},{224... | collective-permute-start | bytes 608264 | tf_op jit(solution)/shard_map/ppermute | solution.py:285
  94.4 55.6 %copy-start.1 = (bf16[1,24,4096]{2,1,0:T(8,128)(2,1)S(1)}, bf16[1,24,4096]{2,1,0:T(8,128)(2,1)}, u32[]{:S(2)}) copy-start(bf16[1,24,4096]{2,1,0:T(8,128)(2,1)} %latent_ref.1) | copy-start | bytes 589828
  94.4 55.6 %copy-start.2 = (f32[16,4096]{1,0:T(8,128)S(1)}, f32[16,4096]{1,0:T(8,128)}, u32[]{:S(2)}) copy-start(f32[16,4096]{1,0:T(8,128)} %gate_ref.1) | copy-start | bytes 786436
  94.4 55.6 %copy-start.6 = (bf16[24,4096]{1,0:T(8,128)(2,1)S(1)}, bf16[24,4096]{1,0:T(8,128)(2,1)}, u32[]{:S(2)}) copy-start(bf16[24,4096]{1,0:T(8,128)(2,1)} %entering_ref.1) | copy-start | bytes 589828
  94.5 11.4 %collective-permute-start.1 = (bf16[144,960]{1,0:T(8,128)(2,1)S(1)}, bf16[144,960]{1,0:T(8,128)(2,1)S(1)}, u32[]{:S(2)}, u32[]{:S(2)}) collective-permute-start(bf16[144,960]{1,0:T(8,128)(2,1)S(1)} %get-tuple-element.28), channel_id=1, source_target_pairs={{0,128},{128,256},{256,384},{1,129},{129,257},{257,385},{2,130},{1... | collective-permute-start | bytes 829448 | tf_op jit(solution)/shard_map/ppermute | solution.py:292
  96.5 18.5 %collective-permute-start.2 = (bf16[144,960]{1,0:T(8,128)(2,1)S(1)}, bf16[144,960]{1,0:T(8,128)(2,1)S(1)}, u32[]{:S(2)}, u32[]{:S(2)}) collective-permute-start(bf16[144,960]{1,0:T(8,128)(2,1)S(1)} %get-tuple-element.29), channel_id=1, source_target_pairs={{0,256},{128,384},{1,257},{129,385},{2,258},{130,386},{3,259},{131... | collective-permute-start | bytes 829448 | tf_op jit(solution)/shard_map/ppermute | solution.py:292
  97.8 17.2 %collective-permute-start.3 = (bf16[144,960]{1,0:T(8,128)(2,1)S(1)}, bf16[144,960]{1,0:T(8,128)(2,1)S(1)}, u32[]{:S(2)}, u32[]{:S(2)}) collective-permute-start(bf16[144,960]{1,0:T(8,128)(2,1)S(1)} %get-tuple-element.30), channel_id=1, source_target_pairs={{0,384},{1,385},{2,386},{3,387},{4,388},{5,389},{6,390},{7,391},{8... | collective-permute-start | bytes 829448 | tf_op jit(solution)/shard_map/ppermute | solution.py:292
  116.1 33.9 %all-to-all-start.2 = ((bf16[32,2,24,128]{3,2,1,0:T(8,128)(2,1)}), bf16[32,2,24,128]{3,2,1,0:T(8,128)(2,1)S(1)}, u32[]{:S(2)}, u32[]{:S(2)}) async-start(bf16[32,2,24,128]{3,2,1,0:T(8,128)(2,1)} %shard_map.106), calls=%async_computation.2 | async-start | bytes 786432 | tf_op jit(solution)/shard_map/all_to_all | solution.py:296

commit v3 on v2

--- a/solution.py
+++ b/solution.py
@@ -14,6 +14,7 @@
 QUARTER = 192
 BLOCK = 768
 STAT = 16
+LANES = 256
 SCALE = math.log2(math.e) / math.sqrt(HD)
 LOW = -1e30
 f32 = jnp.float32
@@ -70,7 +71,7 @@
 
 def attend_kernel(
     count_ref, flag_ref, place_ref, kv_ref, q_ref, o0, o1, o2, o3,
-    q_sc, k_sc, v_sc, m_sc, acc_sc, s0, s1, p0, p1, a0, a1, units,
+    q_sc, k_sc, v_sc, m_sc, acc_sc, s0, s1, units,
 ):
     def build(e, n):
         slot, t = e // 4, e % 4
@@ -108,44 +109,44 @@
 
     m_sc[...] = jnp.full(m_sc.shape, LOW, f32)
     acc_sc[...] = jnp.zeros(acc_sc.shape, f32)
-    lane = lax.broadcasted_iota(jnp.int32, (8, BLOCK), 1)
-
-    def score(i, s):
-        slot = jnp.minimum(units[0, i], 3)
-        s[...] = lax.dot_general(
-            k_sc[units[1, i]], q_sc[slot], (((1,), (1,)), ((), ())), preferred_element_type=f32
-        )
-
-    def weigh(i, s, p, a):
+    lane = lax.broadcasted_iota(jnp.int32, (8, LANES), 1)
+
+    def unit(i, j, s_read, s_write):
+        span = slice(j * LANES, (j + 1) * LANES)
         slot, t = units[0, i], units[1, i]
         first = jnp.minimum(slot, 3) * 4
-        flag = jnp.full((8, BLOCK), flag_ref[first, t], jnp.int32)
+        flag = jnp.full((8, LANES), flag_ref[first + (j * LANES) // QUARTER, t], jnp.int32)
         for g in range(1, 4):
-            flag = jnp.where(lane >= g * QUARTER, flag_ref[first + g, t], flag)
+            if j * LANES < g * QUARTER < (j + 1) * LANES:
+                flag = jnp.where(lane + j * LANES >= g * QUARTER, flag_ref[first + g, t], flag)
         on = flag == 1
-        old = m_sc[slot]
-        top = jnp.max(s[...], axis=0, keepdims=True) * SCALE
+        old = m_sc[slot, :, span]
+        top = jnp.max(s_read[:, span], axis=0, keepdims=True) * SCALE
         new = jnp.where(on, jnp.maximum(old, top), old)
-        m_sc[slot] = new
-        a[...] = jnp.exp2(old - new)
-        p[...] = jnp.exp2(s[...] * SCALE - jnp.where(on, new, -LOW)[:1]).astype(bf16)
-
-    def gather(i, p, a):
-        slot = units[0, i]
-        part = jnp.dot(v_sc[units[1, i]], p[...], preferred_element_type=f32)
-        acc_sc[slot] = acc_sc[slot] * a[:1] + part
+        m_sc[slot, :, span] = new
+        a = jnp.exp2(old - new)
+        p = jnp.exp2(s_read[:, span] * SCALE - jnp.where(on, new, -LOW)[:1]).astype(bf16)
+        score(i + 1, span, s_write)
+        part = jnp.dot(v_sc[t], p, preferred_element_type=f32)
+        acc_sc[slot, :, span] = acc_sc[slot, :, span] * a[:1] + part
+
+    def score(i, span, s):
+        slot = jnp.minimum(units[0, i], 3)
+        s[:, span] = lax.dot_general(
+            k_sc[units[1, i]], q_sc[slot, span], (((1,), (1,)), ((), ())), preferred_element_type=f32
+        )
 
     def step(h, carry):
         i = 2 + 2 * h
-        gather(i - 2, p0, a0)
-        weigh(i - 1, s1, p1, a1)
-        score(i, s0)
-        gather(i - 1, p1, a1)
-        weigh(i, s0, p0, a0)
-        score(i + 1, s1)
+        for j in range(BLOCK // LANES):
+            unit(i, j, s0, s1)
+        for j in range(BLOCK // LANES):
+            unit(i + 1, j, s1, s0)
         return carry
 
-    lax.fori_loop(0, (n + 1) // 2, step, 0)
+    for j in range(BLOCK // LANES):
+        score(2, slice(j * LANES, (j + 1) * LANES), s0)
+    lax.fori_loop(0, (n - 1) // 2, step, 0)
 
     outs = (o0, o1, o2, o3)
     for slot in range(4):
@@ -183,10 +184,6 @@
             vmem((5, HD + STAT, BLOCK), f32),
             vmem((BLOCK, BLOCK), f32),
             vmem((BLOCK, BLOCK), f32),
-            vmem((BLOCK, BLOCK), bf16),
-            vmem((BLOCK, BLOCK), bf16),
-            vmem((8, BLOCK), f32),
-            vmem((8, BLOCK), f32),
             pltpu.SMEM((2, 24), jnp.int32),
         ],
         compiler_params=PARAMS,
@@ -273,7 +270,8 @@
     queries, keys, values, latent, entering, noise_level, token_counts, block_mask, gate_table
 ):
     x = lax.axis_index("x")
-    packed, latent_level = pack(noise_level, queries, keys, values, latent)
+    queries, keys, values, latent_in = (pltpu.with_memory_space_constraint(a, pltpu.HBM) for a in (queries, keys, values, latent))
+    packed, latent_level = pack(noise_level, queries, keys, values, latent_in)
     packed = lax.all_to_all(packed, HEAD_AXES, split_axis=0, concat_axis=0, tiled=True)
     packed, latent_level = lax.optimization_barrier((packed, latent_level))
     kv = packed[:, 1:3].reshape(4, 8, 2, ROWS, HD)

time: 152 us -> 146 us (0.961)
  local copies, waits for them, and re-layouts: 5.41 us -> 1.71 us
    unnamed x18 -> x10, local copies, waits for them, and re-layouts: 3.72 us -> 0.02 us
    pallas_call x1, Pallas kernels: 10.4 us -> 8.83 us  [attend(): pl.pallas_call(attend_kernel, out_shape=[jax.ShapeDtypeStruct((HD + STAT,...]
  transfers between devices with their start and end apart: 6 -> 6, of which waited for: 4 -> 4; matrix products, arithmetic and copies ran while one was open for 0% -> 0% of each run, Pallas kernels for 7% -> 6%
where the time goes in v3:
time: 146 us; the launch traced here: 145 us
  blocking collectives  63.4 us (43%)
  waiting for transfers between devices  50.7 us (35%)
  starting transfers between devices  16.1 us (11%)
  Pallas kernels  12.2 us (8%)
  local copies, waits for them, and re-layouts  1.71 us (1%)
    all_to_all x1, blocking collectives, local(): lax.all_to_all(packed, HEAD_AXES, split_axis=0, concat_axis=0, tiled=True)  52 us
    all_to_all x1, waiting for transfers between devices, local(): lax.all_to_all(attended, HEAD_AXES, split_axis=0, concat_axis=0, tiled=True)  28 us
    ppermute x3, waiting for transfers between devices, local(): lax.ppermute(parts[k], 'x', [(source, source + k) for source in range(4 -...  16.1 us
    all_gather x1, blocking collectives, local(): q = lax.all_gather(packed[:, 0], 'x', axis=0, tiled=False)  11.4 us
    pallas_call x1, Pallas kernels, attend(): pl.pallas_call(attend_kernel, out_shape=[jax.ShapeDtypeStruct((HD + STAT,...  8.83 us
    all_to_all x1, waiting for transfers between devices, local(): kv = lax.all_to_all(kv, 'y', split_axis=0, concat_axis=0, tiled=True)  6.52 us
    all_to_all x1, starting transfers between devices, local(): lax.all_to_all(attended, HEAD_AXES, split_axis=0, concat_axis=0, tiled=True)  5.82 us
    all_to_all x1, starting transfers between devices, local(): kv = lax.all_to_all(kv, 'y', split_axis=0, concat_axis=0, tiled=True)  4.31 us
  transfers between devices with their start and end apart: 6, of which 4 were waited for; matrix products, arithmetic and copies ran while one was open for 0% of the time, Pallas kernels for 6%

profile of v3, /device:TPU:5, one launch (start us, length us, event | category | flops | bytes accessed | tf_op | source)
XLA Modules:
  0.0 145.4 jit_solution(2937479855846206188)
XLA Ops:
  1.3 1.3 shard_map.104
  2.6 52.0 %all_to_all.15 = bf16[32,3,24,128]{3,2,1,0:T(8,128)(2,1)S(1)} all-to-all(bf16[32,3,24,128]{3,2,1,0:T(8,128)(2,1)S(1)} %get-tuple-element.17), channel_id=1, replica_groups=mesh['x'=4,'zh'=4,'zl'=4,'y'=4,'c'=2] {'zh','zl','c'}, dimensions={0} | all-to-all | bytes 1179648 | tf_op jit(solution)/shard_map/all_to_all | solution.py:275
  54.6 1.5 %broadcast_in_dim.2 = bf16[4,4,8,2,24,128]{5,4,3,2,1,0:T(8,128)(2,1)} broadcast(bf16[4,8,2,24,128]{4,3,2,1,0:T(8,128)(2,1)S(1)} %bitcast.5), dimensions={1,2,3,4,5} | broadcast | bytes 1966080 | tf_op jit(solution)/shard_map/broadcast_in_dim | solution.py:280
  56.1 0.0 copy-start.4
  56.1 0.0 copy-start.3
  56.1 4.3 %all-to-all-start.1 = ((bf16[4,4,8,2,24,128]{5,4,3,2,1,0:T(8,128)(2,1)}), bf16[4,4,8,2,24,128]{5,4,3,2,1,0:T(8,128)(2,1)S(1)}, u32[]{:S(2)}, u32[]{:S(2)}) async-start(bf16[4,4,8,2,24,128]{5,4,3,2,1,0:T(8,128)(2,1)} %broadcast_in_dim.2), calls=%async_computation.1 | async-start | bytes 3145728 | tf_op jit(solution)/shard_map/all_to_all | solution.py:281
  60.4 0.0 copy-done.4
  60.4 0.1 dynamic_slice.6.count_ref
  60.5 0.0 copy-done.3
  60.5 0.1 pad_dynamic-slice_fusion.flag_ref
  60.6 1.9 %collective-permute-start = (bf16[1,24,4224]{2,1,0:T(8,128)(2,1)S(1)}, bf16[1,24,4224]{2,1,0:T(8,128)(2,1)S(1)}, u32[]{:S(2)}, u32[]{:S(2)}) collective-permute-start(bf16[1,24,4224]{2,1,0:T(8,128)(2,1)S(1)} %get-tuple-element.26), channel_id=1, source_target_pairs={{0,32},{32,64},{64,96},{96,128},{128,160},{160,192},{192,224},{224... | collective-permute-start | bytes 608264 | tf_op jit(solution)/shard_map/ppermute | solution.py:283
  62.5 11.4 %all-gather = bf16[128,1,24,128]{3,2,1,0:T(8,128)(2,1)S(1)} all-gather(bf16[32,1,24,128]{3,2,1,0:T(8,128)(2,1)S(1)} %slice.7), channel_id=2, replica_groups=mesh['x'=4,'zh'=4,'zl'=4,'y'=4,'c'=2] {'x'}, dimensions={0}, use_global_device_ids=true | all-gather | bytes 983040 | tf_op jit(solution)/shard_map/all_gather | solution.py:279
  73.9 6.5 %all-to-all-done.1.kv_ref = bf16[4,4,8,2,24,128]{5,4,3,2,1,0:T(8,128)(2,1)S(1)} async-done(((bf16[4,4,8,2,24,128]{5,4,3,2,1,0:T(8,128)(2,1)}), bf16[4,4,8,2,24,128]{5,4,3,2,1,0:T(8,128)(2,1)S(1)}, u32[]{:S(2)}, u32[]{:S(2)}) %all-to-all-start.1) | async-done | bytes 1572896 | tf_op jit(solution)/shard_map/all_to_all | solution.py:281
  80.4 8.8 %shard_map.105 = (bf16[144,768]{1,0:T(8,128)(2,1)S(1)}, bf16[144,960]{1,0:T(8,128)(2,1)S(1)}, bf16[144,960]{1,0:T(8,128)(2,1)S(1)}, bf16[144,960]{1,0:T(8,128)(2,1)S(1)}) custom-call(s32[4]{0:T(128)S(1)} %dynamic_slice.6.count_ref, s32[16,4]{1,0:T(8,128)S(1)} %pad_dynamic-slice_fusion.flag_ref, s32[1]{0:T(128)} %bitcast.1.place_ref.x_ref, ...), custom_call_target="tpu_custom_call" | custom-call | flops 4831838208 | bytes 8388608 | tf_op jit(solution)/shard_map/pallas_call | solution.py:171
  89.2 0.0 copy-start
  89.2 0.0 copy-start.1
  89.2 0.0 copy-start.2
  89.3 0.0 collective-permute-done.latent_before_ref
  89.3 2.1 %collective-permute-start.1 = (bf16[144,960]{1,0:T(8,128)(2,1)S(1)}, bf16[144,960]{1,0:T(8,128)(2,1)S(1)}, u32[]{:S(2)}, u32[]{:S(2)}) collective-permute-start(bf16[144,960]{1,0:T(8,128)(2,1)S(1)} %get-tuple-element.28), channel_id=1, source_target_pairs={{0,128},{128,256},{256,384},{1,129},{129,257},{257,385},{2,130},{1... | collective-permute-start | bytes 829448 | tf_op jit(solution)/shard_map/ppermute | solution.py:290
  91.3 1.3 collective-permute-start.2
  92.6 0.7 collective-permute-start.3
  93.3 7.2 %collective-permute-done.1.r1 = bf16[144,960]{1,0:T(8,128)(2,1)S(1)} collective-permute-done((bf16[144,960]{1,0:T(8,128)(2,1)S(1)}, bf16[144,960]{1,0:T(8,128)(2,1)S(1)}, u32[]{:S(2)}, u32[]{:S(2)}) %collective-permute-start.1) | collective-permute-done | bytes 276512 | tf_op jit(solution)/shard_map/ppermute | solution.py:290
  100.5 8.9 %collective-permute-done.2.r2 = bf16[144,960]{1,0:T(8,128)(2,1)S(1)} collective-permute-done((bf16[144,960]{1,0:T(8,128)(2,1)S(1)}, bf16[144,960]{1,0:T(8,128)(2,1)S(1)}, u32[]{:S(2)}, u32[]{:S(2)}) %collective-permute-start.2) | collective-permute-done | bytes 276512 | tf_op jit(solution)/shard_map/ppermute | solution.py:290
  109.4 0.0 collective-permute-done.3.r3
  109.4 1.1 shard_map.106
  110.5 5.8 %all-to-all-start.2 = ((bf16[32,2,24,128]{3,2,1,0:T(8,128)(2,1)}), bf16[32,2,24,128]{3,2,1,0:T(8,128)(2,1)S(1)}, u32[]{:S(2)}, u32[]{:S(2)}) async-start(bf16[32,2,24,128]{3,2,1,0:T(8,128)(2,1)} %shard_map.106), calls=%async_computation.2 | async-start | bytes 786432 | tf_op jit(solution)/shard_map/all_to_all | solution.py:294
  116.4 28.0 %all-to-all-done.2.r_ref = bf16[32,2,24,128]{3,2,1,0:T(8,128)(2,1)S(1)} async-done(((bf16[32,2,24,128]{3,2,1,0:T(8,128)(2,1)}), bf16[32,2,24,128]{3,2,1,0:T(8,128)(2,1)S(1)}, u32[]{:S(2)}, u32[]{:S(2)}) %all-to-all-start.2) | async-done | bytes 393248 | tf_op jit(solution)/shard_map/all_to_all | solution.py:294
  144.4 0.0 copy-done
  144.4 0.0 copy-done.1
  144.4 0.0 copy-done.2
  144.4 1.0 shard_map.107
  (2 shorter events, 0.1 us)
Async XLA Ops:
  56.1 4.3 %copy-start.4 = (s32[16]{0:T(128)S(1)}, s32[16]{0:T(128)}, u32[]{:S(2)}) copy-start(s32[16]{0:T(128)} %param.15) | copy-start | bytes 196
  56.1 4.4 %copy-start.3 = (s32[16,16]{1,0:T(8,128)S(1)}, s32[16,16]{1,0:T(8,128)}, u32[]{:S(2)}) copy-start(s32[16,16]{1,0:T(8,128)} %param.16) | copy-start | bytes 3076
  56.1 24.3 %all-to-all-start.1 = ((bf16[4,4,8,2,24,128]{5,4,3,2,1,0:T(8,128)(2,1)}), bf16[4,4,8,2,24,128]{5,4,3,2,1,0:T(8,128)(2,1)S(1)}, u32[]{:S(2)}, u32[]{:S(2)}) async-start(bf16[4,4,8,2,24,128]{5,4,3,2,1,0:T(8,128)(2,1)} %broadcast_in_dim.2), calls=%async_computation.1 | async-start | bytes 3145728 | tf_op jit(solution)/shard_map/all_to_all | solution.py:281
  60.6 28.7 %collective-permute-start = (bf16[1,24,4224]{2,1,0:T(8,128)(2,1)S(1)}, bf16[1,24,4224]{2,1,0:T(8,128)(2,1)S(1)}, u32[]{:S(2)}, u32[]{:S(2)}) collective-permute-start(bf16[1,24,4224]{2,1,0:T(8,128)(2,1)S(1)} %get-tuple-element.26), channel_id=1, source_target_pairs={{0,32},{32,64},{64,96},{96,128},{128,160},{160,192},{192,224},{224... | collective-permute-start | bytes 608264 | tf_op jit(solution)/shard_map/ppermute | solution.py:283
  89.2 55.2 %copy-start = (bf16[1,24,4096]{2,1,0:T(8,128)(2,1)S(1)}, bf16[1,24,4096]{2,1,0:T(8,128)(2,1)}, u32[]{:S(2)}) copy-start(bf16[1,24,4096]{2,1,0:T(8,128)(2,1)} %latent_ref.1) | copy-start | bytes 589828
  89.2 55.2 %copy-start.1 = (f32[16,4096]{1,0:T(8,128)S(1)}, f32[16,4096]{1,0:T(8,128)}, u32[]{:S(2)}) copy-start(f32[16,4096]{1,0:T(8,128)} %gate_ref.1) | copy-start | bytes 786436
  89.2 55.1 %copy-start.2 = (bf16[24,4096]{1,0:T(8,128)(2,1)S(1)}, bf16[24,4096]{1,0:T(8,128)(2,1)}, u32[]{:S(2)}) copy-start(bf16[24,4096]{1,0:T(8,128)(2,1)} %entering_ref.1) | copy-start | bytes 589828
  89.3 11.2 %collective-permute-start.1 = (bf16[144,960]{1,0:T(8,128)(2,1)S(1)}, bf16[144,960]{1,0:T(8,128)(2,1)S(1)}, u32[]{:S(2)}, u32[]{:S(2)}) collective-permute-start(bf16[144,960]{1,0:T(8,128)(2,1)S(1)} %get-tuple-element.28), channel_id=1, source_target_pairs={{0,128},{128,256},{256,384},{1,129},{129,257},{257,385},{2,130},{1... | collective-permute-start | bytes 829448 | tf_op jit(solution)/shard_map/ppermute | solution.py:290
  91.3 18.1 %collective-permute-start.2 = (bf16[144,960]{1,0:T(8,128)(2,1)S(1)}, bf16[144,960]{1,0:T(8,128)(2,1)S(1)}, u32[]{:S(2)}, u32[]{:S(2)}) collective-permute-start(bf16[144,960]{1,0:T(8,128)(2,1)S(1)} %get-tuple-element.29), channel_id=1, source_target_pairs={{0,256},{128,384},{1,257},{129,385},{2,258},{130,386},{3,259},{131... | collective-permute-start | bytes 829448 | tf_op jit(solution)/shard_map/ppermute | solution.py:290
  92.6 16.8 %collective-permute-start.3 = (bf16[144,960]{1,0:T(8,128)(2,1)S(1)}, bf16[144,960]{1,0:T(8,128)(2,1)S(1)}, u32[]{:S(2)}, u32[]{:S(2)}) collective-permute-start(bf16[144,960]{1,0:T(8,128)(2,1)S(1)} %get-tuple-element.30), channel_id=1, source_target_pairs={{0,384},{1,385},{2,386},{3,387},{4,388},{5,389},{6,390},{7,391},{8... | collective-permute-start | bytes 829448 | tf_op jit(solution)/shard_map/ppermute | solution.py:290
  110.5 33.9 %all-to-all-start.2 = ((bf16[32,2,24,128]{3,2,1,0:T(8,128)(2,1)}), bf16[32,2,24,128]{3,2,1,0:T(8,128)(2,1)S(1)}, u32[]{:S(2)}, u32[]{:S(2)}) async-start(bf16[32,2,24,128]{3,2,1,0:T(8,128)(2,1)} %shard_map.106), calls=%async_computation.2 | async-start | bytes 786432 | tf_op jit(solution)/shard_map/all_to_all | solution.py:294

commit v4 on v3

--- a/solution.py
+++ b/solution.py
@@ -14,6 +14,7 @@
 QUARTER = 192
 BLOCK = 768
 STAT = 16
+SENT = 8
 LANES = 256
 SCALE = math.log2(math.e) / math.sqrt(HD)
 LOW = -1e30
@@ -60,6 +61,25 @@
     )(level, queries, keys, values, latent)
 
 
+def unpack_kernel(packed_ref, q_ref, kv_ref):
+    q_ref[...] = packed_ref[:, 0]
+    for copy in range(4):
+        kv_ref[copy] = packed_ref[:, 1:]
+
+
+def unpack(packed):
+    return pl.pallas_call(
+        unpack_kernel,
+        out_shape=[
+            jax.ShapeDtypeStruct((HEADS, ROWS, HD), bf16),
+            jax.ShapeDtypeStruct((4, HEADS, 2, ROWS, HD), bf16),
+        ],
+        in_specs=[VM],
+        out_specs=[VM] * 2,
+        compiler_params=PARAMS,
+    )(packed)
+
+
 def token_of(shape, dim):
     i = lax.broadcasted_iota(jnp.int32, shape, dim)
     one, nil = jnp.int32(1), jnp.int32(0)
@@ -69,12 +89,9 @@
     return inner + run * (QUARTER - 48) + part * 48
 
 
-def attend_kernel(
-    count_ref, flag_ref, place_ref, kv_ref, q_ref, o0, o1, o2, o3,
-    q_sc, k_sc, v_sc, m_sc, acc_sc, s0, s1, units,
-):
+def list_units(units, flag_ref, slots, dummy):
     def build(e, n):
-        slot, t = e // 4, e % 4
+        slot, t = slots[0] + e // 4, e % 4
         active = flag_ref[slot * 4, t]
         for g in range(1, 4):
             active = active | flag_ref[slot * 4 + g, t]
@@ -86,35 +103,28 @@
 
         return n + active
 
+    n = lax.fori_loop(0, 4 * len(slots), build, jnp.int32(0))
     for i in range(2):
-        units[0, i] = 4
-        units[1, i] = 0
-    n = lax.fori_loop(0, 16, build, jnp.int32(2))
-    for i in range(4):
-        units[0, n + i] = 4
+        units[0, n + i] = dummy
         units[1, n + i] = 0
-
-    for slot in range(4):
-        q_sc[slot] = q_ref[jnp.minimum(place_ref[0] + slot, 3)].reshape(BLOCK, HD)
-
-    token = token_of((BLOCK, HD), 0)
-    token_row = token_of((STAT, BLOCK), 1)
-    for t in range(4):
-        k = jnp.concatenate([kv_ref[y, t, :, 0].reshape(QUARTER, HD) for y in range(4)])
-        v = jnp.concatenate([kv_ref[y, t, :, 1].reshape(QUARTER, HD) for y in range(4)])
-        valid = token < count_ref[t]
-        k_sc[t] = jnp.where(valid, k, jnp.broadcast_to(k[0:1], k.shape))
-        v_sc[t, :HD] = jnp.where(valid, v, jnp.zeros_like(v)).T
-        v_sc[t, HD:] = jnp.where(token_row < count_ref[t], 1.0, 0.0).astype(bf16)
-
-    m_sc[...] = jnp.full(m_sc.shape, LOW, f32)
-    acc_sc[...] = jnp.zeros(acc_sc.shape, f32)
+    return n
+
+
+def run_units(units, steps, flag_ref, q_sc, k_ref, v_ref, m_sc, acc_sc, s0, s1):
+    real = q_sc.shape[0]
     lane = lax.broadcasted_iota(jnp.int32, (8, LANES), 1)
 
-    def unit(i, j, s_read, s_write):
+    def score(i, j, s):
+        span = slice(j * LANES, (j + 1) * LANES)
+        slot = jnp.minimum(units[0, i], real - 1)
+        s[:, span] = lax.dot_general(
+            k_ref[units[1, i]], q_sc[slot, span], (((1,), (1,)), ((), ())), preferred_element_type=f32
+        )
+
+    def weigh(i, j, s_read, s_write):
         span = slice(j * LANES, (j + 1) * LANES)
         slot, t = units[0, i], units[1, i]
-        first = jnp.minimum(slot, 3) * 4
+        first = jnp.minimum(slot, real - 1) * 4
         flag = jnp.full((8, LANES), flag_ref[first + (j * LANES) // QUARTER, t], jnp.int32)
         for g in range(1, 4):
             if j * LANES < g * QUARTER < (j + 1) * LANES:
@@ -126,71 +136,138 @@
         m_sc[slot, :, span] = new
         a = jnp.exp2(old - new)
         p = jnp.exp2(s_read[:, span] * SCALE - jnp.where(on, new, -LOW)[:1]).astype(bf16)
-        score(i + 1, span, s_write)
-        part = jnp.dot(v_sc[t], p, preferred_element_type=f32)
+        score(i + 1, j, s_write)
+        part = jnp.dot(v_ref[t], p, preferred_element_type=f32)
         acc_sc[slot, :, span] = acc_sc[slot, :, span] * a[:1] + part
 
-    def score(i, span, s):
-        slot = jnp.minimum(units[0, i], 3)
-        s[:, span] = lax.dot_general(
-            k_sc[units[1, i]], q_sc[slot, span], (((1,), (1,)), ((), ())), preferred_element_type=f32
-        )
-
-    def step(h, carry):
-        i = 2 + 2 * h
-        for j in range(BLOCK // LANES):
-            unit(i, j, s0, s1)
-        for j in range(BLOCK // LANES):
-            unit(i + 1, j, s1, s0)
+    def pair(h, carry):
+        for j in steps:
+            weigh(2 * h, j, s0, s1)
+        for j in steps:
+            weigh(2 * h + 1, j, s1, s0)
         return carry
 
-    for j in range(BLOCK // LANES):
-        score(2, slice(j * LANES, (j + 1) * LANES), s0)
-    lax.fori_loop(0, (n - 1) // 2, step, 0)
-
-    outs = (o0, o1, o2, o3)
+    def run(n):
+        for j in steps:
+            score(0, j, s0)
+        lax.fori_loop(0, (n + 1) // 2, pair, 0)
+
+    return run
+
+
+def partial(m, acc):
+    total = acc[HD : HD + 1]
+    some = total > 0.0
+    safe = jnp.where(some, total, 1.0)
+    level = jnp.where(some, m[:1] + jnp.log2(safe), LOW)
+    hi = level.astype(bf16)
+    mid = (level - hi.astype(f32)).astype(bf16)
+    lo = (level - hi.astype(f32) - mid.astype(f32)).astype(bf16)
+    stat = jnp.concatenate([hi, mid, lo, jnp.zeros((SENT - 3, level.shape[1]), bf16)], axis=0)
+    return (acc[:HD] * (1.0 / safe)).astype(bf16), stat
+
+
+def put(ref, span, part):
+    head, stat = part
+    ref[:HD, span] = head
+    ref[HD:, span] = stat
+
+
+def outer_kernel(
+    count_ref, flag_ref, place_ref, kv_ref, q_ref, o0, o1, o2, o3, k_ref, v_ref,
+    q_sc, m_sc, acc_sc, s0, s1, units,
+):
     for slot in range(4):
-        total = acc_sc[slot, HD : HD + 1]
-        some = total > 0.0
-        safe = jnp.where(some, total, 1.0)
-        head = (acc_sc[slot, :HD] * (1.0 / safe)).astype(bf16)
-        level = jnp.where(some, m_sc[slot, :1] + jnp.log2(safe), LOW)
-        hi = level.astype(bf16)
-        mid = (level - hi.astype(f32)).astype(bf16)
-        lo = (level - hi.astype(f32) - mid.astype(f32)).astype(bf16)
-        stat = jnp.concatenate([hi, mid, lo, jnp.zeros((STAT - 3, BLOCK), bf16)], axis=0)
-        outs[slot][:HD, :BLOCK] = head
-        outs[slot][HD:, :BLOCK] = stat
-        if slot < 3:
-            outs[slot + 1][:HD, BLOCK:] = head[:, BLOCK - QUARTER :]
-            outs[slot + 1][HD:, BLOCK:] = stat[:, BLOCK - QUARTER :]
-
-
-def attend(counts, flags, place, q, kv):
+        q_sc[slot] = q_ref[jnp.minimum(place_ref[0] + slot, 3)].reshape(BLOCK, HD)
+
+    token = token_of((BLOCK, HD), 0)
+    token_row = token_of((STAT, BLOCK), 1)
+    for t in range(4):
+        k = jnp.concatenate([kv_ref[y, t, :, 0].reshape(QUARTER, HD) for y in range(4)])
+        v = jnp.concatenate([kv_ref[y, t, :, 1].reshape(QUARTER, HD) for y in range(4)])
+        valid = token < count_ref[t]
+        k_ref[t] = jnp.where(valid, k, jnp.broadcast_to(k[0:1], k.shape))
+        v_ref[t, :HD] = jnp.where(valid, v, jnp.zeros_like(v)).T
+        v_ref[t, HD:] = jnp.where(token_row < count_ref[t], 1.0, 0.0).astype(bf16)
+
+    m_sc[...] = jnp.full(m_sc.shape, LOW, f32)
+    acc_sc[...] = jnp.zeros(acc_sc.shape, f32)
+    refs = (flag_ref, q_sc, k_ref, v_ref, m_sc, acc_sc, s0, s1)
+    run_units(units, (0, 1, 2), *refs)(list_units(units, flag_ref, (1, 2, 3), 4))
+    run_units(units, (2,), *refs)(list_units(units, flag_ref, (0,), 4))
+
+    last = BLOCK - LANES
+    own = partial(m_sc[0, :, last:], acc_sc[0, :, last:])
+    put(o0, slice(0, LANES), own)
+    before = [piece[:, LANES - QUARTER :] for piece in own]
+    for slot, ref in ((1, o1), (2, o2), (3, o3)):
+        part = partial(m_sc[slot], acc_sc[slot])
+        put(ref, slice(0, BLOCK), part)
+        put(ref, slice(BLOCK, BLOCK + QUARTER), before)
+        before = [piece[:, BLOCK - QUARTER :] for piece in part]
+
+
+def own_kernel(
+    flag_ref, place_ref, q_ref, k_ref, v_ref, o_ref, q_sc, m_sc, acc_sc, s0, s1, units
+):
+    q_sc[0] = q_ref[place_ref[0]].reshape(BLOCK, HD)
+    m_sc[...] = jnp.full(m_sc.shape, LOW, f32)
+    acc_sc[...] = jnp.zeros(acc_sc.shape, f32)
+    refs = (flag_ref, q_sc, k_ref, v_ref, m_sc, acc_sc, s0, s1)
+    run_units(units, (0, 1), *refs)(list_units(units, flag_ref, (0,), 1))
+    rest = BLOCK - LANES
+    put(o_ref, slice(0, rest), partial(m_sc[0, :, :rest], acc_sc[0, :, :rest]))
+
+
+def scratch(slots):
     vmem = pltpu.VMEM
-    return pl.pallas_call(
-        attend_kernel,
+    return [
+        vmem((slots, BLOCK, HD), bf16),
+        vmem((slots + 1, 8, BLOCK), f32),
+        vmem((slots + 1, HD + STAT, BLOCK), f32),
+        vmem((BLOCK, BLOCK), f32),
+        vmem((BLOCK, BLOCK), f32),
+        pltpu.SMEM((2, 16), jnp.int32),
+    ]
+
+
+def cost(units):
+    return pl.CostEstimate(
+        flops=4 * units * BLOCK * BLOCK * HD,
+        bytes_accessed=8 << 20,
+        transcendentals=units * BLOCK * BLOCK,
+    )
+
+
+def attend_outer(counts, flags, place, q, kv):
+    return pl.pallas_call(
+        outer_kernel,
         out_shape=[
-            jax.ShapeDtypeStruct((HD + STAT, BLOCK + (QUARTER if slot else 0)), bf16)
-            for slot in range(4)
+            jax.ShapeDtypeStruct((HD + SENT, columns), bf16)
+            for columns in (LANES, BLOCK + QUARTER, BLOCK + QUARTER, BLOCK + QUARTER)
+        ]
+        + [
+            jax.ShapeDtypeStruct((4, BLOCK, HD), bf16),
+            jax.ShapeDtypeStruct((4, HD + STAT, BLOCK), bf16),
         ],
         in_specs=[SM] * 3 + [VM] * 2,
-        out_specs=[VM] * 4,
-        scratch_shapes=[
-            vmem((4, BLOCK, HD), bf16),
-            vmem((4, BLOCK, HD), bf16),
-            vmem((4, HD + STAT, BLOCK), bf16),
-            vmem((5, 8, BLOCK), f32),
-            vmem((5, HD + STAT, BLOCK), f32),
-            vmem((BLOCK, BLOCK), f32),
-            vmem((BLOCK, BLOCK), f32),
-            pltpu.SMEM((2, 24), jnp.int32),
-        ],
-        compiler_params=PARAMS,
-        cost_estimate=pl.CostEstimate(
-            flops=64 * BLOCK * BLOCK * HD, bytes_accessed=8 << 20, transcendentals=16 * BLOCK * BLOCK
-        ),
+        out_specs=[VM] * 6,
+        scratch_shapes=scratch(4),
+        compiler_params=PARAMS,
+        cost_estimate=cost(14),
     )(counts, flags, place, kv, q)
+
+
+def attend_own(flags, place, q, k, v):
+    return pl.pallas_call(
+        own_kernel,
+        out_shape=jax.ShapeDtypeStruct((HD + SENT, BLOCK - LANES), bf16),
+        in_specs=[SM] * 2 + [VM] * 3,
+        out_specs=VM,
+        scratch_shapes=scratch(1),
+        compiler_params=PARAMS,
+        cost_estimate=cost(4),
+    )(flags, place, q, k, v)
 
 
 def blend(stats, heads):
@@ -204,8 +281,9 @@
     return total.T.astype(bf16)
 
 
-def merge_kernel(x_ref, r0, r1, r2, r3, o_ref):
-    stats, heads = [r0[HD:].astype(f32)], [r0[:HD]]
+def merge_kernel(x_ref, r0, r0_last, r1, r2, r3, o_ref):
+    own = jnp.concatenate([r0[...], r0_last[...]], axis=1)
+    stats, heads = [own[HD:].astype(f32)], [own[:HD]]
     for k, ref in ((1, r1), (2, r2), (3, r3)):
         stat = ref[HD:].astype(f32)
         row = lax.broadcasted_iota(jnp.int32, stat.shape, 0)
@@ -223,7 +301,7 @@
     return pl.pallas_call(
         merge_kernel,
         out_shape=jax.ShapeDtypeStruct((HEADS, 2, ROWS, HD), bf16),
-        in_specs=[SM] + [VM] * 4,
+        in_specs=[SM] + [VM] * 5,
         out_specs=VM,
         compiler_params=PARAMS,
     )(x, *parts)
@@ -270,27 +348,31 @@
     queries, keys, values, latent, entering, noise_level, token_counts, block_mask, gate_table
 ):
     x = lax.axis_index("x")
-    queries, keys, values, latent_in = (pltpu.with_memory_space_constraint(a, pltpu.HBM) for a in (queries, keys, values, latent))
-    packed, latent_level = pack(noise_level, queries, keys, values, latent_in)
+    sources = [
+        pltpu.with_memory_space_constraint(source, pltpu.HBM)
+        for source in (queries, keys, values, latent)
+    ]
+    packed, latent_level = pack(noise_level, *sources)
     packed = lax.all_to_all(packed, HEAD_AXES, split_axis=0, concat_axis=0, tiled=True)
     packed, latent_level = lax.optimization_barrier((packed, latent_level))
-    kv = packed[:, 1:3].reshape(4, 8, 2, ROWS, HD)
-    kv, packed = lax.optimization_barrier((kv, packed))
-    q = lax.all_gather(packed[:, 0], "x", axis=0, tiled=False)
-    kv = jnp.broadcast_to(kv[None], (4, *kv.shape))
+    q, kv = unpack(packed)
+    q = lax.all_gather(q, "x", axis=0, tiled=False)
     kv = lax.all_to_all(kv, "y", split_axis=0, concat_axis=0, tiled=True)
+    kv = kv.reshape(4, 4, 8, 2, ROWS, HD)
     onward = [(s, s + 1) for s in range(15)]
     latent_before = lax.ppermute(latent_level, ("x", "zh"), onward)
     padded = jnp.concatenate([block_mask, jnp.zeros_like(block_mask)], axis=0)
     flags = lax.dynamic_slice(padded, (4 * x, 4 * x), (16, 4))
     counts = lax.dynamic_slice(token_counts, (4 * x,), (4,))
-    parts = attend(counts, flags, x.reshape(1), q, kv)
+    place = x.reshape(1)
+    *parts, k, v = attend_outer(counts, flags, place, q, kv)
     parts, latent_before = lax.optimization_barrier((parts, latent_before))
-    received = [parts[0]] + [
+    received = [
         lax.ppermute(parts[k], "x", [(source, source + k) for source in range(4 - k)])
         for k in (1, 2, 3)
     ]
-    attended = merge(x.reshape(1), received)
+    own = attend_own(flags, place, q, k, v)
+    attended = merge(place, [own, parts[0], *received])
     returned = lax.all_to_all(attended, HEAD_AXES, split_axis=0, concat_axis=0, tiled=True)
     first = ((x == 0) & (lax.axis_index("zh") == 0)).astype(jnp.int32).reshape(1)
     return tuple(

time: 146 us -> 141 us (0.966)
  the two profiles are of different devices: /device:TPU:5 before, /device:TPU:7 now
where the time goes in v4:
time: 141 us
  blocking collectives  63.3 us (45%)
  waiting for transfers between devices  49.8 us (35%)
  starting transfers between devices  14.1 us (10%)
  Pallas kernels  12.2 us (9%)
    all_to_all x1, blocking collectives, local(): lax.all_to_all(packed, HEAD_AXES, split_axis=0, concat_axis=0, tiled=True)  52 us
    all_to_all x1, waiting for transfers between devices, local(): lax.all_to_all(attended, HEAD_AXES, split_axis=0, concat_axis=0, tiled=True)  28 us
    ppermute x3, waiting for transfers between devices, local(): lax.ppermute(parts[k], 'x', [(source, source + k) for source in range(4 -...  15.2 us
    all_gather x1, blocking collectives, local(): q = lax.all_gather(q, 'x', axis=0, tiled=False)  11.3 us
    all_to_all x1, waiting for transfers between devices, local(): kv = lax.all_to_all(kv, 'y', split_axis=0, concat_axis=0, tiled=True)  6.63 us
    all_to_all x1, starting transfers between devices, local(): kv = lax.all_to_all(kv, 'y', split_axis=0, concat_axis=0, tiled=True)  4.31 us
    all_to_all x1, starting transfers between devices, local(): lax.all_to_all(attended, HEAD_AXES, split_axis=0, concat_axis=0, tiled=True)  4.02 us
    pallas_call x1, Pallas kernels, attend_outer(): pl.pallas_call(outer_kernel, out_shape=[jax.ShapeDtypeStruct((HD + SENT,...  3.91 us
  transfers between devices with their start and end apart: 6, of which 5 were waited for; matrix products, arithmetic and copies ran while one was open for 0% of the time, Pallas kernels for 5%

profile of v4, /device:TPU:7, one launch (start us, length us, event | category | flops | bytes accessed | tf_op | source)
XLA Modules:
  0.0 141.0 jit_solution(10468111323649010657)
XLA Ops:
  1.3 1.3 shard_map.104
  2.6 52.0 %all_to_all.15.packed_ref = bf16[32,3,24,128]{3,2,1,0:T(8,128)(2,1)S(1)} all-to-all(bf16[32,3,24,128]{3,2,1,0:T(8,128)(2,1)S(1)} %get-tuple-element.19), channel_id=1, replica_groups=mesh['x'=4,'zh'=4,'zl'=4,'y'=4,'c'=2] {'zh','zl','c'}, dimensions={0} | all-to-all | bytes 1179648 | tf_op jit(solution)/shard_map/all_to_all | solution.py:356
  54.5 1.4 shard_map.105
  55.9 0.0 copy-start.4
  55.9 0.0 copy-start.3
  55.9 4.3 %all-to-all-start.1 = ((bf16[4,32,2,24,128]{4,3,2,1,0:T(8,128)(2,1)}), bf16[4,32,2,24,128]{4,3,2,1,0:T(8,128)(2,1)S(1)}, u32[]{:S(2)}, u32[]{:S(2)}) async-start(bf16[4,32,2,24,128]{4,3,2,1,0:T(8,128)(2,1)} %get-tuple-element.23), calls=%async_computation.1 | async-start | bytes 3145728 | tf_op jit(solution)/shard_map/all_to_all | solution.py:360
  60.2 0.0 copy-done.4
  60.3 0.1 dynamic_slice.7.count_ref
  60.3 0.0 copy-done.3
  60.3 0.1 pad_dynamic-slice_fusion.flag_ref
  60.4 1.9 %collective-permute-start = (bf16[1,24,4224]{2,1,0:T(8,128)(2,1)S(1)}, bf16[1,24,4224]{2,1,0:T(8,128)(2,1)S(1)}, u32[]{:S(2)}, u32[]{:S(2)}) collective-permute-start(bf16[1,24,4224]{2,1,0:T(8,128)(2,1)S(1)} %get-tuple-element.30), channel_id=1, source_target_pairs={{0,32},{32,64},{64,96},{96,128},{128,160},{160,192},{192,224},{224... | collective-permute-start | bytes 608264 | tf_op jit(solution)/shard_map/ppermute | solution.py:363
  62.3 11.3 %all-gather = bf16[128,24,128]{2,1,0:T(8,128)(2,1)S(1)} all-gather(bf16[32,24,128]{2,1,0:T(8,128)(2,1)S(1)} %get-tuple-element.22), channel_id=2, replica_groups=mesh['x'=4,'zh'=4,'zl'=4,'y'=4,'c'=2] {'x'}, dimensions={0}, use_global_device_ids=true | all-gather | bytes 983040 | tf_op jit(solution)/shard_map/all_gather | solution.py:359
  73.6 6.6 %all-to-all-done.1 = bf16[4,32,2,24,128]{4,3,2,1,0:T(8,128)(2,1)S(1)} async-done(((bf16[4,32,2,24,128]{4,3,2,1,0:T(8,128)(2,1)}), bf16[4,32,2,24,128]{4,3,2,1,0:T(8,128)(2,1)S(1)}, u32[]{:S(2)}, u32[]{:S(2)}) %all-to-all-start.1) | async-done | bytes 1572896 | tf_op jit(solution)/shard_map/all_to_all | solution.py:360
  80.3 3.9 %shard_map.106 = (bf16[136,256]{1,0:T(8,128)(2,1)S(1)}, bf16[136,960]{1,0:T(8,128)(2,1)S(1)}, bf16[136,960]{1,0:T(8,128)(2,1)S(1)}, bf16[136,960]{1,0:T(8,128)(2...) custom-call(s32[4]{0:T(128)S(1)} %dynamic_slice.7.count_ref, ...), custom_call_target="tpu_custom_call" | custom-call | flops 4227858432 | bytes 8388608 | tf_op jit(solution)/shard_map/pallas_call | solution.py:243
  84.2 0.0 collective-permute-done.latent_before_ref
  84.2 1.3 collective-permute-start.1
  85.5 1.3 collective-permute-start.2
  86.8 1.3 collective-permute-start.3
  88.1 3.6 %shard_map.107.r0 = bf16[136,512]{1,0:T(8,128)(2,1)S(1)} custom-call(s32[16,4]{1,0:T(8,128)S(1)} %pad_dynamic-slice_fusion.flag_ref, s32[1]{0:T(128)} %bitcast.1.place_ref.x_ref, bf16[4,32,24,128]{3,2,1,0:T(8,128)(2,1)S(1)} %bitcast.6, bf16[4,768,128]{2,1,0:T(8,128)(2,1)S(1)} %get-tuple-element.24.k_ref, bf16[4,144,768]{2,1,0:T(8,128)(2,1)S(1)} %get-tuple-element.25.v_ref), custom_call_target="tpu_custom_call" | custom-call | flops 1207959552 | bytes 8388608 | tf_op jit(solution)/shard_map/pallas_call | solution.py:262
  91.7 0.0 copy-start
  91.7 0.0 copy-start.1
  91.7 0.0 copy-start.2
  91.7 2.9 %collective-permute-done.1.r1 = bf16[136,960]{1,0:T(8,128)(2,1)S(1)} collective-permute-done((bf16[136,960]{1,0:T(8,128)(2,1)S(1)}, bf16[136,960]{1,0:T(8,128)(2,1)S(1)}, u32[]{:S(2)}, u32[]{:S(2)}) %collective-permute-start.1) | collective-permute-done | bytes 261152 | tf_op jit(solution)/shard_map/ppermute | solution.py:371
  94.6 4.5 %collective-permute-done.2.r2 = bf16[136,960]{1,0:T(8,128)(2,1)S(1)} collective-permute-done((bf16[136,960]{1,0:T(8,128)(2,1)S(1)}, bf16[136,960]{1,0:T(8,128)(2,1)S(1)}, u32[]{:S(2)}, u32[]{:S(2)}) %collective-permute-start.2) | collective-permute-done | bytes 261152 | tf_op jit(solution)/shard_map/ppermute | solution.py:371
  99.1 7.7 %collective-permute-done.3.r3 = bf16[136,960]{1,0:T(8,128)(2,1)S(1)} collective-permute-done((bf16[136,960]{1,0:T(8,128)(2,1)S(1)}, bf16[136,960]{1,0:T(8,128)(2,1)S(1)}, u32[]{:S(2)}, u32[]{:S(2)}) %collective-permute-start.3) | collective-permute-done | bytes 261152 | tf_op jit(solution)/shard_map/ppermute | solution.py:371
  106.9 1.1 shard_map.108
  108.0 4.0 %all-to-all-start.2 = ((bf16[32,2,24,128]{3,2,1,0:T(8,128)(2,1)}), bf16[32,2,24,128]{3,2,1,0:T(8,128)(2,1)S(1)}, u32[]{:S(2)}, u32[]{:S(2)}) async-start(bf16[32,2,24,128]{3,2,1,0:T(8,128)(2,1)} %shard_map.108), calls=%async_computation.2 | async-start | bytes 786432 | tf_op jit(solution)/shard_map/all_to_all | solution.py:376
  112.0 28.0 %all-to-all-done.2.r_ref = bf16[32,2,24,128]{3,2,1,0:T(8,128)(2,1)S(1)} async-done(((bf16[32,2,24,128]{3,2,1,0:T(8,128)(2,1)}), bf16[32,2,24,128]{3,2,1,0:T(8,128)(2,1)S(1)}, u32[]{:S(2)}, u32[]{:S(2)}) %all-to-all-start.2) | async-done | bytes 393248 | tf_op jit(solution)/shard_map/all_to_all | solution.py:376
  140.0 0.0 copy-done
  140.0 0.0 copy-done.1
  140.0 0.0 copy-done.2
  140.0 1.0 shard_map.109
Async XLA Ops:
  55.9 4.3 %copy-start.4 = (s32[16]{0:T(128)S(1)}, s32[16]{0:T(128)}, u32[]{:S(2)}) copy-start(s32[16]{0:T(128)} %param.15) | copy-start | bytes 196
  55.9 4.4 %copy-start.3 = (s32[16,16]{1,0:T(8,128)S(1)}, s32[16,16]{1,0:T(8,128)}, u32[]{:S(2)}) copy-start(s32[16,16]{1,0:T(8,128)} %param.16) | copy-start | bytes 3076
  55.9 24.3 %all-to-all-start.1 = ((bf16[4,32,2,24,128]{4,3,2,1,0:T(8,128)(2,1)}), bf16[4,32,2,24,128]{4,3,2,1,0:T(8,128)(2,1)S(1)}, u32[]{:S(2)}, u32[]{:S(2)}) async-start(bf16[4,32,2,24,128]{4,3,2,1,0:T(8,128)(2,1)} %get-tuple-element.23), calls=%async_computation.1 | async-start | bytes 3145728 | tf_op jit(solution)/shard_map/all_to_all | solution.py:360
  60.4 23.8 %collective-permute-start = (bf16[1,24,4224]{2,1,0:T(8,128)(2,1)S(1)}, bf16[1,24,4224]{2,1,0:T(8,128)(2,1)S(1)}, u32[]{:S(2)}, u32[]{:S(2)}) collective-permute-start(bf16[1,24,4224]{2,1,0:T(8,128)(2,1)S(1)} %get-tuple-element.30), channel_id=1, source_target_pairs={{0,32},{32,64},{64,96},{96,128},{128,160},{160,192},{192,224},{224... | collective-permute-start | bytes 608264 | tf_op jit(solution)/shard_map/ppermute | solution.py:363
  84.2 10.4 %collective-permute-start.1 = (bf16[136,960]{1,0:T(8,128)(2,1)S(1)}, bf16[136,960]{1,0:T(8,128)(2,1)S(1)}, u32[]{:S(2)}, u32[]{:S(2)}) collective-permute-start(bf16[136,960]{1,0:T(8,128)(2,1)S(1)} %get-tuple-element.32), channel_id=1, source_target_pairs={{0,128},{128,256},{256,384},{1,129},{129,257},{257,385},{2,130},{1... | collective-permute-start | bytes 783368 | tf_op jit(solution)/shard_map/ppermute | solution.py:371
  85.5 13.6 %collective-permute-start.2 = (bf16[136,960]{1,0:T(8,128)(2,1)S(1)}, bf16[136,960]{1,0:T(8,128)(2,1)S(1)}, u32[]{:S(2)}, u32[]{:S(2)}) collective-permute-start(bf16[136,960]{1,0:T(8,128)(2,1)S(1)} %get-tuple-element.33), channel_id=1, source_target_pairs={{0,256},{128,384},{1,257},{129,385},{2,258},{130,386},{3,259},{131... | collective-permute-start | bytes 783368 | tf_op jit(solution)/shard_map/ppermute | solution.py:371
  86.8 20.1 %collective-permute-start.3 = (bf16[136,960]{1,0:T(8,128)(2,1)S(1)}, bf16[136,960]{1,0:T(8,128)(2,1)S(1)}, u32[]{:S(2)}, u32[]{:S(2)}) collective-permute-start(bf16[136,960]{1,0:T(8,128)(2,1)S(1)} %get-tuple-element.34), channel_id=1, source_target_pairs={{0,384},{1,385},{2,386},{3,387},{4,388},{5,389},{6,390},{7,391},{8... | collective-permute-start | bytes 783368 | tf_op jit(solution)/shard_map/ppermute | solution.py:371
  91.7 48.3 %copy-start = (bf16[1,24,4096]{2,1,0:T(8,128)(2,1)S(1)}, bf16[1,24,4096]{2,1,0:T(8,128)(2,1)}, u32[]{:S(2)}) copy-start(bf16[1,24,4096]{2,1,0:T(8,128)(2,1)} %latent_ref.1) | copy-start | bytes 589828
  91.7 48.3 %copy-start.1 = (f32[16,4096]{1,0:T(8,128)S(1)}, f32[16,4096]{1,0:T(8,128)}, u32[]{:S(2)}) copy-start(f32[16,4096]{1,0:T(8,128)} %gate_ref.1) | copy-start | bytes 786436
  91.7 48.3 %copy-start.2 = (bf16[24,4096]{1,0:T(8,128)(2,1)S(1)}, bf16[24,4096]{1,0:T(8,128)(2,1)}, u32[]{:S(2)}) copy-start(bf16[24,4096]{1,0:T(8,128)(2,1)} %entering_ref.1) | copy-start | bytes 589828
  108.0 32.1 %all-to-all-start.2 = ((bf16[32,2,24,128]{3,2,1,0:T(8,128)(2,1)}), bf16[32,2,24,128]{3,2,1,0:T(8,128)(2,1)S(1)}, u32[]{:S(2)}, u32[]{:S(2)}) async-start(bf16[32,2,24,128]{3,2,1,0:T(8,128)(2,1)} %shard_map.108), calls=%async_computation.2 | async-start | bytes 786432 | tf_op jit(solution)/shard_map/all_to_all | solution.py:376

commit v5 on v4

--- a/solution.py
+++ b/solution.py
@@ -155,6 +155,11 @@
     return run
 
 
+def clear(m_sc, acc_sc):
+    m_sc[...] = jnp.full(m_sc.shape, LOW, f32)
+    acc_sc[...] = jnp.zeros(acc_sc.shape, f32)
+
+
 def partial(m, acc):
     total = acc[HD : HD + 1]
     some = total > 0.0
@@ -173,11 +178,11 @@
     ref[HD:, span] = stat
 
 
-def outer_kernel(
-    count_ref, flag_ref, place_ref, kv_ref, q_ref, o0, o1, o2, o3, k_ref, v_ref,
+def far_kernel(
+    count_ref, flag_ref, place_ref, kv_ref, q_ref, o1_last, o2, o3, k_ref, v_ref,
     q_sc, m_sc, acc_sc, s0, s1, units,
 ):
-    for slot in range(4):
+    for slot in range(1, 4):
         q_sc[slot] = q_ref[jnp.minimum(place_ref[0] + slot, 3)].reshape(BLOCK, HD)
 
     token = token_of((BLOCK, HD), 0)
@@ -190,33 +195,66 @@
         v_ref[t, :HD] = jnp.where(valid, v, jnp.zeros_like(v)).T
         v_ref[t, HD:] = jnp.where(token_row < count_ref[t], 1.0, 0.0).astype(bf16)
 
-    m_sc[...] = jnp.full(m_sc.shape, LOW, f32)
-    acc_sc[...] = jnp.zeros(acc_sc.shape, f32)
+    clear(m_sc, acc_sc)
     refs = (flag_ref, q_sc, k_ref, v_ref, m_sc, acc_sc, s0, s1)
-    run_units(units, (0, 1, 2), *refs)(list_units(units, flag_ref, (1, 2, 3), 4))
-    run_units(units, (2,), *refs)(list_units(units, flag_ref, (0,), 4))
+    run_units(units, (0, 1, 2), *refs)(list_units(units, flag_ref, (2, 3), 4))
+    run_units(units, (2,), *refs)(list_units(units, flag_ref, (1,), 4))
 
     last = BLOCK - LANES
-    own = partial(m_sc[0, :, last:], acc_sc[0, :, last:])
-    put(o0, slice(0, LANES), own)
-    before = [piece[:, LANES - QUARTER :] for piece in own]
-    for slot, ref in ((1, o1), (2, o2), (3, o3)):
+    part = partial(m_sc[1, :, last:], acc_sc[1, :, last:])
+    put(o1_last, slice(0, LANES), part)
+    for slot, ref in ((2, o2), (3, o3)):
+        put(ref, slice(BLOCK, BLOCK + QUARTER), [piece[:, -QUARTER:] for piece in part])
         part = partial(m_sc[slot], acc_sc[slot])
         put(ref, slice(0, BLOCK), part)
-        put(ref, slice(BLOCK, BLOCK + QUARTER), before)
-        before = [piece[:, BLOCK - QUARTER :] for piece in part]
+
+
+def attend_rest(out_ref, units, flag_ref, q_sc, k_ref, v_ref, m_sc, acc_sc, s0, s1):
+    dummy = q_sc.shape[0]
+    refs = (flag_ref, q_sc, k_ref, v_ref, m_sc, acc_sc, s0, s1)
+    run_units(units, (0, 1), *refs)(list_units(units, flag_ref, (0,), dummy))
+    rest = BLOCK - LANES
+    put(out_ref, slice(0, rest), partial(m_sc[0, :, :rest], acc_sc[0, :, :rest]))
+
+
+def next_kernel(
+    flag_ref, place_ref, q_ref, k_ref, v_ref, o1_last, o0_last, o0_rest, o1,
+    q_sc, m_sc, acc_sc, s0, s1, units,
+):
+    for slot in range(2):
+        q_sc[slot] = q_ref[jnp.minimum(place_ref[0] + slot, 3)].reshape(BLOCK, HD)
+    clear(m_sc, acc_sc)
+    refs = (flag_ref, q_sc, k_ref, v_ref, m_sc, acc_sc, s0, s1)
+    run_units(units, (0, 1), *refs)(list_units(units, flag_ref, (1,), 2))
+    run_units(units, (2,), *refs)(list_units(units, flag_ref, (0,), 2))
+    last = BLOCK - LANES
+    put(o1, slice(0, last), partial(m_sc[1, :, :last], acc_sc[1, :, :last]))
+    o1[:, last:BLOCK] = o1_last[...]
+    part = partial(m_sc[0, :, last:], acc_sc[0, :, last:])
+    put(o0_last, slice(0, LANES), part)
+    put(o1, slice(BLOCK, BLOCK + QUARTER), [piece[:, -QUARTER:] for piece in part])
+
+    @pl.when(place_ref[0] >= 2)
+    def _():
+        attend_rest(o0_rest, units, *refs)
+
+    @pl.when(place_ref[0] < 2)
+    def _():
+        o0_rest[...] = jnp.zeros(o0_rest.shape, bf16)
 
 
 def own_kernel(
-    flag_ref, place_ref, q_ref, k_ref, v_ref, o_ref, q_sc, m_sc, acc_sc, s0, s1, units
+    flag_ref, place_ref, q_ref, k_ref, v_ref, rest_ref, o_ref, q_sc, m_sc, acc_sc, s0, s1, units
 ):
-    q_sc[0] = q_ref[place_ref[0]].reshape(BLOCK, HD)
-    m_sc[...] = jnp.full(m_sc.shape, LOW, f32)
-    acc_sc[...] = jnp.zeros(acc_sc.shape, f32)
-    refs = (flag_ref, q_sc, k_ref, v_ref, m_sc, acc_sc, s0, s1)
-    run_units(units, (0, 1), *refs)(list_units(units, flag_ref, (0,), 1))
-    rest = BLOCK - LANES
-    put(o_ref, slice(0, rest), partial(m_sc[0, :, :rest], acc_sc[0, :, :rest]))
+    @pl.when(place_ref[0] >= 2)
+    def _():
+        o_ref[...] = rest_ref[...]
+
+    @pl.when(place_ref[0] < 2)
+    def _():
+        q_sc[0] = q_ref[place_ref[0]].reshape(BLOCK, HD)
+        clear(m_sc, acc_sc)
+        attend_rest(o_ref, units, flag_ref, q_sc, k_ref, v_ref, m_sc, acc_sc, s0, s1)
 
 
 def scratch(slots):
@@ -239,35 +277,50 @@
     )
 
 
-def attend_outer(counts, flags, place, q, kv):
-    return pl.pallas_call(
-        outer_kernel,
+def result(columns):
+    return jax.ShapeDtypeStruct((HD + SENT, columns), bf16)
+
+
+def attend_far(counts, flags, place, q, kv):
+    return pl.pallas_call(
+        far_kernel,
         out_shape=[
-            jax.ShapeDtypeStruct((HD + SENT, columns), bf16)
-            for columns in (LANES, BLOCK + QUARTER, BLOCK + QUARTER, BLOCK + QUARTER)
-        ]
-        + [
+            result(LANES),
+            result(BLOCK + QUARTER),
+            result(BLOCK + QUARTER),
             jax.ShapeDtypeStruct((4, BLOCK, HD), bf16),
             jax.ShapeDtypeStruct((4, HD + STAT, BLOCK), bf16),
         ],
         in_specs=[SM] * 3 + [VM] * 2,
-        out_specs=[VM] * 6,
+        out_specs=[VM] * 5,
         scratch_shapes=scratch(4),
         compiler_params=PARAMS,
-        cost_estimate=cost(14),
+        cost_estimate=cost(10),
     )(counts, flags, place, kv, q)
 
 
-def attend_own(flags, place, q, k, v):
+def attend_next(flags, place, q, k, v, last):
+    return pl.pallas_call(
+        next_kernel,
+        out_shape=[result(LANES), result(BLOCK - LANES), result(BLOCK + QUARTER)],
+        in_specs=[SM] * 2 + [VM] * 4,
+        out_specs=[VM] * 3,
+        scratch_shapes=scratch(2),
+        compiler_params=PARAMS,
+        cost_estimate=cost(4),
+    )(flags, place, q, k, v, last)
+
+
+def attend_own(flags, place, q, k, v, rest):
     return pl.pallas_call(
         own_kernel,
-        out_shape=jax.ShapeDtypeStruct((HD + SENT, BLOCK - LANES), bf16),
-        in_specs=[SM] * 2 + [VM] * 3,
+        out_shape=result(BLOCK - LANES),
+        in_specs=[SM] * 2 + [VM] * 4,
         out_specs=VM,
         scratch_shapes=scratch(1),
         compiler_params=PARAMS,
         cost_estimate=cost(4),
-    )(flags, place, q, k, v)
+    )(flags, place, q, k, v, rest)
 
 
 def blend(stats, heads):
@@ -278,7 +331,7 @@
     shares = [jnp.exp2(level - top) for level in levels]
     whole = sum(shares[1:], shares[0])
     total = sum(head.astype(f32) * (share / whole) for head, share in zip(heads, shares))
-    return total.T.astype(bf16)
+    return total.astype(bf16).T
 
 
 def merge_kernel(x_ref, r0, r0_last, r1, r2, r3, o_ref):
@@ -365,14 +418,18 @@
     flags = lax.dynamic_slice(padded, (4 * x, 4 * x), (16, 4))
     counts = lax.dynamic_slice(token_counts, (4 * x,), (4,))
     place = x.reshape(1)
-    *parts, k, v = attend_outer(counts, flags, place, q, kv)
-    parts, latent_before = lax.optimization_barrier((parts, latent_before))
-    received = [
-        lax.ppermute(parts[k], "x", [(source, source + k) for source in range(4 - k)])
-        for k in (1, 2, 3)
-    ]
-    own = attend_own(flags, place, q, k, v)
-    attended = merge(place, [own, parts[0], *received])
+    last, part2, part3, k, v = attend_far(counts, flags, place, q, kv)
+    part2, part3, latent_before = lax.optimization_barrier((part2, part3, latent_before))
+
+    def onward_in_x(part, steps):
+        return lax.ppermute(part, "x", [(source, source + steps) for source in range(4 - steps)])
+
+    received3, received2 = onward_in_x(part3, 3), onward_in_x(part2, 2)
+    own_last, own_rest, part1 = attend_next(flags, place, q, k, v, last)
+    received1 = onward_in_x(part1, 1)
+    q, received2, received3 = lax.optimization_barrier((q, received2, received3))
+    own = attend_own(flags, place, q, k, v, own_rest)
+    attended = merge(place, [own, own_last, received1, received2, received3])
     returned = lax.all_to_all(attended, HEAD_AXES, split_axis=0, concat_axis=0, tiled=True)
     first = ((x == 0) & (lax.axis_index("zh") == 0)).astype(jnp.int32).reshape(1)
     return tuple(

time: 141 us -> 140 us (level)
  the two profiles are of different devices: /device:TPU:7 before, /device:TPU:3 now
where the time goes in v5:
time: 140 us
  blocking collectives  66 us (47%)
  waiting for transfers between devices  35.4 us (25%)
  Pallas kernels  19.9 us (14%)
  starting transfers between devices  17 us (12%)
  between operations  1.41 us (1%)
    all_to_all x1, blocking collectives, local(): lax.all_to_all(packed, HEAD_AXES, split_axis=0, concat_axis=0, tiled=True)  52 us
    all_to_all x1, waiting for transfers between devices, local(): lax.all_to_all(attended, HEAD_AXES, split_axis=0, concat_axis=0, tiled=True)  28 us
    all_gather x1, blocking collectives, local(): q = lax.all_gather(q, 'x', axis=0, tiled=False)  14 us
    pallas_call x1, Pallas kernels, attend_far(): pl.pallas_call(far_kernel, out_shape=[result(LANES), result(BLOCK + QUART...  6.42 us
    all_to_all x1, starting transfers between devices, local(): lax.all_to_all(attended, HEAD_AXES, split_axis=0, concat_axis=0, tiled=True)  5.83 us
    pallas_call x1, Pallas kernels, attend_next(): pl.pallas_call(next_kernel, out_shape=[result(LANES), result(BLOCK - LANE...  5.19 us
    ppermute x3, starting transfers between devices, onward_in_x(): lax.ppermute(part, 'x', [(source, source + steps) for source in range(4 -...  5 us
    all_to_all x1, starting transfers between devices, local(): kv = lax.all_to_all(kv, 'y', split_axis=0, concat_axis=0, tiled=True)  4.31 us
  transfers between devices with their start and end apart: 6, of which 3 were waited for; matrix products, arithmetic and copies ran while one was open for 0% of the time, Pallas kernels for 11%

profile of v5, /device:TPU:3, one launch (start us, length us, event | category | flops | bytes accessed | tf_op | source)
XLA Modules:
  0.0 140.0 jit_solution(2159889237613832851)
XLA Ops:
  1.3 1.3 shard_map.104
  2.6 52.0 %all_to_all.15.packed_ref = bf16[32,3,24,128]{3,2,1,0:T(8,128)(2,1)S(1)} all-to-all(bf16[32,3,24,128]{3,2,1,0:T(8,128)(2,1)S(1)} %get-tuple-element.22), channel_id=1, replica_groups=mesh['x'=4,'zh'=4,'zl'=4,'y'=4,'c'=2] {'zh','zl','c'}, dimensions={0} | all-to-all | bytes 1179648 | tf_op jit(solution)/shard_map/all_to_all | solution.py:409
  54.5 1.4 shard_map.105
  55.9 0.0 copy-start.4
  55.9 4.3 %all-to-all-start.1 = ((bf16[4,32,2,24,128]{4,3,2,1,0:T(8,128)(2,1)}), bf16[4,32,2,24,128]{4,3,2,1,0:T(8,128)(2,1)S(1)}, u32[]{:S(2)}, u32[]{:S(2)}) async-start(bf16[4,32,2,24,128]{4,3,2,1,0:T(8,128)(2,1)} %get-tuple-element.26), calls=%async_computation.1 | async-start | bytes 3145728 | tf_op jit(solution)/shard_map/all_to_all | solution.py:413
  60.3 0.0 copy-done.4
  60.3 0.1 dynamic_slice.7.count_ref
  60.3 0.0 copy-done.3
  60.3 0.1 pad_dynamic-slice_fusion.flag_ref
  60.4 1.9 %collective-permute-start = (bf16[1,24,4224]{2,1,0:T(8,128)(2,1)S(1)}, bf16[1,24,4224]{2,1,0:T(8,128)(2,1)S(1)}, u32[]{:S(2)}, u32[]{:S(2)}) collective-permute-start(bf16[1,24,4224]{2,1,0:T(8,128)(2,1)S(1)} %get-tuple-element.29), channel_id=1, source_target_pairs={{0,32},{32,64},{64,96},{96,128},{128,160},{160,192},{192,224},{224... | collective-permute-start | bytes 608264 | tf_op jit(solution)/shard_map/ppermute | solution.py:416
  62.3 14.0 %all-gather = bf16[128,24,128]{2,1,0:T(8,128)(2,1)S(1)} all-gather(bf16[32,24,128]{2,1,0:T(8,128)(2,1)S(1)} %get-tuple-element.25), channel_id=2, replica_groups=mesh['x'=4,'zh'=4,'zl'=4,'y'=4,'c'=2] {'x'}, dimensions={0}, use_global_device_ids=true | all-gather | bytes 983040 | tf_op jit(solution)/shard_map/all_gather | solution.py:412
  76.4 3.9 %all-to-all-done.1 = bf16[4,32,2,24,128]{4,3,2,1,0:T(8,128)(2,1)S(1)} async-done(((bf16[4,32,2,24,128]{4,3,2,1,0:T(8,128)(2,1)}), bf16[4,32,2,24,128]{4,3,2,1,0:T(8,128)(2,1)S(1)}, u32[]{:S(2)}, u32[]{:S(2)}) %all-to-all-start.1) | async-done | bytes 1572896 | tf_op jit(solution)/shard_map/all_to_all | solution.py:413
  80.3 6.4 %shard_map.106 = (bf16[136,256]{1,0:T(8,128)(2,1)S(1)}, bf16[136,960]{1,0:T(8,128)(2,1)S(1)}, bf16[136,960]{1,0:T(8,128)(2,1)S(1)}, bf16[4,768,128]{2,1,0:T(8,128)(2,1)S(1)}, bf16[4,144,768]{2,1,0:T(8,128)(2,1)S(1)}) custom-call(s32[4]{0:T(128)S(1)} %dynamic_slice.7.count_ref, s32[16,4]{1,0:T(8,128)S(1)} %pad_dynamic-slice_fusion.flag_ref, ...), custom_call_target="tpu_custom_call" | custom-call | flops 3019898880 | bytes 8388608 | tf_op jit(solution)/shard_map/pallas_call | solution.py:285
  86.7 0.0 collective-permute-done.latent_before_ref
  86.7 1.3 collective-permute-start.1
  88.0 0.7 collective-permute-start.2
  88.7 5.2 %shard_map.107 = (bf16[136,256]{1,0:T(8,128)(2,1)S(1)}, bf16[136,512]{1,0:T(8,128)(2,1)S(1)}, bf16[136,960]{1,0:T(8,128)(2,1)S(1)}) custom-call(s32[16,4]{1,0:T(8,128)S(1)} %pad_dynamic-slice_fusion.flag_ref, s32[1]{0:T(128)} %bitcast.1.place_ref.x_ref, bf16[4,32,24,128]{3,2,1,0:T(8,128)(2,1)S(1)} %bitcast.6, ...), custom_call_target="tpu_custom_call" | custom-call | flops 1207959552 | bytes 8388608 | tf_op jit(solution)/shard_map/pallas_call | solution.py:303
  93.9 3.0 %collective-permute-start.3 = (bf16[136,960]{1,0:T(8,128)(2,1)S(1)}, bf16[136,960]{1,0:T(8,128)(2,1)S(1)}, u32[]{:S(2)}, u32[]{:S(2)}) collective-permute-start(bf16[136,960]{1,0:T(8,128)(2,1)S(1)} %get-tuple-element.38), channel_id=1, source_target_pairs={{0,128},{128,256},{256,384},{1,129},{129,257},{257,385},{2,130},{1... | collective-permute-start | bytes 783368 | tf_op jit(solution)/shard_map/ppermute | solution.py:425
  96.9 0.0 collective-permute-done.1.r2
  96.9 0.0 collective-permute-done.2.r3
  96.9 3.6 %shard_map.108.r0 = bf16[136,512]{1,0:T(8,128)(2,1)S(1)} custom-call(s32[16,4]{1,0:T(8,128)S(1)} %pad_dynamic-slice_fusion.flag_ref, s32[1]{0:T(128)} %bitcast.1.place_ref.x_ref, bf16[4,32,24,128]{3,2,1,0:T(8,128)(2,1)S(1)} %bitcast.7, bf16[4,768,128]{2,1,0:T(8,128)(2,1)S(1)} %get-tuple-element.33.k_ref, bf16[4,144,768]{2,1,0:T(8,128)(2,1)S(1)} %get-tuple-element.34.v_ref, ...), custom_call_target="tpu_custom_call" | custom-call | flops 1207959552 | bytes 8388608 | tf_op jit(solution)/shard_map/pallas_call | solution.py:315
  100.5 0.0 copy-start
  100.5 0.0 copy-start.1
  100.5 0.0 copy-start.2
  100.6 3.5 %collective-permute-done.3.r1 = bf16[136,960]{1,0:T(8,128)(2,1)S(1)} collective-permute-done((bf16[136,960]{1,0:T(8,128)(2,1)S(1)}, bf16[136,960]{1,0:T(8,128)(2,1)S(1)}, u32[]{:S(2)}, u32[]{:S(2)}) %collective-permute-start.3) | collective-permute-done | bytes 261152 | tf_op jit(solution)/shard_map/ppermute | solution.py:425
  104.0 1.1 shard_map.109
  105.1 5.8 %all-to-all-start.2 = ((bf16[32,2,24,128]{3,2,1,0:T(8,128)(2,1)}), bf16[32,2,24,128]{3,2,1,0:T(8,128)(2,1)S(1)}, u32[]{:S(2)}, u32[]{:S(2)}) async-start(bf16[32,2,24,128]{3,2,1,0:T(8,128)(2,1)} %shard_map.109), calls=%async_computation.2 | async-start | bytes 786432 | tf_op jit(solution)/shard_map/all_to_all | solution.py:433
  110.9 28.0 %all-to-all-done.2.r_ref = bf16[32,2,24,128]{3,2,1,0:T(8,128)(2,1)S(1)} async-done(((bf16[32,2,24,128]{3,2,1,0:T(8,128)(2,1)}), bf16[32,2,24,128]{3,2,1,0:T(8,128)(2,1)S(1)}, u32[]{:S(2)}, u32[]{:S(2)}) %all-to-all-start.2) | async-done | bytes 393248 | tf_op jit(solution)/shard_map/all_to_all | solution.py:433
  139.0 0.0 copy-done
  139.0 0.0 copy-done.1
  139.0 0.0 copy-done.2
  139.0 1.0 shard_map.110
  (1 shorter events, 0.0 us)
Async XLA Ops:
  55.9 4.3 %copy-start.4 = (s32[16]{0:T(128)S(1)}, s32[16]{0:T(128)}, u32[]{:S(2)}) copy-start(s32[16]{0:T(128)} %param.15) | copy-start | bytes 196
  55.9 4.4 %copy-start.3 = (s32[16,16]{1,0:T(8,128)S(1)}, s32[16,16]{1,0:T(8,128)}, u32[]{:S(2)}) copy-start(s32[16,16]{1,0:T(8,128)} %param.16) | copy-start | bytes 3076
  55.9 24.3 %all-to-all-start.1 = ((bf16[4,32,2,24,128]{4,3,2,1,0:T(8,128)(2,1)}), bf16[4,32,2,24,128]{4,3,2,1,0:T(8,128)(2,1)S(1)}, u32[]{:S(2)}, u32[]{:S(2)}) async-start(bf16[4,32,2,24,128]{4,3,2,1,0:T(8,128)(2,1)} %get-tuple-element.26), calls=%async_computation.1 | async-start | bytes 3145728 | tf_op jit(solution)/shard_map/all_to_all | solution.py:413
  60.4 26.3 %collective-permute-start = (bf16[1,24,4224]{2,1,0:T(8,128)(2,1)S(1)}, bf16[1,24,4224]{2,1,0:T(8,128)(2,1)S(1)}, u32[]{:S(2)}, u32[]{:S(2)}) collective-permute-start(bf16[1,24,4224]{2,1,0:T(8,128)(2,1)S(1)} %get-tuple-element.29), channel_id=1, source_target_pairs={{0,32},{32,64},{64,96},{96,128},{128,160},{160,192},{192,224},{224... | collective-permute-start | bytes 608264 | tf_op jit(solution)/shard_map/ppermute | solution.py:416
  86.7 10.2 %collective-permute-start.1 = (bf16[136,960]{1,0:T(8,128)(2,1)S(1)}, bf16[136,960]{1,0:T(8,128)(2,1)S(1)}, u32[]{:S(2)}, u32[]{:S(2)}) collective-permute-start(bf16[136,960]{1,0:T(8,128)(2,1)S(1)} %get-tuple-element.30), channel_id=1, source_target_pairs={{0,256},{128,384},{1,257},{129,385},{2,258},{130,386},{3,259},{131... | collective-permute-start | bytes 783368 | tf_op jit(solution)/shard_map/ppermute | solution.py:425
  88.0 8.9 %collective-permute-start.2 = (bf16[136,960]{1,0:T(8,128)(2,1)S(1)}, bf16[136,960]{1,0:T(8,128)(2,1)S(1)}, u32[]{:S(2)}, u32[]{:S(2)}) collective-permute-start(bf16[136,960]{1,0:T(8,128)(2,1)S(1)} %get-tuple-element.31), channel_id=1, source_target_pairs={{0,384},{1,385},{2,386},{3,387},{4,388},{5,389},{6,390},{7,391},{8... | collective-permute-start | bytes 783368 | tf_op jit(solution)/shard_map/ppermute | solution.py:425
  93.9 10.1 %collective-permute-start.3 = (bf16[136,960]{1,0:T(8,128)(2,1)S(1)}, bf16[136,960]{1,0:T(8,128)(2,1)S(1)}, u32[]{:S(2)}, u32[]{:S(2)}) collective-permute-start(bf16[136,960]{1,0:T(8,128)(2,1)S(1)} %get-tuple-element.38), channel_id=1, source_target_pairs={{0,128},{128,256},{256,384},{1,129},{129,257},{257,385},{2,130},{1... | collective-permute-start | bytes 783368 | tf_op jit(solution)/shard_map/ppermute | solution.py:425
  100.5 38.4 %copy-start = (bf16[1,24,4096]{2,1,0:T(8,128)(2,1)S(1)}, bf16[1,24,4096]{2,1,0:T(8,128)(2,1)}, u32[]{:S(2)}) copy-start(bf16[1,24,4096]{2,1,0:T(8,128)(2,1)} %latent_ref.1) | copy-start | bytes 589828
  100.5 38.4 %copy-start.1 = (f32[16,4096]{1,0:T(8,128)S(1)}, f32[16,4096]{1,0:T(8,128)}, u32[]{:S(2)}) copy-start(f32[16,4096]{1,0:T(8,128)} %gate_ref.1) | copy-start | bytes 786436
  100.5 38.4 %copy-start.2 = (bf16[24,4096]{1,0:T(8,128)(2,1)S(1)}, bf16[24,4096]{1,0:T(8,128)(2,1)}, u32[]{:S(2)}) copy-start(bf16[24,4096]{1,0:T(8,128)(2,1)} %entering_ref.1) | copy-start | bytes 589828
  105.1 33.9 %all-to-all-start.2 = ((bf16[32,2,24,128]{3,2,1,0:T(8,128)(2,1)}), bf16[32,2,24,128]{3,2,1,0:T(8,128)(2,1)S(1)}, u32[]{:S(2)}, u32[]{:S(2)}) async-start(bf16[32,2,24,128]{3,2,1,0:T(8,128)(2,1)} %shard_map.109), calls=%async_computation.2 | async-start | bytes 786432 | tf_op jit(solution)/shard_map/all_to_all | solution.py:433

commit v6 on v5

--- a/solution.py
+++ b/solution.py
@@ -24,7 +24,8 @@
 VM = pl.BlockSpec(memory_space=pltpu.VMEM)
 SM = pl.BlockSpec(memory_space=pltpu.SMEM)
 PARAMS = pltpu.CompilerParams(vmem_limit_bytes=48 * 2**20)
-HEAD_AXES = ("zh", "zl", "c")
+HEAD_AXES = ("zl", "zh", "c")
+PAIR_ORDER = [(2 * (4 * zl + zh), 2 * (4 * zh + zl)) for zh in range(4) for zl in range(4)]
 
 
 def pack_kernel(level_ref, q_hbm, k_hbm, v_hbm, latent_hbm, o_ref, latent_ref, buf, sems):
@@ -62,9 +63,11 @@
 
 
 def unpack_kernel(packed_ref, q_ref, kv_ref):
-    q_ref[...] = packed_ref[:, 0]
-    for copy in range(4):
-        kv_ref[copy] = packed_ref[:, 1:]
+    for source, place in PAIR_ORDER:
+        q_ref[place : place + 2] = packed_ref[source : source + 2, 0]
+        kv = packed_ref[source : source + 2, 1:]
+        for copy in range(4):
+            kv_ref[copy, place : place + 2] = kv
 
 
 def unpack(packed):
@@ -345,9 +348,10 @@
     own = blend([stat[:, :BLOCK] for stat in stats], [head[:, :BLOCK] for head in heads])
     tail = blend([stat[:, BLOCK:] for stat in stats[1:]], [head[:, BLOCK:] for head in heads[1:]])
     own = own.reshape(HEADS, ROWS, HD)
-    o_ref[:, 0] = own
-    o_ref[:8, 1] = tail.reshape(8, ROWS, HD)
-    o_ref[8:, 1] = own[: HEADS - 8]
+    before = jnp.concatenate([tail.reshape(8, ROWS, HD), own[: HEADS - 8]])
+    for target, place in PAIR_ORDER:
+        o_ref[target : target + 2, 0] = own[place : place + 2]
+        o_ref[target : target + 2, 1] = before[place : place + 2]
 
 
 def merge(x, parts):

time: 140 us -> 138 us (0.986)
  the two profiles are of different devices: /device:TPU:3 before, /device:TPU:40 now
where the time goes in v6:
time: 138 us; the launch traced here: 137 us
  blocking collectives  64.5 us (47%)
  waiting for transfers between devices  27.3 us (20%)
  Pallas kernels  22.6 us (16%)
  starting transfers between devices  21.3 us (15%)
  between operations  1.41 us (1%)
    all_to_all x1, blocking collectives, local(): lax.all_to_all(packed, HEAD_AXES, split_axis=0, concat_axis=0, tiled=True)  49.8 us
    all_to_all x1, waiting for transfers between devices, local(): lax.all_to_all(attended, HEAD_AXES, split_axis=0, concat_axis=0, tiled=True)  26.3 us
    all_gather x1, blocking collectives, local(): q = lax.all_gather(q, 'x', axis=0, tiled=False)  14.7 us
    pallas_call x1, Pallas kernels, attend_far(): pl.pallas_call(far_kernel, out_shape=[result(LANES), result(BLOCK + QUART...  9.05 us
    all_to_all x1, starting transfers between devices, local(): lax.all_to_all(attended, HEAD_AXES, split_axis=0, concat_axis=0, tiled=True)  8.54 us
    pallas_call x1, Pallas kernels, attend_next(): pl.pallas_call(next_kernel, out_shape=[result(LANES), result(BLOCK - LANE...  5.19 us
    all_to_all x1, starting transfers between devices, local(): kv = lax.all_to_all(kv, 'y', split_axis=0, concat_axis=0, tiled=True)  5.04 us
    ppermute x3, starting transfers between devices, onward_in_x(): lax.ppermute(part, 'x', [(source, source + steps) for source in range(4 -...  4.92 us
  transfers between devices with their start and end apart: 6, of which 3 were waited for; matrix products, arithmetic and copies ran while one was open for 0% of the time, Pallas kernels for 13%

profile of v6, /device:TPU:40, one launch (start us, length us, event | category | flops | bytes accessed | tf_op | source)
XLA Modules:
  0.0 137.2 jit_solution(7596476394776047956)
XLA Ops:
  1.3 1.3 shard_map.104
  2.6 49.8 %all_to_all.15.packed_ref = bf16[32,3,24,128]{3,2,1,0:T(8,128)(2,1)S(1)} all-to-all(bf16[32,3,24,128]{3,2,1,0:T(8,128)(2,1)S(1)} %get-tuple-element.22), channel_id=1, replica_groups=mesh['x'=4,'zh'=4,'zl'=4,'y'=4,'c'=2] {'zl','zh','c'}, dimensions={0} | all-to-all | bytes 1179648 | tf_op jit(solution)/shard_map/all_to_all | solution.py:413
  52.3 1.4 %shard_map.105 = (bf16[32,24,128]{2,1,0:T(8,128)(2,1)S(1)}, bf16[4,32,2,24,128]{4,3,2,1,0:T(8,128)(2,1)}) custom-call(bf16[32,3,24,128]{3,2,1,0:T(8,128)(2,1)S(1)} %all_to_all.15.packed_ref), custom_call_target="tpu_custom_call" | custom-call | tf_op jit(solution)/shard_map/pallas_call | solution.py:74
  53.7 0.0 copy-start.3
  53.7 5.0 %all-to-all-start.1 = ((bf16[4,32,2,24,128]{4,3,2,1,0:T(8,128)(2,1)}), bf16[4,32,2,24,128]{4,3,2,1,0:T(8,128)(2,1)S(1)}, u32[]{:S(2)}, u32[]{:S(2)}) async-start(bf16[4,32,2,24,128]{4,3,2,1,0:T(8,128)(2,1)} %get-tuple-element.26), calls=%async_computation.1 | async-start | bytes 3145728 | tf_op jit(solution)/shard_map/all_to_all | solution.py:417
  58.8 0.0 copy-done.4
  58.8 0.1 dynamic_slice.7.count_ref
  58.9 0.0 copy-done.3
  58.9 0.1 pad_dynamic-slice_fusion.flag_ref
  58.9 2.8 %collective-permute-start = (bf16[1,24,4224]{2,1,0:T(8,128)(2,1)S(1)}, bf16[1,24,4224]{2,1,0:T(8,128)(2,1)S(1)}, u32[]{:S(2)}, u32[]{:S(2)}) collective-permute-start(bf16[1,24,4224]{2,1,0:T(8,128)(2,1)S(1)} %get-tuple-element.29), channel_id=1, source_target_pairs={{0,32},{32,64},{64,96},{96,128},{128,160},{160,192},{192,224},{224... | collective-permute-start | bytes 608264 | tf_op jit(solution)/shard_map/ppermute | solution.py:420
  61.8 14.7 %all-gather = bf16[128,24,128]{2,1,0:T(8,128)(2,1)S(1)} all-gather(bf16[32,24,128]{2,1,0:T(8,128)(2,1)S(1)} %get-tuple-element.25), channel_id=2, replica_groups=mesh['x'=4,'zh'=4,'zl'=4,'y'=4,'c'=2] {'x'}, dimensions={0}, use_global_device_ids=true | all-gather | bytes 983040 | tf_op jit(solution)/shard_map/all_gather | solution.py:416
  76.5 0.5 all-to-all-done.1
  77.0 9.1 %shard_map.106 = (bf16[136,256]{1,0:T(8,128)(2,1)S(1)}, bf16[136,960]{1,0:T(8,128)(2,1)S(1)}, bf16[136,960]{1,0:T(8,128)(2,1)S(1)}, bf16[4,768,128]{2,1,0:T(8,128)(2,1)S(1)}, bf16[4,144,768]{2,1,0:T(8,128)(2,1)S(1)}) custom-call(s32[4]{0:T(128)S(1)} %dynamic_slice.7.count_ref, s32[16,4]{1,0:T(8,128)S(1)} %pad_dynamic-slice_fusion.flag_ref, ...), custom_call_target="tpu_custom_call" | custom-call | flops 3019898880 | bytes 8388608 | tf_op jit(solution)/shard_map/pallas_call | solution.py:288
  86.1 0.0 collective-permute-done.latent_before_ref
  86.1 1.8 %collective-permute-start.1 = (bf16[136,960]{1,0:T(8,128)(2,1)S(1)}, bf16[136,960]{1,0:T(8,128)(2,1)S(1)}, u32[]{:S(2)}, u32[]{:S(2)}) collective-permute-start(bf16[136,960]{1,0:T(8,128)(2,1)S(1)} %get-tuple-element.30), channel_id=1, source_target_pairs={{0,256},{128,384},{1,257},{129,385},{2,258},{130,386},{3,259},{131... | collective-permute-start | bytes 783368 | tf_op jit(solution)/shard_map/ppermute | solution.py:429
  87.8 1.3 collective-permute-start.2
  89.1 5.2 %shard_map.107 = (bf16[136,256]{1,0:T(8,128)(2,1)S(1)}, bf16[136,512]{1,0:T(8,128)(2,1)S(1)}, bf16[136,960]{1,0:T(8,128)(2,1)S(1)}) custom-call(s32[16,4]{1,0:T(8,128)S(1)} %pad_dynamic-slice_fusion.flag_ref, s32[1]{0:T(128)} %bitcast.1.place_ref.x_ref, bf16[4,32,24,128]{3,2,1,0:T(8,128)(2,1)S(1)} %bitcast.6, ...), custom_call_target="tpu_custom_call" | custom-call | flops 1207959552 | bytes 8388608 | tf_op jit(solution)/shard_map/pallas_call | solution.py:306
  94.3 1.9 %collective-permute-start.3 = (bf16[136,960]{1,0:T(8,128)(2,1)S(1)}, bf16[136,960]{1,0:T(8,128)(2,1)S(1)}, u32[]{:S(2)}, u32[]{:S(2)}) collective-permute-start(bf16[136,960]{1,0:T(8,128)(2,1)S(1)} %get-tuple-element.38), channel_id=1, source_target_pairs={{0,128},{128,256},{256,384},{1,129},{129,257},{257,385},{2,130},{1... | collective-permute-start | bytes 783368 | tf_op jit(solution)/shard_map/ppermute | solution.py:429
  96.2 0.0 collective-permute-done.1.r2
  96.2 0.0 collective-permute-done.2.r3
  96.2 3.6 %shard_map.108.r0 = bf16[136,512]{1,0:T(8,128)(2,1)S(1)} custom-call(s32[16,4]{1,0:T(8,128)S(1)} %pad_dynamic-slice_fusion.flag_ref, s32[1]{0:T(128)} %bitcast.1.place_ref.x_ref, bf16[4,32,24,128]{3,2,1,0:T(8,128)(2,1)S(1)} %bitcast.7, bf16[4,768,128]{2,1,0:T(8,128)(2,1)S(1)} %get-tuple-element.33.k_ref, bf16[4,144,768]{2,1,0:T(8,128)(2,1)S(1)} %get-tuple-element.34.v_ref, ...), custom_call_target="tpu_custom_call" | custom-call | flops 1207959552 | bytes 8388608 | tf_op jit(solution)/shard_map/pallas_call | solution.py:318
  99.8 0.0 copy-start
  99.8 0.0 copy-start.1
  99.8 0.0 copy-start.2
  99.8 0.4 collective-permute-done.3.r1
  100.2 1.1 shard_map.109
  101.3 8.5 %all-to-all-start.2 = ((bf16[32,2,24,128]{3,2,1,0:T(8,128)(2,1)}), bf16[32,2,24,128]{3,2,1,0:T(8,128)(2,1)S(1)}, u32[]{:S(2)}, u32[]{:S(2)}) async-start(bf16[32,2,24,128]{3,2,1,0:T(8,128)(2,1)} %shard_map.109), calls=%async_computation.2 | async-start | bytes 786432 | tf_op jit(solution)/shard_map/all_to_all | solution.py:437
  109.9 26.3 %all-to-all-done.2.r_ref = bf16[32,2,24,128]{3,2,1,0:T(8,128)(2,1)S(1)} async-done(((bf16[32,2,24,128]{3,2,1,0:T(8,128)(2,1)}), bf16[32,2,24,128]{3,2,1,0:T(8,128)(2,1)S(1)}, u32[]{:S(2)}, u32[]{:S(2)}) %all-to-all-start.2) | async-done | bytes 393248 | tf_op jit(solution)/shard_map/all_to_all | solution.py:437
  136.2 0.0 copy-done
  136.2 0.0 copy-done.1
  136.2 0.0 copy-done.2
  136.2 1.0 shard_map.110
  (1 shorter events, 0.0 us)
Async XLA Ops:
  53.7 5.0 %copy-start.4 = (s32[16]{0:T(128)S(1)}, s32[16]{0:T(128)}, u32[]{:S(2)}) copy-start(s32[16]{0:T(128)} %param.15) | copy-start | bytes 196
  53.7 5.1 %copy-start.3 = (s32[16,16]{1,0:T(8,128)S(1)}, s32[16,16]{1,0:T(8,128)}, u32[]{:S(2)}) copy-start(s32[16,16]{1,0:T(8,128)} %param.16) | copy-start | bytes 3076
  53.7 23.3 %all-to-all-start.1 = ((bf16[4,32,2,24,128]{4,3,2,1,0:T(8,128)(2,1)}), bf16[4,32,2,24,128]{4,3,2,1,0:T(8,128)(2,1)S(1)}, u32[]{:S(2)}, u32[]{:S(2)}) async-start(bf16[4,32,2,24,128]{4,3,2,1,0:T(8,128)(2,1)} %get-tuple-element.26), calls=%async_computation.1 | async-start | bytes 3145728 | tf_op jit(solution)/shard_map/all_to_all | solution.py:417
  58.9 27.1 %collective-permute-start = (bf16[1,24,4224]{2,1,0:T(8,128)(2,1)S(1)}, bf16[1,24,4224]{2,1,0:T(8,128)(2,1)S(1)}, u32[]{:S(2)}, u32[]{:S(2)}) collective-permute-start(bf16[1,24,4224]{2,1,0:T(8,128)(2,1)S(1)} %get-tuple-element.29), channel_id=1, source_target_pairs={{0,32},{32,64},{64,96},{96,128},{128,160},{160,192},{192,224},{224... | collective-permute-start | bytes 608264 | tf_op jit(solution)/shard_map/ppermute | solution.py:420
  86.1 10.1 %collective-permute-start.1 = (bf16[136,960]{1,0:T(8,128)(2,1)S(1)}, bf16[136,960]{1,0:T(8,128)(2,1)S(1)}, u32[]{:S(2)}, u32[]{:S(2)}) collective-permute-start(bf16[136,960]{1,0:T(8,128)(2,1)S(1)} %get-tuple-element.30), channel_id=1, source_target_pairs={{0,256},{128,384},{1,257},{129,385},{2,258},{130,386},{3,259},{131... | collective-permute-start | bytes 783368 | tf_op jit(solution)/shard_map/ppermute | solution.py:429
  87.8 8.4 %collective-permute-start.2 = (bf16[136,960]{1,0:T(8,128)(2,1)S(1)}, bf16[136,960]{1,0:T(8,128)(2,1)S(1)}, u32[]{:S(2)}, u32[]{:S(2)}) collective-permute-start(bf16[136,960]{1,0:T(8,128)(2,1)S(1)} %get-tuple-element.31), channel_id=1, source_target_pairs={{0,384},{1,385},{2,386},{3,387},{4,388},{5,389},{6,390},{7,391},{8... | collective-permute-start | bytes 783368 | tf_op jit(solution)/shard_map/ppermute | solution.py:429
  94.3 5.9 %collective-permute-start.3 = (bf16[136,960]{1,0:T(8,128)(2,1)S(1)}, bf16[136,960]{1,0:T(8,128)(2,1)S(1)}, u32[]{:S(2)}, u32[]{:S(2)}) collective-permute-start(bf16[136,960]{1,0:T(8,128)(2,1)S(1)} %get-tuple-element.38), channel_id=1, source_target_pairs={{0,128},{128,256},{256,384},{1,129},{129,257},{257,385},{2,130},{1... | collective-permute-start | bytes 783368 | tf_op jit(solution)/shard_map/ppermute | solution.py:429
  99.8 36.4 %copy-start = (bf16[1,24,4096]{2,1,0:T(8,128)(2,1)S(1)}, bf16[1,24,4096]{2,1,0:T(8,128)(2,1)}, u32[]{:S(2)}) copy-start(bf16[1,24,4096]{2,1,0:T(8,128)(2,1)} %latent_ref.1) | copy-start | bytes 589828
  99.8 36.4 %copy-start.1 = (f32[16,4096]{1,0:T(8,128)S(1)}, f32[16,4096]{1,0:T(8,128)}, u32[]{:S(2)}) copy-start(f32[16,4096]{1,0:T(8,128)} %gate_ref.1) | copy-start | bytes 786436
  99.8 36.4 %copy-start.2 = (bf16[24,4096]{1,0:T(8,128)(2,1)S(1)}, bf16[24,4096]{1,0:T(8,128)(2,1)}, u32[]{:S(2)}) copy-start(bf16[24,4096]{1,0:T(8,128)(2,1)} %entering_ref.1) | copy-start | bytes 589828
  101.3 34.9 %all-to-all-start.2 = ((bf16[32,2,24,128]{3,2,1,0:T(8,128)(2,1)}), bf16[32,2,24,128]{3,2,1,0:T(8,128)(2,1)S(1)}, u32[]{:S(2)}, u32[]{:S(2)}) async-start(bf16[32,2,24,128]{3,2,1,0:T(8,128)(2,1)} %shard_map.109), calls=%async_computation.2 | async-start | bytes 786432 | tf_op jit(solution)/shard_map/all_to_all | solution.py:437

commit v7 on v6

--- a/solution.py
+++ b/solution.py
@@ -182,11 +182,11 @@
 
 
 def far_kernel(
-    count_ref, flag_ref, place_ref, kv_ref, q_ref, o1_last, o2, o3, k_ref, v_ref,
+    count_ref, flag_ref, kv_ref, q1_ref, q2_ref, q3_ref, o1_last, o2, o3, k_ref, v_ref,
     q_sc, m_sc, acc_sc, s0, s1, units,
 ):
-    for slot in range(1, 4):
-        q_sc[slot] = q_ref[jnp.minimum(place_ref[0] + slot, 3)].reshape(BLOCK, HD)
+    for slot, ref in ((1, q1_ref), (2, q2_ref), (3, q3_ref)):
+        q_sc[slot] = ref[...].reshape(BLOCK, HD)
 
     token = token_of((BLOCK, HD), 0)
     token_row = token_of((STAT, BLOCK), 1)
@@ -221,11 +221,11 @@
 
 
 def next_kernel(
-    flag_ref, place_ref, q_ref, k_ref, v_ref, o1_last, o0_last, o0_rest, o1,
+    flag_ref, place_ref, q0_ref, q1_ref, k_ref, v_ref, o1_last, o0_last, o0_rest, o1,
     q_sc, m_sc, acc_sc, s0, s1, units,
 ):
-    for slot in range(2):
-        q_sc[slot] = q_ref[jnp.minimum(place_ref[0] + slot, 3)].reshape(BLOCK, HD)
+    for slot, ref in ((0, q0_ref), (1, q1_ref)):
+        q_sc[slot] = ref[...].reshape(BLOCK, HD)
     clear(m_sc, acc_sc)
     refs = (flag_ref, q_sc, k_ref, v_ref, m_sc, acc_sc, s0, s1)
     run_units(units, (0, 1), *refs)(list_units(units, flag_ref, (1,), 2))
@@ -255,7 +255,7 @@
 
     @pl.when(place_ref[0] < 2)
     def _():
-        q_sc[0] = q_ref[place_ref[0]].reshape(BLOCK, HD)
+        q_sc[0] = q_ref[...].reshape(BLOCK, HD)
         clear(m_sc, acc_sc)
         attend_rest(o_ref, units, flag_ref, q_sc, k_ref, v_ref, m_sc, acc_sc, s0, s1)
 
@@ -284,7 +284,7 @@
     return jax.ShapeDtypeStruct((HD + SENT, columns), bf16)
 
 
-def attend_far(counts, flags, place, q, kv):
+def attend_far(counts, flags, kv, q1, q2, q3):
     return pl.pallas_call(
         far_kernel,
         out_shape=[
@@ -294,24 +294,24 @@
             jax.ShapeDtypeStruct((4, BLOCK, HD), bf16),
             jax.ShapeDtypeStruct((4, HD + STAT, BLOCK), bf16),
         ],
-        in_specs=[SM] * 3 + [VM] * 2,
+        in_specs=[SM] * 2 + [VM] * 4,
         out_specs=[VM] * 5,
         scratch_shapes=scratch(4),
         compiler_params=PARAMS,
         cost_estimate=cost(10),
-    )(counts, flags, place, kv, q)
-
-
-def attend_next(flags, place, q, k, v, last):
+    )(counts, flags, kv, q1, q2, q3)
+
+
+def attend_next(flags, place, q0, q1, k, v, last):
     return pl.pallas_call(
         next_kernel,
         out_shape=[result(LANES), result(BLOCK - LANES), result(BLOCK + QUARTER)],
-        in_specs=[SM] * 2 + [VM] * 4,
+        in_specs=[SM] * 2 + [VM] * 5,
         out_specs=[VM] * 3,
         scratch_shapes=scratch(2),
         compiler_params=PARAMS,
         cost_estimate=cost(4),
-    )(flags, place, q, k, v, last)
+    )(flags, place, q0, q1, k, v, last)
 
 
 def attend_own(flags, place, q, k, v, rest):
@@ -413,7 +413,10 @@
     packed = lax.all_to_all(packed, HEAD_AXES, split_axis=0, concat_axis=0, tiled=True)
     packed, latent_level = lax.optimization_barrier((packed, latent_level))
     q, kv = unpack(packed)
-    q = lax.all_gather(q, "x", axis=0, tiled=False)
+    q1, q2, q3 = (
+        lax.ppermute(q, "x", [(source, source - steps) for source in range(steps, 4)])
+        for steps in (1, 2, 3)
+    )
     kv = lax.all_to_all(kv, "y", split_axis=0, concat_axis=0, tiled=True)
     kv = kv.reshape(4, 4, 8, 2, ROWS, HD)
     onward = [(s, s + 1) for s in range(15)]
@@ -422,16 +425,17 @@
     flags = lax.dynamic_slice(padded, (4 * x, 4 * x), (16, 4))
     counts = lax.dynamic_slice(token_counts, (4 * x,), (4,))
     place = x.reshape(1)
-    last, part2, part3, k, v = attend_far(counts, flags, place, q, kv)
-    part2, part3, latent_before = lax.optimization_barrier((part2, part3, latent_before))
+    last, part2, part3, k, v = attend_far(counts, flags, kv, q1, q2, q3)
 
     def onward_in_x(part, steps):
         return lax.ppermute(part, "x", [(source, source + steps) for source in range(4 - steps)])
 
     received3, received2 = onward_in_x(part3, 3), onward_in_x(part2, 2)
-    own_last, own_rest, part1 = attend_next(flags, place, q, k, v, last)
+    own_last, own_rest, part1 = attend_next(flags, place, q, q1, k, v, last)
     received1 = onward_in_x(part1, 1)
-    q, received2, received3 = lax.optimization_barrier((q, received2, received3))
+    q, received2, received3, latent_before = lax.optimization_barrier(
+        (q, received2, received3, latent_before)
+    )
     own = attend_own(flags, place, q, k, v, own_rest)
     attended = merge(place, [own, own_last, received1, received2, received3])
     returned = lax.all_to_all(attended, HEAD_AXES, split_axis=0, concat_axis=0, tiled=True)

time: 138 us -> 138 us (level)
  the two profiles are of different devices: /device:TPU:40 before, /device:TPU:34 now
where the time goes in v7:
time: 138 us; the launch traced here: 137 us
  blocking collectives  49.8 us (36%)
  waiting for transfers between devices  40.6 us (29%)
  starting transfers between devices  25.1 us (18%)
  Pallas kernels  19.9 us (14%)
  between operations  1.46 us (1%)
    all_to_all x1, blocking collectives, local(): lax.all_to_all(packed, HEAD_AXES, split_axis=0, concat_axis=0, tiled=True)  49.8 us
    all_to_all x1, waiting for transfers between devices, local(): lax.all_to_all(attended, HEAD_AXES, split_axis=0, concat_axis=0, tiled=True)  26.3 us
    all_to_all x1, starting transfers between devices, local(): lax.all_to_all(attended, HEAD_AXES, split_axis=0, concat_axis=0, tiled=True)  7.44 us
    pallas_call x1, Pallas kernels, attend_far(): pl.pallas_call(far_kernel, out_shape=[result(LANES), result(BLOCK + QUART...  6.41 us
    all_to_all x1, waiting for transfers between devices, local(): kv = lax.all_to_all(kv, 'y', split_axis=0, concat_axis=0, tiled=True)  6.07 us
    ppermute x3, waiting for transfers between devices, local(): lax.ppermute(q, 'x', [(source, source - steps) for source in range(steps,...  5.56 us
    ppermute x3, starting transfers between devices, onward_in_x(): lax.ppermute(part, 'x', [(source, source + steps) for source in range(4 -...  5.26 us
    pallas_call x1, Pallas kernels, attend_next(): pl.pallas_call(next_kernel, out_shape=[result(LANES), result(BLOCK - LANE...  5.18 us
  transfers between devices with their start and end apart: 9, of which 5 were waited for; matrix products, arithmetic and copies ran while one was open for 0% of the time, Pallas kernels for 11%

profile of v7, /device:TPU:34, one launch (start us, length us, event | category | flops | bytes accessed | tf_op | source)
XLA Modules:
  0.0 137.1 jit_solution(8558531482259549662)
XLA Ops:
  1.3 1.3 shard_map.104
  2.6 49.8 %all_to_all.15.packed_ref = bf16[32,3,24,128]{3,2,1,0:T(8,128)(2,1)S(1)} all-to-all(bf16[32,3,24,128]{3,2,1,0:T(8,128)(2,1)S(1)} %get-tuple-element.20), channel_id=1, replica_groups=mesh['x'=4,'zh'=4,'zl'=4,'y'=4,'c'=2] {'zl','zh','c'}, dimensions={0} | all-to-all | bytes 1179648 | tf_op jit(solution)/shard_map/all_to_all | solution.py:413
  52.3 1.4 %shard_map.105 = (bf16[32,24,128]{2,1,0:T(8,128)(2,1)S(1)}, bf16[4,32,2,24,128]{4,3,2,1,0:T(8,128)(2,1)}) custom-call(bf16[32,3,24,128]{3,2,1,0:T(8,128)(2,1)S(1)} %all_to_all.15.packed_ref), custom_call_target="tpu_custom_call" | custom-call | tf_op jit(solution)/shard_map/pallas_call | solution.py:74
  53.7 4.6 %all-to-all-start.1 = ((bf16[4,32,2,24,128]{4,3,2,1,0:T(8,128)(2,1)}), bf16[4,32,2,24,128]{4,3,2,1,0:T(8,128)(2,1)S(1)}, u32[]{:S(2)}, u32[]{:S(2)}) async-start(bf16[4,32,2,24,128]{4,3,2,1,0:T(8,128)(2,1)} %get-tuple-element.24), calls=%async_computation.1 | async-start | bytes 3145728 | tf_op jit(solution)/shard_map/all_to_all | solution.py:420
  58.3 0.7 collective-permute-start.2
  59.0 1.3 collective-permute-start.1
  60.3 3.1 %collective-permute-start = (bf16[32,24,128]{2,1,0:T(8,128)(2,1)S(1)}, bf16[32,24,128]{2,1,0:T(8,128)(2,1)S(1)}, u32[]{:S(2)}, u32[]{:S(2)}) collective-permute-start(bf16[32,24,128]{2,1,0:T(8,128)(2,1)S(1)} %get-tuple-element.28.q0_ref.q_ref), channel_id=1, source_target_pairs={{128,0},{256,128},{384,256},{129,1},{257,129},{385,257},{130,2},{2... | collective-permute-start | bytes 589832 | tf_op jit(solution)/shard_map/ppermute | solution.py:417
  63.4 0.1 dynamic_slice.7.count_ref
  63.5 0.1 pad_dynamic-slice_fusion.flag_ref
  63.6 2.8 %collective-permute-start.5 = (bf16[1,24,4224]{2,1,0:T(8,128)(2,1)S(1)}, bf16[1,24,4224]{2,1,0:T(8,128)(2,1)S(1)}, u32[]{:S(2)}, u32[]{:S(2)}) collective-permute-start(bf16[1,24,4224]{2,1,0:T(8,128)(2,1)S(1)} %get-tuple-element.27), channel_id=1, source_target_pairs={{0,32},{32,64},{64,96},{96,128},{128,160},{160,192},{192,224},{224... | collective-permute-start | bytes 608264 | tf_op jit(solution)/shard_map/ppermute | solution.py:423
  66.4 0.0 collective-permute-done.2.q3_ref
  66.4 3.6 %collective-permute-done.1.q2_ref = bf16[32,24,128]{2,1,0:T(8,128)(2,1)S(1)} collective-permute-done((bf16[32,24,128]{2,1,0:T(8,128)(2,1)S(1)}, bf16[32,24,128]{2,1,0:T(8,128)(2,1)S(1)}, u32[]{:S(2)}, u32[]{:S(2)}) %collective-permute-start.1) | collective-permute-done | bytes 196640 | tf_op jit(solution)/shard_map/ppermute | solution.py:417
  70.0 2.0 %collective-permute-done.q1_ref = bf16[32,24,128]{2,1,0:T(8,128)(2,1)S(1)} collective-permute-done((bf16[32,24,128]{2,1,0:T(8,128)(2,1)S(1)}, bf16[32,24,128]{2,1,0:T(8,128)(2,1)S(1)}, u32[]{:S(2)}, u32[]{:S(2)}) %collective-permute-start) | collective-permute-done | bytes 196640 | tf_op jit(solution)/shard_map/ppermute | solution.py:417
  72.0 6.1 %all-to-all-done.1 = bf16[4,32,2,24,128]{4,3,2,1,0:T(8,128)(2,1)S(1)} async-done(((bf16[4,32,2,24,128]{4,3,2,1,0:T(8,128)(2,1)}), bf16[4,32,2,24,128]{4,3,2,1,0:T(8,128)(2,1)S(1)}, u32[]{:S(2)}, u32[]{:S(2)}) %all-to-all-start.1) | async-done | bytes 1572896 | tf_op jit(solution)/shard_map/all_to_all | solution.py:420
  78.0 6.4 %shard_map.106 = (bf16[136,256]{1,0:T(8,128)(2,1)S(1)}, bf16[136,960]{1,0:T(8,128)(2,1)S(1)}, bf16[136,960]{1,0:T(8,128)(2,1)S(1)}, bf16[4,768,128]{2,1,0:T(8,128)(2,1)S(1)}, bf16[4,144,768]{2,1,0:T(8,128)(2,1)S(1)}) custom-call(s32[4]{0:T(128)S(1)} %dynamic_slice.7.count_ref, s32[16,4]{1,0:T(8,128)S(1)} %pad_dynamic-slice_fusion.flag_ref, ...), custom_call_target="tpu_custom_call" | custom-call | flops 3019898880 | bytes 8388608 | tf_op jit(solution)/shard_map/pallas_call | solution.py:288
  84.4 1.3 collective-permute-start.3
  85.8 0.7 collective-permute-start.4
  86.4 5.2 %shard_map.107 = (bf16[136,256]{1,0:T(8,128)(2,1)S(1)}, bf16[136,512]{1,0:T(8,128)(2,1)S(1)}, bf16[136,960]{1,0:T(8,128)(2,1)S(1)}) custom-call(s32[16,4]{1,0:T(8,128)S(1)} %pad_dynamic-slice_fusion.flag_ref, s32[1]{0:T(128)} %bitcast.1.place_ref.x_ref, bf16[32,24,128]{2,1,0:T(8,128)(2,1)S(1)} %get-tuple-element.28.q0_ref.q_ref, ...), custom_call_target="tpu_custom_call" | custom-call | flops 1207959552 | bytes 8388608 | tf_op jit(solution)/shard_map/pallas_call | solution.py:306
  91.6 3.3 %collective-permute-start.6 = (bf16[136,960]{1,0:T(8,128)(2,1)S(1)}, bf16[136,960]{1,0:T(8,128)(2,1)S(1)}, u32[]{:S(2)}, u32[]{:S(2)}) collective-permute-start(bf16[136,960]{1,0:T(8,128)(2,1)S(1)} %get-tuple-element.34), channel_id=1, source_target_pairs={{0,128},{128,256},{256,384},{1,129},{129,257},{257,385},{2,130},{1... | collective-permute-start | bytes 783368 | tf_op jit(solution)/shard_map/ppermute | solution.py:431
  94.9 0.0 collective-permute-done.5.latent_before_ref
  94.9 0.0 collective-permute-done.3.r2
  94.9 0.0 collective-permute-done.4.r3
  94.9 3.5 %shard_map.108.r0 = bf16[136,512]{1,0:T(8,128)(2,1)S(1)} custom-call(s32[16,4]{1,0:T(8,128)S(1)} %pad_dynamic-slice_fusion.flag_ref, s32[1]{0:T(128)} %bitcast.1.place_ref.x_ref, bf16[32,24,128]{2,1,0:T(8,128)(2,1)S(1)} %get-tuple-element.28.q0_ref.q_ref, bf16[4,768,128]{2,1,0:T(8,128)(2,1)S(1)} %get-tuple-element.29.k_ref, ...), custom_call_target="tpu_custom_call" | custom-call | flops 1207959552 | bytes 8388608 | tf_op jit(solution)/shard_map/pallas_call | solution.py:318
  98.5 0.0 copy-start
  98.5 0.0 copy-start.1
  98.5 0.0 copy-start.2
  98.5 2.7 %collective-permute-done.6.r1 = bf16[136,960]{1,0:T(8,128)(2,1)S(1)} collective-permute-done((bf16[136,960]{1,0:T(8,128)(2,1)S(1)}, bf16[136,960]{1,0:T(8,128)(2,1)S(1)}, u32[]{:S(2)}, u32[]{:S(2)}) %collective-permute-start.6) | collective-permute-done | bytes 261152 | tf_op jit(solution)/shard_map/ppermute | solution.py:431
  101.2 1.1 shard_map.109
  102.3 7.4 %all-to-all-start.2 = ((bf16[32,2,24,128]{3,2,1,0:T(8,128)(2,1)}), bf16[32,2,24,128]{3,2,1,0:T(8,128)(2,1)S(1)}, u32[]{:S(2)}, u32[]{:S(2)}) async-start(bf16[32,2,24,128]{3,2,1,0:T(8,128)(2,1)} %shard_map.109), calls=%async_computation.2 | async-start | bytes 786432 | tf_op jit(solution)/shard_map/all_to_all | solution.py:441
  109.7 26.3 %all-to-all-done.2.r_ref = bf16[32,2,24,128]{3,2,1,0:T(8,128)(2,1)S(1)} async-done(((bf16[32,2,24,128]{3,2,1,0:T(8,128)(2,1)}), bf16[32,2,24,128]{3,2,1,0:T(8,128)(2,1)S(1)}, u32[]{:S(2)}, u32[]{:S(2)}) %all-to-all-start.2) | async-done | bytes 393248 | tf_op jit(solution)/shard_map/all_to_all | solution.py:441
  136.1 0.0 copy-done.2
  136.1 1.0 shard_map.110
  (6 shorter events, 0.0 us)
Async XLA Ops:
  53.7 9.6 %copy-start.4 = (s32[16]{0:T(128)S(1)}, s32[16]{0:T(128)}, u32[]{:S(2)}) copy-start(s32[16]{0:T(128)} %param.15) | copy-start | bytes 196
  53.7 9.7 %copy-start.3 = (s32[16,16]{1,0:T(8,128)S(1)}, s32[16,16]{1,0:T(8,128)}, u32[]{:S(2)}) copy-start(s32[16,16]{1,0:T(8,128)} %param.16) | copy-start | bytes 3076
  53.7 24.3 %all-to-all-start.1 = ((bf16[4,32,2,24,128]{4,3,2,1,0:T(8,128)(2,1)}), bf16[4,32,2,24,128]{4,3,2,1,0:T(8,128)(2,1)S(1)}, u32[]{:S(2)}, u32[]{:S(2)}) async-start(bf16[4,32,2,24,128]{4,3,2,1,0:T(8,128)(2,1)} %get-tuple-element.24), calls=%async_computation.1 | async-start | bytes 3145728 | tf_op jit(solution)/shard_map/all_to_all | solution.py:420
  58.3 8.1 %collective-permute-start.2 = (bf16[32,24,128]{2,1,0:T(8,128)(2,1)S(1)}, bf16[32,24,128]{2,1,0:T(8,128)(2,1)S(1)}, u32[]{:S(2)}, u32[]{:S(2)}) collective-permute-start(bf16[32,24,128]{2,1,0:T(8,128)(2,1)S(1)} %get-tuple-element.28.q0_ref.q_ref), channel_id=1, source_target_pairs={{384,0},{385,1},{386,2},{387,3},{388,4},{389,5},{390,6},{391,7},{3... | collective-permute-start | bytes 589832 | tf_op jit(solution)/shard_map/ppermute | solution.py:417
  59.0 11.0 %collective-permute-start.1 = (bf16[32,24,128]{2,1,0:T(8,128)(2,1)S(1)}, bf16[32,24,128]{2,1,0:T(8,128)(2,1)S(1)}, u32[]{:S(2)}, u32[]{:S(2)}) collective-permute-start(bf16[32,24,128]{2,1,0:T(8,128)(2,1)S(1)} %get-tuple-element.28.q0_ref.q_ref), channel_id=1, source_target_pairs={{256,0},{384,128},{257,1},{385,129},{258,2},{386,130},{259,3},{387... | collective-permute-start | bytes 589832 | tf_op jit(solution)/shard_map/ppermute | solution.py:417
  60.3 11.7 %collective-permute-start = (bf16[32,24,128]{2,1,0:T(8,128)(2,1)S(1)}, bf16[32,24,128]{2,1,0:T(8,128)(2,1)S(1)}, u32[]{:S(2)}, u32[]{:S(2)}) collective-permute-start(bf16[32,24,128]{2,1,0:T(8,128)(2,1)S(1)} %get-tuple-element.28.q0_ref.q_ref), channel_id=1, source_target_pairs={{128,0},{256,128},{384,256},{129,1},{257,129},{385,257},{130,2},{2... | collective-permute-start | bytes 589832 | tf_op jit(solution)/shard_map/ppermute | solution.py:417
  63.6 31.4 %collective-permute-start.5 = (bf16[1,24,4224]{2,1,0:T(8,128)(2,1)S(1)}, bf16[1,24,4224]{2,1,0:T(8,128)(2,1)S(1)}, u32[]{:S(2)}, u32[]{:S(2)}) collective-permute-start(bf16[1,24,4224]{2,1,0:T(8,128)(2,1)S(1)} %get-tuple-element.27), channel_id=1, source_target_pairs={{0,32},{32,64},{64,96},{96,128},{128,160},{160,192},{192,224},{224... | collective-permute-start | bytes 608264 | tf_op jit(solution)/shard_map/ppermute | solution.py:423
  84.4 10.5 %collective-permute-start.3 = (bf16[136,960]{1,0:T(8,128)(2,1)S(1)}, bf16[136,960]{1,0:T(8,128)(2,1)S(1)}, u32[]{:S(2)}, u32[]{:S(2)}) collective-permute-start(bf16[136,960]{1,0:T(8,128)(2,1)S(1)} %get-tuple-element.25), channel_id=1, source_target_pairs={{0,256},{128,384},{1,257},{129,385},{2,258},{130,386},{3,259},{131... | collective-permute-start | bytes 783368 | tf_op jit(solution)/shard_map/ppermute | solution.py:431
  85.8 9.2 %collective-permute-start.4 = (bf16[136,960]{1,0:T(8,128)(2,1)S(1)}, bf16[136,960]{1,0:T(8,128)(2,1)S(1)}, u32[]{:S(2)}, u32[]{:S(2)}) collective-permute-start(bf16[136,960]{1,0:T(8,128)(2,1)S(1)} %get-tuple-element.26), channel_id=1, source_target_pairs={{0,384},{1,385},{2,386},{3,387},{4,388},{5,389},{6,390},{7,391},{8... | collective-permute-start | bytes 783368 | tf_op jit(solution)/shard_map/ppermute | solution.py:431
  91.6 9.6 %collective-permute-start.6 = (bf16[136,960]{1,0:T(8,128)(2,1)S(1)}, bf16[136,960]{1,0:T(8,128)(2,1)S(1)}, u32[]{:S(2)}, u32[]{:S(2)}) collective-permute-start(bf16[136,960]{1,0:T(8,128)(2,1)S(1)} %get-tuple-element.34), channel_id=1, source_target_pairs={{0,128},{128,256},{256,384},{1,129},{129,257},{257,385},{2,130},{1... | collective-permute-start | bytes 783368 | tf_op jit(solution)/shard_map/ppermute | solution.py:431
  98.5 37.6 %copy-start = (bf16[1,24,4096]{2,1,0:T(8,128)(2,1)S(1)}, bf16[1,24,4096]{2,1,0:T(8,128)(2,1)}, u32[]{:S(2)}) copy-start(bf16[1,24,4096]{2,1,0:T(8,128)(2,1)} %latent_ref.1) | copy-start | bytes 589828
  98.5 37.6 %copy-start.1 = (f32[16,4096]{1,0:T(8,128)S(1)}, f32[16,4096]{1,0:T(8,128)}, u32[]{:S(2)}) copy-start(f32[16,4096]{1,0:T(8,128)} %gate_ref.1) | copy-start | bytes 786436
  98.5 37.6 %copy-start.2 = (bf16[24,4096]{1,0:T(8,128)(2,1)S(1)}, bf16[24,4096]{1,0:T(8,128)(2,1)}, u32[]{:S(2)}) copy-start(bf16[24,4096]{1,0:T(8,128)(2,1)} %entering_ref.1) | copy-start | bytes 589828
  102.3 33.8 %all-to-all-start.2 = ((bf16[32,2,24,128]{3,2,1,0:T(8,128)(2,1)}), bf16[32,2,24,128]{3,2,1,0:T(8,128)(2,1)S(1)}, u32[]{:S(2)}, u32[]{:S(2)}) async-start(bf16[32,2,24,128]{3,2,1,0:T(8,128)(2,1)} %shard_map.109), calls=%async_computation.2 | async-start | bytes 786432 | tf_op jit(solution)/shard_map/all_to_all | solution.py:441

commit v8 on v7

--- a/solution.py
+++ b/solution.py
@@ -419,6 +419,7 @@
     )
     kv = lax.all_to_all(kv, "y", split_axis=0, concat_axis=0, tiled=True)
     kv = kv.reshape(4, 4, 8, 2, ROWS, HD)
+    q1, latent_level = lax.optimization_barrier((q1, latent_level))
     onward = [(s, s + 1) for s in range(15)]
     latent_before = lax.ppermute(latent_level, ("x", "zh"), onward)
     padded = jnp.concatenate([block_mask, jnp.zeros_like(block_mask)], axis=0)

time: 138 us -> 138 us (level)
  no operation moved by 1% of the time
where the time goes in v8:
time: 138 us; the launch traced here: 137 us
  blocking collectives  49.8 us (36%)
  waiting for transfers between devices  40.9 us (30%)
  starting transfers between devices  24.9 us (18%)
  Pallas kernels  19.9 us (14%)
  between operations  1.46 us (1%)
    all_to_all x1, blocking collectives, local(): lax.all_to_all(packed, HEAD_AXES, split_axis=0, concat_axis=0, tiled=True)  49.8 us
    all_to_all x1, waiting for transfers between devices, local(): lax.all_to_all(attended, HEAD_AXES, split_axis=0, concat_axis=0, tiled=True)  26.3 us
    all_to_all x1, starting transfers between devices, local(): lax.all_to_all(attended, HEAD_AXES, split_axis=0, concat_axis=0, tiled=True)  7.44 us
    all_to_all x1, waiting for transfers between devices, local(): kv = lax.all_to_all(kv, 'y', split_axis=0, concat_axis=0, tiled=True)  7 us
    pallas_call x1, Pallas kernels, attend_far(): pl.pallas_call(far_kernel, out_shape=[result(LANES), result(BLOCK + QUART...  6.41 us
    ppermute x3, starting transfers between devices, onward_in_x(): lax.ppermute(part, 'x', [(source, source + steps) for source in range(4 -...  5.26 us
    pallas_call x1, Pallas kernels, attend_next(): pl.pallas_call(next_kernel, out_shape=[result(LANES), result(BLOCK - LANE...  5.18 us
    ppermute x3, waiting for transfers between devices, local(): lax.ppermute(q, 'x', [(source, source - steps) for source in range(steps,...  4.9 us
  transfers between devices with their start and end apart: 9, of which 5 were waited for; matrix products, arithmetic and copies ran while one was open for 0% of the time, Pallas kernels for 11%

profile of v8, /device:TPU:34, one launch (start us, length us, event | category | flops | bytes accessed | tf_op | source)
XLA Modules:
  0.0 137.1 jit_solution(17764941060287805134)
XLA Ops:
  1.3 1.3 shard_map.104
  2.6 49.8 %all_to_all.15.packed_ref = bf16[32,3,24,128]{3,2,1,0:T(8,128)(2,1)S(1)} all-to-all(bf16[32,3,24,128]{3,2,1,0:T(8,128)(2,1)S(1)} %get-tuple-element.22), channel_id=1, replica_groups=mesh['x'=4,'zh'=4,'zl'=4,'y'=4,'c'=2] {'zl','zh','c'}, dimensions={0} | all-to-all | bytes 1179648 | tf_op jit(solution)/shard_map/all_to_all | solution.py:413
  52.3 1.4 %shard_map.105 = (bf16[32,24,128]{2,1,0:T(8,128)(2,1)S(1)}, bf16[4,32,2,24,128]{4,3,2,1,0:T(8,128)(2,1)}) custom-call(bf16[32,3,24,128]{3,2,1,0:T(8,128)(2,1)S(1)} %all_to_all.15.packed_ref), custom_call_target="tpu_custom_call" | custom-call | tf_op jit(solution)/shard_map/pallas_call | solution.py:74
  53.7 4.6 %all-to-all-start.1 = ((bf16[4,32,2,24,128]{4,3,2,1,0:T(8,128)(2,1)}), bf16[4,32,2,24,128]{4,3,2,1,0:T(8,128)(2,1)S(1)}, u32[]{:S(2)}, u32[]{:S(2)}) async-start(bf16[4,32,2,24,128]{4,3,2,1,0:T(8,128)(2,1)} %get-tuple-element.26), calls=%async_computation.1 | async-start | bytes 3145728 | tf_op jit(solution)/shard_map/all_to_all | solution.py:420
  58.3 2.4 %collective-permute-start = (bf16[32,24,128]{2,1,0:T(8,128)(2,1)S(1)}, bf16[32,24,128]{2,1,0:T(8,128)(2,1)S(1)}, u32[]{:S(2)}, u32[]{:S(2)}) collective-permute-start(bf16[32,24,128]{2,1,0:T(8,128)(2,1)S(1)} %get-tuple-element.32.q0_ref.q_ref), channel_id=1, source_target_pairs={{128,0},{256,128},{384,256},{129,1},{257,129},{385,257},{130,2},{2... | collective-permute-start | bytes 589832 | tf_op jit(solution)/shard_map/ppermute | solution.py:417
  60.8 0.7 collective-permute-start.2
  61.5 1.3 collective-permute-start.1
  62.8 0.1 dynamic_slice.7.count_ref
  62.9 0.1 pad_dynamic-slice_fusion.flag_ref
  62.9 3.1 %collective-permute-done.q1_ref = bf16[32,24,128]{2,1,0:T(8,128)(2,1)S(1)} collective-permute-done((bf16[32,24,128]{2,1,0:T(8,128)(2,1)S(1)}, bf16[32,24,128]{2,1,0:T(8,128)(2,1)S(1)}, u32[]{:S(2)}, u32[]{:S(2)}) %collective-permute-start) | collective-permute-done | bytes 196640 | tf_op jit(solution)/shard_map/ppermute | solution.py:417
  66.1 3.2 %collective-permute-start.5 = (bf16[1,24,4224]{2,1,0:T(8,128)(2,1)S(1)}, bf16[1,24,4224]{2,1,0:T(8,128)(2,1)S(1)}, u32[]{:S(2)}, u32[]{:S(2)}) collective-permute-start(bf16[1,24,4224]{2,1,0:T(8,128)(2,1)S(1)} %get-tuple-element.31), channel_id=1, source_target_pairs={{0,32},{32,64},{64,96},{96,128},{128,160},{160,192},{192,224},{224... | collective-permute-start | bytes 608264 | tf_op jit(solution)/shard_map/ppermute | solution.py:424
  69.3 0.0 collective-permute-done.2.q3_ref
  69.3 1.8 %collective-permute-done.1.q2_ref = bf16[32,24,128]{2,1,0:T(8,128)(2,1)S(1)} collective-permute-done((bf16[32,24,128]{2,1,0:T(8,128)(2,1)S(1)}, bf16[32,24,128]{2,1,0:T(8,128)(2,1)S(1)}, u32[]{:S(2)}, u32[]{:S(2)}) %collective-permute-start.1) | collective-permute-done | bytes 196640 | tf_op jit(solution)/shard_map/ppermute | solution.py:417
  71.0 7.0 %all-to-all-done.1 = bf16[4,32,2,24,128]{4,3,2,1,0:T(8,128)(2,1)S(1)} async-done(((bf16[4,32,2,24,128]{4,3,2,1,0:T(8,128)(2,1)}), bf16[4,32,2,24,128]{4,3,2,1,0:T(8,128)(2,1)S(1)}, u32[]{:S(2)}, u32[]{:S(2)}) %all-to-all-start.1) | async-done | bytes 1572896 | tf_op jit(solution)/shard_map/all_to_all | solution.py:420
  78.0 6.4 %shard_map.106 = (bf16[136,256]{1,0:T(8,128)(2,1)S(1)}, bf16[136,960]{1,0:T(8,128)(2,1)S(1)}, bf16[136,960]{1,0:T(8,128)(2,1)S(1)}, bf16[4,768,128]{2,1,0:T(8,128)(2,1)S(1)}, bf16[4,144,768]{2,1,0:T(8,128)(2,1)S(1)}) custom-call(s32[4]{0:T(128)S(1)} %dynamic_slice.7.count_ref, s32[16,4]{1,0:T(8,128)S(1)} %pad_dynamic-slice_fusion.flag_ref, ...), custom_call_target="tpu_custom_call" | custom-call | flops 3019898880 | bytes 8388608 | tf_op jit(solution)/shard_map/pallas_call | solution.py:288
  84.4 1.3 collective-permute-start.3
  85.8 0.7 collective-permute-start.4
  86.4 5.2 %shard_map.107 = (bf16[136,256]{1,0:T(8,128)(2,1)S(1)}, bf16[136,512]{1,0:T(8,128)(2,1)S(1)}, bf16[136,960]{1,0:T(8,128)(2,1)S(1)}) custom-call(s32[16,4]{1,0:T(8,128)S(1)} %pad_dynamic-slice_fusion.flag_ref, s32[1]{0:T(128)} %bitcast.1.place_ref.x_ref, bf16[32,24,128]{2,1,0:T(8,128)(2,1)S(1)} %get-tuple-element.32.q0_ref.q_ref, ...), custom_call_target="tpu_custom_call" | custom-call | flops 1207959552 | bytes 8388608 | tf_op jit(solution)/shard_map/pallas_call | solution.py:306
  91.6 3.3 %collective-permute-start.6 = (bf16[136,960]{1,0:T(8,128)(2,1)S(1)}, bf16[136,960]{1,0:T(8,128)(2,1)S(1)}, u32[]{:S(2)}, u32[]{:S(2)}) collective-permute-start(bf16[136,960]{1,0:T(8,128)(2,1)S(1)} %get-tuple-element.38), channel_id=1, source_target_pairs={{0,128},{128,256},{256,384},{1,129},{129,257},{257,385},{2,130},{1... | collective-permute-start | bytes 783368 | tf_op jit(solution)/shard_map/ppermute | solution.py:432
  94.9 0.0 collective-permute-done.5.latent_before_ref
  94.9 0.0 collective-permute-done.3.r2
  94.9 0.0 collective-permute-done.4.r3
  94.9 3.5 %shard_map.108.r0 = bf16[136,512]{1,0:T(8,128)(2,1)S(1)} custom-call(s32[16,4]{1,0:T(8,128)S(1)} %pad_dynamic-slice_fusion.flag_ref, s32[1]{0:T(128)} %bitcast.1.place_ref.x_ref, bf16[32,24,128]{2,1,0:T(8,128)(2,1)S(1)} %get-tuple-element.32.q0_ref.q_ref, bf16[4,768,128]{2,1,0:T(8,128)(2,1)S(1)} %get-tuple-element.33.k_ref, ...), custom_call_target="tpu_custom_call" | custom-call | flops 1207959552 | bytes 8388608 | tf_op jit(solution)/shard_map/pallas_call | solution.py:318
  98.5 0.0 copy-start
  98.5 0.0 copy-start.1
  98.5 0.0 copy-start.2
  98.5 2.7 %collective-permute-done.6.r1 = bf16[136,960]{1,0:T(8,128)(2,1)S(1)} collective-permute-done((bf16[136,960]{1,0:T(8,128)(2,1)S(1)}, bf16[136,960]{1,0:T(8,128)(2,1)S(1)}, u32[]{:S(2)}, u32[]{:S(2)}) %collective-permute-start.6) | collective-permute-done | bytes 261152 | tf_op jit(solution)/shard_map/ppermute | solution.py:432
  101.2 1.1 shard_map.109
  102.3 7.4 %all-to-all-start.2 = ((bf16[32,2,24,128]{3,2,1,0:T(8,128)(2,1)}), bf16[32,2,24,128]{3,2,1,0:T(8,128)(2,1)S(1)}, u32[]{:S(2)}, u32[]{:S(2)}) async-start(bf16[32,2,24,128]{3,2,1,0:T(8,128)(2,1)} %shard_map.109), calls=%async_computation.2 | async-start | bytes 786432 | tf_op jit(solution)/shard_map/all_to_all | solution.py:442
  109.7 26.3 %all-to-all-done.2.r_ref = bf16[32,2,24,128]{3,2,1,0:T(8,128)(2,1)S(1)} async-done(((bf16[32,2,24,128]{3,2,1,0:T(8,128)(2,1)}), bf16[32,2,24,128]{3,2,1,0:T(8,128)(2,1)S(1)}, u32[]{:S(2)}, u32[]{:S(2)}) %all-to-all-start.2) | async-done | bytes 393248 | tf_op jit(solution)/shard_map/all_to_all | solution.py:442
  136.1 0.0 copy-done.2
  136.1 1.0 shard_map.110
  (6 shorter events, 0.0 us)
Async XLA Ops:
  53.7 9.0 %copy-start.4 = (s32[16]{0:T(128)S(1)}, s32[16]{0:T(128)}, u32[]{:S(2)}) copy-start(s32[16]{0:T(128)} %param.15) | copy-start | bytes 196
  53.7 9.1 %copy-start.3 = (s32[16,16]{1,0:T(8,128)S(1)}, s32[16,16]{1,0:T(8,128)}, u32[]{:S(2)}) copy-start(s32[16,16]{1,0:T(8,128)} %param.16) | copy-start | bytes 3076
  53.7 24.3 %all-to-all-start.1 = ((bf16[4,32,2,24,128]{4,3,2,1,0:T(8,128)(2,1)}), bf16[4,32,2,24,128]{4,3,2,1,0:T(8,128)(2,1)S(1)}, u32[]{:S(2)}, u32[]{:S(2)}) async-start(bf16[4,32,2,24,128]{4,3,2,1,0:T(8,128)(2,1)} %get-tuple-element.26), calls=%async_computation.1 | async-start | bytes 3145728 | tf_op jit(solution)/shard_map/all_to_all | solution.py:420
  58.3 7.7 %collective-permute-start = (bf16[32,24,128]{2,1,0:T(8,128)(2,1)S(1)}, bf16[32,24,128]{2,1,0:T(8,128)(2,1)S(1)}, u32[]{:S(2)}, u32[]{:S(2)}) collective-permute-start(bf16[32,24,128]{2,1,0:T(8,128)(2,1)S(1)} %get-tuple-element.32.q0_ref.q_ref), channel_id=1, source_target_pairs={{128,0},{256,128},{384,256},{129,1},{257,129},{385,257},{130,2},{2... | collective-permute-start | bytes 589832 | tf_op jit(solution)/shard_map/ppermute | solution.py:417
  60.8 8.5 %collective-permute-start.2 = (bf16[32,24,128]{2,1,0:T(8,128)(2,1)S(1)}, bf16[32,24,128]{2,1,0:T(8,128)(2,1)S(1)}, u32[]{:S(2)}, u32[]{:S(2)}) collective-permute-start(bf16[32,24,128]{2,1,0:T(8,128)(2,1)S(1)} %get-tuple-element.32.q0_ref.q_ref), channel_id=1, source_target_pairs={{384,0},{385,1},{386,2},{387,3},{388,4},{389,5},{390,6},{391,7},{3... | collective-permute-start | bytes 589832 | tf_op jit(solution)/shard_map/ppermute | solution.py:417
  61.5 9.6 %collective-permute-start.1 = (bf16[32,24,128]{2,1,0:T(8,128)(2,1)S(1)}, bf16[32,24,128]{2,1,0:T(8,128)(2,1)S(1)}, u32[]{:S(2)}, u32[]{:S(2)}) collective-permute-start(bf16[32,24,128]{2,1,0:T(8,128)(2,1)S(1)} %get-tuple-element.32.q0_ref.q_ref), channel_id=1, source_target_pairs={{256,0},{384,128},{257,1},{385,129},{258,2},{386,130},{259,3},{387... | collective-permute-start | bytes 589832 | tf_op jit(solution)/shard_map/ppermute | solution.py:417
  66.1 28.8 %collective-permute-start.5 = (bf16[1,24,4224]{2,1,0:T(8,128)(2,1)S(1)}, bf16[1,24,4224]{2,1,0:T(8,128)(2,1)S(1)}, u32[]{:S(2)}, u32[]{:S(2)}) collective-permute-start(bf16[1,24,4224]{2,1,0:T(8,128)(2,1)S(1)} %get-tuple-element.31), channel_id=1, source_target_pairs={{0,32},{32,64},{64,96},{96,128},{128,160},{160,192},{192,224},{224... | collective-permute-start | bytes 608264 | tf_op jit(solution)/shard_map/ppermute | solution.py:424
  84.4 10.5 %collective-permute-start.3 = (bf16[136,960]{1,0:T(8,128)(2,1)S(1)}, bf16[136,960]{1,0:T(8,128)(2,1)S(1)}, u32[]{:S(2)}, u32[]{:S(2)}) collective-permute-start(bf16[136,960]{1,0:T(8,128)(2,1)S(1)} %get-tuple-element.29), channel_id=1, source_target_pairs={{0,256},{128,384},{1,257},{129,385},{2,258},{130,386},{3,259},{131... | collective-permute-start | bytes 783368 | tf_op jit(solution)/shard_map/ppermute | solution.py:432
  85.8 9.2 %collective-permute-start.4 = (bf16[136,960]{1,0:T(8,128)(2,1)S(1)}, bf16[136,960]{1,0:T(8,128)(2,1)S(1)}, u32[]{:S(2)}, u32[]{:S(2)}) collective-permute-start(bf16[136,960]{1,0:T(8,128)(2,1)S(1)} %get-tuple-element.30), channel_id=1, source_target_pairs={{0,384},{1,385},{2,386},{3,387},{4,388},{5,389},{6,390},{7,391},{8... | collective-permute-start | bytes 783368 | tf_op jit(solution)/shard_map/ppermute | solution.py:432
  91.6 9.6 %collective-permute-start.6 = (bf16[136,960]{1,0:T(8,128)(2,1)S(1)}, bf16[136,960]{1,0:T(8,128)(2,1)S(1)}, u32[]{:S(2)}, u32[]{:S(2)}) collective-permute-start(bf16[136,960]{1,0:T(8,128)(2,1)S(1)} %get-tuple-element.38), channel_id=1, source_target_pairs={{0,128},{128,256},{256,384},{1,129},{129,257},{257,385},{2,130},{1... | collective-permute-start | bytes 783368 | tf_op jit(solution)/shard_map/ppermute | solution.py:432
  98.5 37.6 %copy-start = (bf16[1,24,4096]{2,1,0:T(8,128)(2,1)S(1)}, bf16[1,24,4096]{2,1,0:T(8,128)(2,1)}, u32[]{:S(2)}) copy-start(bf16[1,24,4096]{2,1,0:T(8,128)(2,1)} %latent_ref.1) | copy-start | bytes 589828
  98.5 37.6 %copy-start.1 = (f32[16,4096]{1,0:T(8,128)S(1)}, f32[16,4096]{1,0:T(8,128)}, u32[]{:S(2)}) copy-start(f32[16,4096]{1,0:T(8,128)} %gate_ref.1) | copy-start | bytes 786436
  98.5 37.6 %copy-start.2 = (bf16[24,4096]{1,0:T(8,128)(2,1)S(1)}, bf16[24,4096]{1,0:T(8,128)(2,1)}, u32[]{:S(2)}) copy-start(bf16[24,4096]{1,0:T(8,128)(2,1)} %entering_ref.1) | copy-start | bytes 589828
  102.3 33.8 %all-to-all-start.2 = ((bf16[32,2,24,128]{3,2,1,0:T(8,128)(2,1)}), bf16[32,2,24,128]{3,2,1,0:T(8,128)(2,1)S(1)}, u32[]{:S(2)}, u32[]{:S(2)}) async-start(bf16[32,2,24,128]{3,2,1,0:T(8,128)(2,1)} %shard_map.109), calls=%async_computation.2 | async-start | bytes 786432 | tf_op jit(solution)/shard_map/all_to_all | solution.py:442

commit v9 on v8

--- a/solution.py
+++ b/solution.py
@@ -434,8 +434,8 @@
     received3, received2 = onward_in_x(part3, 3), onward_in_x(part2, 2)
     own_last, own_rest, part1 = attend_next(flags, place, q, q1, k, v, last)
     received1 = onward_in_x(part1, 1)
-    q, received2, received3, latent_before = lax.optimization_barrier(
-        (q, received2, received3, latent_before)
+    q, received2, latent_before = lax.optimization_barrier(
+        (q, received2, latent_before)
     )
     own = attend_own(flags, place, q, k, v, own_rest)
     attended = merge(place, [own, own_last, received1, received2, received3])

time: 138 us -> 138 us (level)
  no operation moved by 1% of the time
where the time goes in v9:
time: 138 us; the launch traced here: 137 us
  blocking collectives  49.8 us (36%)
  waiting for transfers between devices  40.9 us (30%)
  starting transfers between devices  24.9 us (18%)
  Pallas kernels  19.9 us (14%)
  between operations  1.46 us (1%)
    all_to_all x1, blocking collectives, local(): lax.all_to_all(packed, HEAD_AXES, split_axis=0, concat_axis=0, tiled=True)  49.8 us
    all_to_all x1, waiting for transfers between devices, local(): lax.all_to_all(attended, HEAD_AXES, split_axis=0, concat_axis=0, tiled=True)  26.3 us
    all_to_all x1, starting transfers between devices, local(): lax.all_to_all(attended, HEAD_AXES, split_axis=0, concat_axis=0, tiled=True)  7.44 us
    all_to_all x1, waiting for transfers between devices, local(): kv = lax.all_to_all(kv, 'y', split_axis=0, concat_axis=0, tiled=True)  7 us
    pallas_call x1, Pallas kernels, attend_far(): pl.pallas_call(far_kernel, out_shape=[result(LANES), result(BLOCK + QUART...  6.41 us
    ppermute x3, starting transfers between devices, onward_in_x(): lax.ppermute(part, 'x', [(source, source + steps) for source in range(4 -...  5.26 us
    pallas_call x1, Pallas kernels, attend_next(): pl.pallas_call(next_kernel, out_shape=[result(LANES), result(BLOCK - LANE...  5.18 us
    ppermute x3, waiting for transfers between devices, local(): lax.ppermute(q, 'x', [(source, source - steps) for source in range(steps,...  4.9 us
  transfers between devices with their start and end apart: 9, of which 5 were waited for; matrix products, arithmetic and copies ran while one was open for 0% of the time, Pallas kernels for 11%

profile of v9, /device:TPU:34, one launch (start us, length us, event | category | flops | bytes accessed | tf_op | source)
XLA Modules:
  0.0 137.1 jit_solution(13335970649094317602)
XLA Ops:
  1.3 1.3 shard_map.104
  2.6 49.8 %all_to_all.15.packed_ref = bf16[32,3,24,128]{3,2,1,0:T(8,128)(2,1)S(1)} all-to-all(bf16[32,3,24,128]{3,2,1,0:T(8,128)(2,1)S(1)} %get-tuple-element.21), channel_id=1, replica_groups=mesh['x'=4,'zh'=4,'zl'=4,'y'=4,'c'=2] {'zl','zh','c'}, dimensions={0} | all-to-all | bytes 1179648 | tf_op jit(solution)/shard_map/all_to_all | solution.py:413
  52.3 1.4 %shard_map.105 = (bf16[32,24,128]{2,1,0:T(8,128)(2,1)S(1)}, bf16[4,32,2,24,128]{4,3,2,1,0:T(8,128)(2,1)}) custom-call(bf16[32,3,24,128]{3,2,1,0:T(8,128)(2,1)S(1)} %all_to_all.15.packed_ref), custom_call_target="tpu_custom_call" | custom-call | tf_op jit(solution)/shard_map/pallas_call | solution.py:74
  53.7 4.6 %all-to-all-start.1 = ((bf16[4,32,2,24,128]{4,3,2,1,0:T(8,128)(2,1)}), bf16[4,32,2,24,128]{4,3,2,1,0:T(8,128)(2,1)S(1)}, u32[]{:S(2)}, u32[]{:S(2)}) async-start(bf16[4,32,2,24,128]{4,3,2,1,0:T(8,128)(2,1)} %get-tuple-element.25), calls=%async_computation.1 | async-start | bytes 3145728 | tf_op jit(solution)/shard_map/all_to_all | solution.py:420
  58.3 2.4 %collective-permute-start = (bf16[32,24,128]{2,1,0:T(8,128)(2,1)S(1)}, bf16[32,24,128]{2,1,0:T(8,128)(2,1)S(1)}, u32[]{:S(2)}, u32[]{:S(2)}) collective-permute-start(bf16[32,24,128]{2,1,0:T(8,128)(2,1)S(1)} %get-tuple-element.30.q0_ref.q_ref), channel_id=1, source_target_pairs={{128,0},{256,128},{384,256},{129,1},{257,129},{385,257},{130,2},{2... | collective-permute-start | bytes 589832 | tf_op jit(solution)/shard_map/ppermute | solution.py:417
  60.8 0.7 collective-permute-start.2
  61.5 1.3 collective-permute-start.1
  62.8 0.1 dynamic_slice.7.count_ref
  62.9 0.1 pad_dynamic-slice_fusion.flag_ref
  62.9 3.1 %collective-permute-done.q1_ref = bf16[32,24,128]{2,1,0:T(8,128)(2,1)S(1)} collective-permute-done((bf16[32,24,128]{2,1,0:T(8,128)(2,1)S(1)}, bf16[32,24,128]{2,1,0:T(8,128)(2,1)S(1)}, u32[]{:S(2)}, u32[]{:S(2)}) %collective-permute-start) | collective-permute-done | bytes 196640 | tf_op jit(solution)/shard_map/ppermute | solution.py:417
  66.1 3.2 %collective-permute-start.4 = (bf16[1,24,4224]{2,1,0:T(8,128)(2,1)S(1)}, bf16[1,24,4224]{2,1,0:T(8,128)(2,1)S(1)}, u32[]{:S(2)}, u32[]{:S(2)}) collective-permute-start(bf16[1,24,4224]{2,1,0:T(8,128)(2,1)S(1)} %get-tuple-element.29), channel_id=1, source_target_pairs={{0,32},{32,64},{64,96},{96,128},{128,160},{160,192},{192,224},{224... | collective-permute-start | bytes 608264 | tf_op jit(solution)/shard_map/ppermute | solution.py:424
  69.3 0.0 collective-permute-done.2.q3_ref
  69.3 1.8 %collective-permute-done.1.q2_ref = bf16[32,24,128]{2,1,0:T(8,128)(2,1)S(1)} collective-permute-done((bf16[32,24,128]{2,1,0:T(8,128)(2,1)S(1)}, bf16[32,24,128]{2,1,0:T(8,128)(2,1)S(1)}, u32[]{:S(2)}, u32[]{:S(2)}) %collective-permute-start.1) | collective-permute-done | bytes 196640 | tf_op jit(solution)/shard_map/ppermute | solution.py:417
  71.0 7.0 %all-to-all-done.1 = bf16[4,32,2,24,128]{4,3,2,1,0:T(8,128)(2,1)S(1)} async-done(((bf16[4,32,2,24,128]{4,3,2,1,0:T(8,128)(2,1)}), bf16[4,32,2,24,128]{4,3,2,1,0:T(8,128)(2,1)S(1)}, u32[]{:S(2)}, u32[]{:S(2)}) %all-to-all-start.1) | async-done | bytes 1572896 | tf_op jit(solution)/shard_map/all_to_all | solution.py:420
  78.0 6.4 %shard_map.106 = (bf16[136,256]{1,0:T(8,128)(2,1)S(1)}, bf16[136,960]{1,0:T(8,128)(2,1)S(1)}, bf16[136,960]{1,0:T(8,128)(2,1)S(1)}, bf16[4,768,128]{2,1,0:T(8,128)(2,1)S(1)}, bf16[4,144,768]{2,1,0:T(8,128)(2,1)S(1)}) custom-call(s32[4]{0:T(128)S(1)} %dynamic_slice.7.count_ref, s32[16,4]{1,0:T(8,128)S(1)} %pad_dynamic-slice_fusion.flag_ref, ...), custom_call_target="tpu_custom_call" | custom-call | flops 3019898880 | bytes 8388608 | tf_op jit(solution)/shard_map/pallas_call | solution.py:288
  84.4 1.3 collective-permute-start.3
  85.8 0.7 collective-permute-start.6
  86.4 5.2 %shard_map.107 = (bf16[136,256]{1,0:T(8,128)(2,1)S(1)}, bf16[136,512]{1,0:T(8,128)(2,1)S(1)}, bf16[136,960]{1,0:T(8,128)(2,1)S(1)}) custom-call(s32[16,4]{1,0:T(8,128)S(1)} %pad_dynamic-slice_fusion.flag_ref, s32[1]{0:T(128)} %bitcast.1.place_ref.x_ref, bf16[32,24,128]{2,1,0:T(8,128)(2,1)S(1)} %get-tuple-element.30.q0_ref.q_ref, ...), custom_call_target="tpu_custom_call" | custom-call | flops 1207959552 | bytes 8388608 | tf_op jit(solution)/shard_map/pallas_call | solution.py:306
  91.6 3.3 %collective-permute-start.5 = (bf16[136,960]{1,0:T(8,128)(2,1)S(1)}, bf16[136,960]{1,0:T(8,128)(2,1)S(1)}, u32[]{:S(2)}, u32[]{:S(2)}) collective-permute-start(bf16[136,960]{1,0:T(8,128)(2,1)S(1)} %get-tuple-element.36), channel_id=1, source_target_pairs={{0,128},{128,256},{256,384},{1,129},{129,257},{257,385},{2,130},{1... | collective-permute-start | bytes 783368 | tf_op jit(solution)/shard_map/ppermute | solution.py:432
  94.9 0.0 collective-permute-done.4.latent_before_ref
  94.9 0.0 collective-permute-done.3.r2
  94.9 3.6 %shard_map.108.r0 = bf16[136,512]{1,0:T(8,128)(2,1)S(1)} custom-call(s32[16,4]{1,0:T(8,128)S(1)} %pad_dynamic-slice_fusion.flag_ref, s32[1]{0:T(128)} %bitcast.1.place_ref.x_ref, bf16[32,24,128]{2,1,0:T(8,128)(2,1)S(1)} %get-tuple-element.30.q0_ref.q_ref, bf16[4,768,128]{2,1,0:T(8,128)(2,1)S(1)} %get-tuple-element.31.k_ref, ...), custom_call_target="tpu_custom_call" | custom-call | flops 1207959552 | bytes 8388608 | tf_op jit(solution)/shard_map/pallas_call | solution.py:318
  98.5 0.0 copy-start
  98.5 0.0 copy-start.1
  98.5 0.0 copy-start.2
  98.5 0.0 collective-permute-done.6.r3
  98.5 2.7 %collective-permute-done.5.r1 = bf16[136,960]{1,0:T(8,128)(2,1)S(1)} collective-permute-done((bf16[136,960]{1,0:T(8,128)(2,1)S(1)}, bf16[136,960]{1,0:T(8,128)(2,1)S(1)}, u32[]{:S(2)}, u32[]{:S(2)}) %collective-permute-start.5) | collective-permute-done | bytes 261152 | tf_op jit(solution)/shard_map/ppermute | solution.py:432
  101.2 1.1 shard_map.109
  102.3 7.4 %all-to-all-start.2 = ((bf16[32,2,24,128]{3,2,1,0:T(8,128)(2,1)}), bf16[32,2,24,128]{3,2,1,0:T(8,128)(2,1)S(1)}, u32[]{:S(2)}, u32[]{:S(2)}) async-start(bf16[32,2,24,128]{3,2,1,0:T(8,128)(2,1)} %shard_map.109), calls=%async_computation.2 | async-start | bytes 786432 | tf_op jit(solution)/shard_map/all_to_all | solution.py:442
  109.7 26.3 %all-to-all-done.2.r_ref = bf16[32,2,24,128]{3,2,1,0:T(8,128)(2,1)S(1)} async-done(((bf16[32,2,24,128]{3,2,1,0:T(8,128)(2,1)}), bf16[32,2,24,128]{3,2,1,0:T(8,128)(2,1)S(1)}, u32[]{:S(2)}, u32[]{:S(2)}) %all-to-all-start.2) | async-done | bytes 393248 | tf_op jit(solution)/shard_map/all_to_all | solution.py:442
  136.1 0.0 copy-done.2
  136.1 1.0 shard_map.110
  (6 shorter events, 0.0 us)
Async XLA Ops:
  53.7 9.0 %copy-start.4 = (s32[16]{0:T(128)S(1)}, s32[16]{0:T(128)}, u32[]{:S(2)}) copy-start(s32[16]{0:T(128)} %param.15) | copy-start | bytes 196
  53.7 9.1 %copy-start.3 = (s32[16,16]{1,0:T(8,128)S(1)}, s32[16,16]{1,0:T(8,128)}, u32[]{:S(2)}) copy-start(s32[16,16]{1,0:T(8,128)} %param.16) | copy-start | bytes 3076
  53.7 24.3 %all-to-all-start.1 = ((bf16[4,32,2,24,128]{4,3,2,1,0:T(8,128)(2,1)}), bf16[4,32,2,24,128]{4,3,2,1,0:T(8,128)(2,1)S(1)}, u32[]{:S(2)}, u32[]{:S(2)}) async-start(bf16[4,32,2,24,128]{4,3,2,1,0:T(8,128)(2,1)} %get-tuple-element.25), calls=%async_computation.1 | async-start | bytes 3145728 | tf_op jit(solution)/shard_map/all_to_all | solution.py:420
  58.3 7.7 %collective-permute-start = (bf16[32,24,128]{2,1,0:T(8,128)(2,1)S(1)}, bf16[32,24,128]{2,1,0:T(8,128)(2,1)S(1)}, u32[]{:S(2)}, u32[]{:S(2)}) collective-permute-start(bf16[32,24,128]{2,1,0:T(8,128)(2,1)S(1)} %get-tuple-element.30.q0_ref.q_ref), channel_id=1, source_target_pairs={{128,0},{256,128},{384,256},{129,1},{257,129},{385,257},{130,2},{2... | collective-permute-start | bytes 589832 | tf_op jit(solution)/shard_map/ppermute | solution.py:417
  60.8 8.5 %collective-permute-start.2 = (bf16[32,24,128]{2,1,0:T(8,128)(2,1)S(1)}, bf16[32,24,128]{2,1,0:T(8,128)(2,1)S(1)}, u32[]{:S(2)}, u32[]{:S(2)}) collective-permute-start(bf16[32,24,128]{2,1,0:T(8,128)(2,1)S(1)} %get-tuple-element.30.q0_ref.q_ref), channel_id=1, source_target_pairs={{384,0},{385,1},{386,2},{387,3},{388,4},{389,5},{390,6},{391,7},{3... | collective-permute-start | bytes 589832 | tf_op jit(solution)/shard_map/ppermute | solution.py:417
  61.5 9.6 %collective-permute-start.1 = (bf16[32,24,128]{2,1,0:T(8,128)(2,1)S(1)}, bf16[32,24,128]{2,1,0:T(8,128)(2,1)S(1)}, u32[]{:S(2)}, u32[]{:S(2)}) collective-permute-start(bf16[32,24,128]{2,1,0:T(8,128)(2,1)S(1)} %get-tuple-element.30.q0_ref.q_ref), channel_id=1, source_target_pairs={{256,0},{384,128},{257,1},{385,129},{258,2},{386,130},{259,3},{387... | collective-permute-start | bytes 589832 | tf_op jit(solution)/shard_map/ppermute | solution.py:417
  66.1 28.8 %collective-permute-start.4 = (bf16[1,24,4224]{2,1,0:T(8,128)(2,1)S(1)}, bf16[1,24,4224]{2,1,0:T(8,128)(2,1)S(1)}, u32[]{:S(2)}, u32[]{:S(2)}) collective-permute-start(bf16[1,24,4224]{2,1,0:T(8,128)(2,1)S(1)} %get-tuple-element.29), channel_id=1, source_target_pairs={{0,32},{32,64},{64,96},{96,128},{128,160},{160,192},{192,224},{224... | collective-permute-start | bytes 608264 | tf_op jit(solution)/shard_map/ppermute | solution.py:424
  84.4 10.5 %collective-permute-start.3 = (bf16[136,960]{1,0:T(8,128)(2,1)S(1)}, bf16[136,960]{1,0:T(8,128)(2,1)S(1)}, u32[]{:S(2)}, u32[]{:S(2)}) collective-permute-start(bf16[136,960]{1,0:T(8,128)(2,1)S(1)} %get-tuple-element.28), channel_id=1, source_target_pairs={{0,256},{128,384},{1,257},{129,385},{2,258},{130,386},{3,259},{131... | collective-permute-start | bytes 783368 | tf_op jit(solution)/shard_map/ppermute | solution.py:432
  85.8 12.8 %collective-permute-start.6 = (bf16[136,960]{1,0:T(8,128)(2,1)S(1)}, bf16[136,960]{1,0:T(8,128)(2,1)S(1)}, u32[]{:S(2)}, u32[]{:S(2)}) collective-permute-start(bf16[136,960]{1,0:T(8,128)(2,1)S(1)} %get-tuple-element.38), channel_id=1, source_target_pairs={{0,384},{1,385},{2,386},{3,387},{4,388},{5,389},{6,390},{7,391},{8... | collective-permute-start | bytes 783368 | tf_op jit(solution)/shard_map/ppermute | solution.py:432
  91.6 9.6 %collective-permute-start.5 = (bf16[136,960]{1,0:T(8,128)(2,1)S(1)}, bf16[136,960]{1,0:T(8,128)(2,1)S(1)}, u32[]{:S(2)}, u32[]{:S(2)}) collective-permute-start(bf16[136,960]{1,0:T(8,128)(2,1)S(1)} %get-tuple-element.36), channel_id=1, source_target_pairs={{0,128},{128,256},{256,384},{1,129},{129,257},{257,385},{2,130},{1... | collective-permute-start | bytes 783368 | tf_op jit(solution)/shard_map/ppermute | solution.py:432
  98.5 37.6 %copy-start = (bf16[1,24,4096]{2,1,0:T(8,128)(2,1)S(1)}, bf16[1,24,4096]{2,1,0:T(8,128)(2,1)}, u32[]{:S(2)}) copy-start(bf16[1,24,4096]{2,1,0:T(8,128)(2,1)} %latent_ref.1) | copy-start | bytes 589828
  98.5 37.6 %copy-start.1 = (f32[16,4096]{1,0:T(8,128)S(1)}, f32[16,4096]{1,0:T(8,128)}, u32[]{:S(2)}) copy-start(f32[16,4096]{1,0:T(8,128)} %gate_ref.1) | copy-start | bytes 786436
  98.5 37.6 %copy-start.2 = (bf16[24,4096]{1,0:T(8,128)(2,1)S(1)}, bf16[24,4096]{1,0:T(8,128)(2,1)}, u32[]{:S(2)}) copy-start(bf16[24,4096]{1,0:T(8,128)(2,1)} %entering_ref.1) | copy-start | bytes 589828
  102.3 33.8 %all-to-all-start.2 = ((bf16[32,2,24,128]{3,2,1,0:T(8,128)(2,1)}), bf16[32,2,24,128]{3,2,1,0:T(8,128)(2,1)S(1)}, u32[]{:S(2)}, u32[]{:S(2)}) async-start(bf16[32,2,24,128]{3,2,1,0:T(8,128)(2,1)} %shard_map.109), calls=%async_computation.2 | async-start | bytes 786432 | tf_op jit(solution)/shard_map/all_to_all | solution.py:442
